TPU v7x, 32 devices: a whole 2x2x4 slice. The times are simulated.
32 devices in a mesh: dp: 16 (over z, y, core), fsdp: 2 (over x).
Axes of the slice: x: 2, y: 2, z: 4, core: 2. Of those that a mesh axis runs over, the one named last changes fastest.
Arguments:
- hidden_in: bfloat16 [8192, 960], P(('dp', 'fsdp')), may hold values from -6 to 6
- cotangent: bfloat16 [8192, 960], P(('dp', 'fsdp')), may hold values from -6 to 6
- norm_attn: float32 [960], P('fsdp'), may hold values from 0.5 to 1.5
- norm_ffn: float32 [960], P('fsdp'), may hold values from 0.5 to 1.5
- router: float32 [960, 3], P('fsdp'), may hold values from -0.125 to 0.125
- w_query: float32 [960, 960], P('fsdp'), may hold values from -0.1875 to 0.1875
- key_weight: float32 [960, 320], P('fsdp'), may hold values from -0.1875 to 0.1875
- value_weight: float32 [960, 320], P('fsdp'), may hold values from -0.1875 to 0.1875
- w_out: float32 [960, 960], P('fsdp'), may hold values from -0.75 to 0.75
- w_gate: float32 [960, 2560], P('fsdp'), may hold values from -0.1875 to 0.1875
- w_up: float32 [960, 2560], P('fsdp'), may hold values from -0.1875 to 0.1875
- w_down: float32 [2560, 960], P('fsdp'), may hold values from -0.15625 to 0.15625
- lengths: int32 [32], P(('dp', 'fsdp')), may hold values from 128 to 256, as said below
- chosen_second: int32 [32, 128], P(('dp', 'fsdp')), may hold values from 0 to 255, as said below
- chosen_third: int32 [32, 32], P(('dp', 'fsdp')), may hold values from 0 to 255, as said below
Outputs:
- hidden_out: bfloat16 [8192, 960], P(('dp', 'fsdp'))
- grad_hidden: float32 [8192, 960], P(('dp', 'fsdp'))
- grad_norm_attn: float32 [960], P('fsdp')
- grad_norm_ffn: float32 [960], P('fsdp')
- grad_router: float32 [960, 3], P('fsdp')
- grad_query: float32 [960, 960], P('fsdp')
- grad_key: float32 [960, 320], P('fsdp')
- grad_value: float32 [960, 320], P('fsdp')
- grad_out: float32 [960, 960], P('fsdp')
- grad_gate: float32 [960, 2560], P('fsdp')
- grad_up: float32 [960, 2560], P('fsdp')
- grad_down: float32 [2560, 960], P('fsdp')
Inputs may be any that keep to these rules, and one draw needn't show every extreme that they name: `lengths`: some sequence is exactly 256 long and another exactly 128. `chosen_second`: each row holds distinct positions in increasing order, all below that sequence's length, among them position 0 and the sequence's last valid position. `chosen_third`: each row holds distinct positions of the same row of chosen_second, in increasing order, among them its first and its last.
All inputs are finite; a program needn't handle non-finite values.
Results may differ from a plain program's by a relative error of at most 0.024.
Values may be sent and summed in bfloat16 or wider, within the bound.
No kernel may reach another device: no remote copies, remote signals or barrier semaphores. Data moves between devices by JAX's collectives and lax.ppermute only.
A program may use at most 384 MiB of HBM per device.

v0:
```python
from functools import partial

import jax
import jax.numpy as jnp
from jax import lax
from jax.sharding import PartitionSpec as P

QUERY_HEADS = 15
KEY_VALUE_HEADS = 5
HEAD_SIZE = 64


epsilon = 1e-05
negative = -1e30
narrow_dtype = jnp.bfloat16
wide_type = jnp.float32


def rotation(positions):
    half_width = HEAD_SIZE // 2
    frequency = 10000.0 ** (-jnp.arange(half_width, dtype=jnp.float32) / half_width)
    angles = positions.astype(jnp.float32)[:, None] * frequency[None, :]
    return (jnp.cos(angles)[:, None, :], jnp.sin(angles)[:, None, :])


def apply_rotary(value_rows, cosine_table, sine_values):
    half_width = value_rows.shape[-1] // 2
    leading = value_rows[..., :half_width]
    trailing = value_rows[..., half_width:]
    return jnp.concatenate(
        [
            leading * cosine_table - trailing * sine_values,
            trailing * cosine_table + leading * sine_values,
        ],
        axis=-1,
    )


def norm_forward(value_rows, gain):
    inverse = lax.rsqrt(jnp.mean(value_rows * value_rows, axis=-1, keepdims=True) + epsilon)
    return (value_rows * inverse * gain, inverse)


def norm_backward(value_rows, inverse, gain, incoming):
    weighted = incoming * gain
    d_values = inverse * weighted - value_rows * inverse**3 * jnp.mean(
        weighted * value_rows, axis=-1, keepdims=True
    )
    return (d_values, jnp.sum(incoming * value_rows * inverse, axis=0))


def build_mask(count_of_rows, key_valid):
    row_order = jnp.arange(count_of_rows)
    return (row_order[None, :] <= row_order[:, None]) & key_valid[None, :]


def head_forward(pieces, allowed, factor):
    query_rows, rotated_keys, value_rows = pieces
    raw_scores = jnp.einsum(
        "qgd,kd->gqk", query_rows, rotated_keys, preferred_element_type=wide_type
    )
    scores = jnp.where(allowed, raw_scores * factor, negative)
    row_peak = jnp.max(scores, axis=-1, keepdims=True)
    expanded = jnp.exp(scores - row_peak)
    row_total = jnp.sum(expanded, axis=-1, keepdims=True)
    probabilities = (expanded / row_total).astype(narrow_dtype)
    attended = jnp.einsum(
        "gqk,kd->qgd", probabilities, value_rows, preferred_element_type=wide_type
    )
    return (attended, row_peak + jnp.log(row_total))


def head_backward(pieces, allowed, factor):
    query_rows, rotated_keys, value_rows, log_total, attended_gradient = pieces
    raw_scores = jnp.einsum(
        "qgd,kd->gqk", query_rows, rotated_keys, preferred_element_type=wide_type
    )
    scores = jnp.where(allowed, raw_scores * factor, negative)
    probabilities = jnp.exp(scores - log_total)
    d_probs = jnp.einsum(
        "qgd,kd->gqk", attended_gradient, value_rows, preferred_element_type=wide_type
    )
    row_dot = jnp.sum(probabilities * d_probs, axis=-1, keepdims=True)
    d_raw = (probabilities * (d_probs - row_dot) * factor).astype(narrow_dtype)
    d_queries = jnp.einsum("gqk,kd->qgd", d_raw, rotated_keys, preferred_element_type=wide_type)
    d_keys = jnp.einsum("gqk,qgd->kd", d_raw, query_rows, preferred_element_type=wide_type)
    d_values = jnp.einsum(
        "gqk,qgd->kd",
        probabilities.astype(narrow_dtype),
        attended_gradient,
        preferred_element_type=wide_type,
    )
    return (d_queries, d_keys, d_values)


def block_forward(current, positions, key_valid, column, weights):
    gain_attn, gain_ffn, router, w_query, key_weight, value_weight, w_out, w_gate, w_up, w_down = (
        weights
    )
    count_of_rows = current.shape[0]
    group_count = QUERY_HEADS // KEY_VALUE_HEADS
    normalized_input, inv_attn = norm_forward(current, gain_attn.astype(wide_type))
    normed_low = normalized_input.astype(narrow_dtype)
    gating = jax.nn.sigmoid(
        jnp.dot(normed_low, router[:, column], preferred_element_type=wide_type)
    )
    cosine_table, sine_values = rotation(positions)
    query_lin = jnp.dot(normed_low, w_query, preferred_element_type=wide_type).reshape(
        count_of_rows, QUERY_HEADS, HEAD_SIZE
    )
    key_lin = jnp.dot(normed_low, key_weight, preferred_element_type=wide_type).reshape(
        count_of_rows, KEY_VALUE_HEADS, HEAD_SIZE
    )
    query_rows = apply_rotary(query_lin, cosine_table, sine_values).astype(narrow_dtype)
    rotated_keys = apply_rotary(key_lin, cosine_table, sine_values).astype(narrow_dtype)
    value_rows = (
        jnp.dot(normed_low, value_weight, preferred_element_type=wide_type)
        .astype(narrow_dtype)
        .reshape(count_of_rows, KEY_VALUE_HEADS, HEAD_SIZE)
    )
    query_per_head = jnp.moveaxis(
        query_rows.reshape(count_of_rows, KEY_VALUE_HEADS, group_count, HEAD_SIZE), 1, 0
    )
    head_key = jnp.moveaxis(rotated_keys, 1, 0)
    head_value = jnp.moveaxis(value_rows, 1, 0)
    allowed = build_mask(count_of_rows, key_valid)
    attended, log_total = lax.map(
        partial(head_forward, allowed=allowed, factor=HEAD_SIZE ** (-0.5)),
        (query_per_head, head_key, head_value),
    )
    attended_low = (
        jnp.moveaxis(attended, 0, 1)
        .reshape(count_of_rows, QUERY_HEADS * HEAD_SIZE)
        .astype(narrow_dtype)
    )
    attn_out = jnp.dot(attended_low, w_out, preferred_element_type=wide_type)
    after_attn = current + attn_out
    normed_ffn, inv_ffn = norm_forward(after_attn, gain_ffn.astype(wide_type))
    ffn_low = normed_ffn.astype(narrow_dtype)
    gate_proj = jnp.dot(ffn_low, w_gate, preferred_element_type=wide_type)
    up_proj = jnp.dot(ffn_low, w_up, preferred_element_type=wide_type)
    hidden = (jax.nn.silu(gate_proj) * up_proj).astype(narrow_dtype)
    ffn_out = jnp.dot(hidden, w_down, preferred_element_type=wide_type)
    kept = (
        current,
        positions,
        normed_low,
        inv_attn,
        query_per_head,
        head_key,
        head_value,
        log_total,
        attended_low,
        after_attn,
        inv_ffn,
        ffn_low,
        gate_proj,
        up_proj,
        hidden,
        gating,
    )
    return (attn_out + ffn_out, gating, kept)


def block_backward(kept, d_change, d_gating, key_valid, column, weights):
    (
        current,
        positions,
        normed_low,
        inv_attn,
        query_per_head,
        head_key,
        head_value,
        log_total,
        attended_low,
        after_attn,
        inv_ffn,
        ffn_low,
        gate_proj,
        up_proj,
        hidden,
        gating,
    ) = kept
    gain_attn, gain_ffn, router, w_query, key_weight, value_weight, w_out, w_gate, w_up, w_down = (
        weights
    )
    count_of_rows = current.shape[0]
    group_count = QUERY_HEADS // KEY_VALUE_HEADS
    d_ffn = d_change.astype(narrow_dtype)
    d_hidden = jnp.einsum("nd,fd->nf", d_ffn, w_down, preferred_element_type=wide_type)
    sigmoid_gate = jax.nn.sigmoid(gate_proj)
    d_gate_low = (
        d_hidden * up_proj * sigmoid_gate * (1.0 + gate_proj * (1.0 - sigmoid_gate))
    ).astype(narrow_dtype)
    d_up_low = (d_hidden * gate_proj * sigmoid_gate).astype(narrow_dtype)
    d_normed_ffn = jnp.einsum("nf,df->nd", d_gate_low, w_gate, preferred_element_type=wide_type)
    d_normed_ffn = d_normed_ffn + jnp.einsum(
        "nf,df->nd", d_up_low, w_up, preferred_element_type=wide_type
    )
    d_after, grad_gain_ffn = norm_backward(
        after_attn, inv_ffn, gain_ffn.astype(wide_type), d_normed_ffn
    )
    d_attn_low = (d_change + d_after).astype(narrow_dtype)
    attended_gradient = jnp.einsum(
        "nd,ad->na", d_attn_low, w_out, preferred_element_type=wide_type
    ).astype(narrow_dtype)
    head_gradient = jnp.moveaxis(
        attended_gradient.reshape(count_of_rows, KEY_VALUE_HEADS, group_count, HEAD_SIZE), 1, 0
    )
    allowed = build_mask(count_of_rows, key_valid)
    d_query_rot, d_key_rot, value_gradient = lax.map(
        partial(head_backward, allowed=allowed, factor=HEAD_SIZE ** (-0.5)),
        (query_per_head, head_key, head_value, log_total, head_gradient),
    )
    cosine_table, sine_values = rotation(positions)
    d_query_low = (
        apply_rotary(
            jnp.moveaxis(d_query_rot, 0, 1).reshape(count_of_rows, QUERY_HEADS, HEAD_SIZE),
            cosine_table,
            -sine_values,
        )
        .astype(narrow_dtype)
        .reshape(count_of_rows, QUERY_HEADS * HEAD_SIZE)
    )
    d_key_low = (
        apply_rotary(jnp.moveaxis(d_key_rot, 0, 1), cosine_table, -sine_values)
        .astype(narrow_dtype)
        .reshape(count_of_rows, KEY_VALUE_HEADS * HEAD_SIZE)
    )
    value_gradient_narrow = (
        jnp.moveaxis(value_gradient, 0, 1)
        .astype(narrow_dtype)
        .reshape(count_of_rows, KEY_VALUE_HEADS * HEAD_SIZE)
    )
    d_logit = d_gating * gating * (1.0 - gating)
    router_column = router[:, column].astype(wide_type)
    d_normed = jnp.einsum("nh,dh->nd", d_query_low, w_query, preferred_element_type=wide_type)
    d_normed = d_normed + jnp.einsum(
        "nh,dh->nd", d_key_low, key_weight, preferred_element_type=wide_type
    )
    d_normed = d_normed + jnp.einsum(
        "nh,dh->nd", value_gradient_narrow, value_weight, preferred_element_type=wide_type
    )
    d_normed = d_normed + d_logit[:, None] * router_column[None, :]
    router_piece = jnp.dot(d_logit, normed_low, preferred_element_type=wide_type)
    d_input, grad_gain_attn = norm_backward(
        current, inv_attn, gain_attn.astype(wide_type), d_normed
    )
    return (
        d_input + d_after,
        (grad_gain_attn, grad_gain_ffn, router_piece),
        (hidden, d_ffn, ffn_low, d_gate_low, d_up_low, attended_low, d_attn_low, normed_low,
         jnp.concatenate([d_query_low, d_key_low], axis=1), value_gradient_narrow),
    )


def partner(value, axis, bit):
    count = lax.axis_size(axis)
    return lax.ppermute(value, axis, [(i, i ^ bit) for i in range(count)])


def side(axis, bit):
    return (lax.axis_index(axis) // bit) % 2


def take_half(value, axis, bit, dim):
    size = value.shape[dim] // 2
    which = side(axis, bit)
    keep = lax.dynamic_slice_in_dim(value, which * size, size, dim)
    send = lax.dynamic_slice_in_dim(value, (1 - which) * size, size, dim)
    return keep, send


def add_half(value, axis, bit, dim):
    keep, send = take_half(value, axis, bit, dim)
    received = partner(send, axis, bit)
    return (keep.astype(wide_type) + received.astype(wide_type)).astype(narrow_dtype)


def join_half(value, axis, bit, dim):
    received = partner(value, axis, bit)
    first = side(axis, bit) == 0
    return jnp.where(
        first,
        jnp.concatenate([value, received], axis=dim),
        jnp.concatenate([received, value], axis=dim),
    )


def bits_of(axis, low):
    found = []
    bit = low
    while bit < lax.axis_size(axis):
        found.append(bit)
        bit = bit * 2
    return found


def split_steps(row_steps):
    steps = [("dp", 1, 0), ("dp", 2, 0)]
    return steps + [("dp", bit, 0 if row_steps else 1) for bit in bits_of("dp", 4)]


def reduce_matrix(gradient, row_steps):
    owners = lax.axis_size("fsdp")
    rows, columns = gradient.shape
    value = gradient.reshape(owners, rows // owners, columns)
    value = add_half(value, "dp", 1, 1)
    for bit in reversed(bits_of("fsdp", 1)):
        value = add_half(value, "fsdp", bit, 0)
    value = value[0]
    steps = split_steps(row_steps)
    for axis, bit, dim in steps[1:]:
        value = add_half(value, axis, bit, dim)
    for axis, bit, dim in reversed(steps):
        value = join_half(value, axis, bit, dim)
    return value


def place(parts, rows, shape):
    full = jnp.zeros(shape, narrow_dtype)
    for index, part in parts:
        full = lax.dynamic_update_slice_in_dim(full, part, index * rows, 0)
    return full


def gather_near(shard):
    owners = lax.axis_size("fsdp")
    mine = lax.axis_index("fsdp")
    half, _ = take_half(shard, "dp", 1, 0)
    parts = [(mine, shard)]
    for offset in range(1, owners):
        parts.append((mine ^ offset, join_half(partner(half, "fsdp", offset), "dp", 1, 0)))
    return place(parts, shard.shape[0], (shard.shape[0] * owners,) + shard.shape[1:])


def gather_far(shard, row_steps):
    owners = lax.axis_size("fsdp")
    mine = lax.axis_index("fsdp")
    steps = split_steps(row_steps)
    piece = shard
    for axis, bit, dim in steps:
        piece, _ = take_half(piece, axis, bit, dim)
    parts = [(mine, shard)]
    for offset in range(1, owners):
        other = partner(piece, "fsdp", offset)
        for axis, bit, dim in reversed(steps):
            other = join_half(other, axis, bit, dim)
        parts.append((mine ^ offset, other))
    return place(parts, shard.shape[0], (shard.shape[0] * owners,) + shard.shape[1:])


def local(
    hidden_in,
    cotangent,
    norm_attn,
    norm_ffn,
    router,
    w_query,
    key_weight,
    value_weight,
    w_out,
    w_gate,
    w_up,
    w_down,
    lengths,
    chosen_second,
    chosen_third,
):
    owners = lax.axis_size("fsdp")
    mine = lax.axis_index("fsdp")
    small = jnp.concatenate(
        [norm_attn[None, :], norm_ffn[None, :], router.T, jnp.zeros((11, norm_attn.shape[0]), wide_type)]
    ).astype(narrow_dtype)
    small_parts = [(mine, small)] + [
        (mine ^ offset, partner(small, "fsdp", offset)) for offset in range(1, owners)
    ]
    small_rows = jnp.zeros((16, owners * small.shape[1]), narrow_dtype)
    for index, part in small_parts:
        small_rows = lax.dynamic_update_slice_in_dim(small_rows, part, index * small.shape[1], 1)
    width = w_query.shape[1]
    kv_width = key_weight.shape[1]
    attn_shard = jnp.concatenate([w_query, key_weight, w_out, value_weight], axis=1).astype(narrow_dtype)
    attn_full = gather_near(attn_shard)
    gate_full = gather_far(w_gate.astype(narrow_dtype), False)
    up_full = gather_far(w_up.astype(narrow_dtype), False)
    down_full = gather_far(w_down.astype(narrow_dtype), True)
    weights = (
        small_rows[0],
        small_rows[1],
        small_rows[2:5].T,
        attn_full[:, :width],
        attn_full[:, width : width + kv_width],
        attn_full[:, 2 * width + kv_width :],
        attn_full[:, width + kv_width : 2 * width + kv_width],
        gate_full,
        up_full,
        down_full,
    )
    token_count = hidden_in.shape[0]
    positions = jnp.arange(token_count, dtype=jnp.int32)
    valid = positions < lengths[0]
    chosen_two = chosen_second[0]
    chosen_three = chosen_third[0]
    every_two = jnp.ones(chosen_two.shape, jnp.bool_)
    every_three = jnp.ones(chosen_three.shape, jnp.bool_)
    start = hidden_in.astype(wide_type)
    change_one, gating_one, kept_one = block_forward(start, positions, valid, 0, weights)
    scale_one = jnp.where(valid, gating_one, 0.0)
    state_one = start + scale_one[:, None] * change_one
    picked_two = jnp.take(state_one, chosen_two, axis=0)
    change_two, gating_two, kept_two = block_forward(picked_two, chosen_two, every_two, 1, weights)
    state_two = state_one.at[chosen_two].set(picked_two + gating_two[:, None] * change_two)
    picked_three = jnp.take(state_two, chosen_three, axis=0)
    change_three, gating_three, kept_three = block_forward(
        picked_three, chosen_three, every_three, 2, weights
    )
    state_three = state_two.at[chosen_three].set(
        picked_three + gating_three[:, None] * change_three
    )
    hidden_out = state_three.astype(narrow_dtype)
    incoming = cotangent.astype(wide_type)
    d_picked = jnp.take(incoming, chosen_three, axis=0)
    d_inner, small_three, factors_three = block_backward(
        kept_three,
        gating_three[:, None] * d_picked,
        jnp.sum(change_three * d_picked, axis=-1),
        every_three,
        2,
        weights,
    )
    incoming = incoming.at[chosen_three].set(d_picked + d_inner)
    d_picked = jnp.take(incoming, chosen_two, axis=0)
    d_inner, small_two, factors_two = block_backward(
        kept_two,
        gating_two[:, None] * d_picked,
        jnp.sum(change_two * d_picked, axis=-1),
        every_two,
        1,
        weights,
    )
    incoming = incoming.at[chosen_two].set(d_picked + d_inner)
    d_inner, small_one, factors_one = block_backward(
        kept_one,
        scale_one[:, None] * incoming,
        jnp.where(valid, jnp.sum(change_one * incoming, axis=-1), 0.0),
        valid,
        0,
        weights,
    )
    grad_hidden = incoming + d_inner
    hidden, d_ffn, ffn_low, d_gate, d_up, attended, d_attn, normed, d_qk, d_v = (
        jnp.concatenate(rows, axis=0) for rows in zip(factors_one, factors_two, factors_three)
    )

    def outer(left, right):
        return jnp.einsum("na,nb->ab", left, right, preferred_element_type=wide_type).astype(narrow_dtype)

    down_shard = reduce_matrix(outer(hidden, d_ffn), True).astype(wide_type)
    gate_shard = reduce_matrix(outer(ffn_low, d_gate), False).astype(wide_type)
    up_shard = reduce_matrix(outer(ffn_low, d_up), False).astype(wide_type)
    attn_grad = jnp.concatenate([outer(normed, d_qk), outer(attended, d_attn), outer(normed, d_v)], axis=1)
    attn_out_shard = reduce_matrix(attn_grad, False).astype(wide_type)
    small_grads = jnp.stack(
        [
            small_one[0] + small_two[0] + small_three[0],
            small_one[1] + small_two[1] + small_three[1],
            small_one[2],
            small_two[2],
            small_three[2],
        ]
        + [jnp.zeros_like(small_one[0])] * 3
    )
    small_sum = lax.psum(small_grads, ("dp", "fsdp"))
    small_sum = lax.dynamic_slice_in_dim(small_sum, mine * small.shape[1], small.shape[1], 1)
    return (
        hidden_out,
        grad_hidden,
        small_sum[0],
        small_sum[1],
        small_sum[2:5].T,
        attn_out_shard[:, :width],
        attn_out_shard[:, width : width + kv_width],
        attn_out_shard[:, 2 * width + kv_width :],
        attn_out_shard[:, width + kv_width : 2 * width + kv_width],
        gate_shard,
        up_shard,
        down_shard,
    )


def solution(mesh):
    in_specs = (
        P(("dp", "fsdp"), None),
        P(("dp", "fsdp"), None),
        P("fsdp"),
        P("fsdp"),
        P("fsdp", None),
        P("fsdp", None),
        P("fsdp", None),
        P("fsdp", None),
        P("fsdp", None),
        P("fsdp", None),
        P("fsdp", None),
        P("fsdp", None),
        P(("dp", "fsdp")),
        P(("dp", "fsdp"), None),
        P(("dp", "fsdp"), None),
    )
    out_specs = (
        P(("dp", "fsdp"), None),
        P(("dp", "fsdp"), None),
        P("fsdp"),
        P("fsdp"),
        P("fsdp", None),
        P("fsdp", None),
        P("fsdp", None),
        P("fsdp", None),
        P("fsdp", None),
        P("fsdp", None),
        P("fsdp", None),
        P("fsdp", None),
    )
    return jax.shard_map(local, mesh=mesh, in_specs=in_specs, out_specs=out_specs, check_vma=False)
```

profile of v0, /device:TPU:1, one launch (start us, length us, event | category | flops | bytes accessed | tf_op | source)
XLA Modules:
  0.0 873.4 jit_solution(1218189553609483174)
XLA Ops:
  24.7 5.0 copy.313
  57.4 11.1 %collective-permute-done.4 = bf16[120,640]{1,0:T(8,128)(2,1)S(1)} collective-permute-done((bf16[120,640]{1,0:T(8,128)(2,1)}, bf16[120,640]{1,0:T(8,128)(2,1)S(1)}, u32[]{:S(2)}, u32[]{:S(2)}) %collective-permute-start.4) | collective-permute-done | bytes 153632 | tf_op jit(solution)/shard_map/ppermute | solution.py:259
  77.0 6.0 collective-permute-done.5
  84.5 5.1 collective-permute-done.10
  92.0 4.7 collective-permute-done.15
  101.8 9.4 %collective-permute-done.11 = bf16[120,2560]{1,0:T(8,128)(2,1)S(1)} collective-permute-done((bf16[120,2560]{1,0:T(8,128)(2,1)S(1)}, bf16[120,2560]{1,0:T(8,128)(2,1)S(1)}, u32[]{:S(2)}, u32[]{:S(2)}) %collective-permute-start.11) | collective-permute-done | bytes 614432 | tf_op jit(solution)/shard_map/ppermute | solution.py:259
  115.0 10.3 %collective-permute-done.16 = bf16[320,960]{1,0:T(8,128)(2,1)S(1)} collective-permute-done((bf16[320,960]{1,0:T(8,128)(2,1)S(1)}, bf16[320,960]{1,0:T(8,128)(2,1)S(1)}, u32[]{:S(2)}, u32[]{:S(2)}) %collective-permute-start.16) | collective-permute-done | bytes 614432 | tf_op jit(solution)/shard_map/ppermute | solution.py:259
  140.4 10.9 %while.90 = (s32[]{:T(128)}, bf16[5,256,3,64]{1,3,2,0:T(8,128)(2,1)S(1)}, f32[5,3,256,1]{2,1,3,0:T(4,128)}, bf16[5,256,64]{1,2,0:T(8,128)(2,1)S(1)}, bf16[5,256,...) while((s32[]{:T(128)}, ...), condition=%wide.region_4.5_spmd.clone.clone, body=%wide.region_1.4_spmd.clone.sunk.clone | while | flops 52034816 | bytes 2880857 | solution.py:127
  159.3 4.0 fusion.359
  173.3 4.6 fusion.183
  177.9 5.9 convert_add_fusion
  196.1 15.5 %while.91 = (s32[]{:T(128)}, bf16[5,128,3,64]{1,3,2,0:T(8,128)(2,1)}, f32[5,3,128,1]{2,1,3,0:T(4,128)}, bf16[5,128,64]{1,2,0:T(8,128)(2,1)}, bf16[5,128,64]{1,2,0:T(8,128)(2,1)}, /*index=5*/bf16[5,128,3,64]{1,3,2,0:T(8,128)(2,1)S(1)}) while((s32[]{:T(128)}, bf16[5,128,3,64]{1,3,2,0:T(8,128)(2,1)}, ...), condition=%wide.region_10.12_spmd.clone.clone, body=%wide.region_7.11_spmd.clone.sunk.clone | while | flops 12992130 | bytes 817745 | solution.py:127
  221.0 5.4 multiply_add_fusion
  240.4 15.1 %while.92 = (s32[]{:T(128)}, bf16[5,32,3,64]{3,1,2,0:T(8,128)(2,1)}, f32[5,3,32,1]{2,1,3,0:T(4,128)}, bf16[5,32,64]{2,1,0:T(8,128)(2,1)}, bf16[5,32,64]{2,1,0:T(8,128)(2,1)}, /*index=5*/bf16[5,32,3,64]{3,1,2,0:T(8,128)(2,1)S(1)}) while((s32[]{:T(128)}, bf16[5,32,3,64]{3,1,2,0:T(8,128)(2,1)}, ...), condition=%wide.region_17.20_spmd.clone.clone, body=%wide.region_14.19_spmd.clone.sunk.clone | while | flops 811938 | bytes 138961 | solution.py:127
  259.9 4.2 fusion.362
  272.5 4.8 multiply_reduce_fusion.17
  284.3 40.6 %while.93 = (s32[]{:T(128)}, f32[5,32,3,64]{3,1,2,0:T(8,128)}, f32[5,32,64]{2,0,1:T(8,128)}, bf16[5,32,64]{2,1,0:T(8,128)(2,1)}, bf16[5,32,64]{2,1,0:T(8,128)(2,...) while((s32[]{:T(128)}, f32[5,32,3,64]{3,1,2,0:T(8,128)}, ...), condition=%wide.region_23.26_spmd.clone.clone, body=%wide.region_21.25_spmd.clone.sunk.clone | while | flops 2010368 | bytes 650481 | solution.py:211
  348.0 5.5 multiply_convert_fusion.4
  353.5 4.3 fusion.364
  363.3 29.9 %while.94 = (s32[]{:T(128)}, f32[5,128,3,64]{1,3,2,0:T(8,128)}, f32[5,128,64]{1,2,0:T(8,128)}, bf16[5,128,64]{1,2,0:T(8,128)(2,1)S(1)}, bf16[5,128,64]{1,2,0:T(8...) while((s32[]{:T(128)}, f32[5,128,3,64]{1,3,2,0:T(8,128)}, ...), condition=%wide.region_30.33_spmd.clone.clone, body=%wide.region_28.32_spmd.clone.sunk.clone | while | flops 32162816 | bytes 2614889 | solution.py:211
  405.1 6.9 multiply_convert_fusion.1
  413.7 4.9 convolution_convert_fusion.1
  418.6 4.4 convolution_convert_fusion.2
  428.7 38.1 %while.95 = (s32[]{:T(128)}, f32[5,256,3,64]{1,3,2,0:T(8,128)}, f32[5,256,64]{1,2,0:T(8,128)}, bf16[5,256,64]{1,2,0:T(8,128)(2,1)}, bf16[5,256,64]{1,2,0:T(8,128...) while((s32[]{:T(128)}, f32[5,256,3,64]{1,3,2,0:T(8,128)}, ...), condition=%wide.region_37.40_spmd.clone.clone, body=%wide.region_35.39_spmd.clone.sunk.clone | while | flops 128714752 | bytes 9615729 | solution.py:211
  477.6 4.5 convolution_convert_fusion.3
  484.6 8.2 concatenate.341
  503.6 4.6 convolution_convert_fusion
  508.2 11.0 %reshape.710 = bf16[2,1280,960]{1,0,2:T(2,128)(2,1)} reshape(bf16[2560,960]{0,1:T(8,128)(2,1)} %convolution_convert_fusion) | data formatting | bytes 9830400 | tf_op jit(solution)/shard_map/reshape | solution.py:307
  519.2 7.2 constant_dynamic-slice_fusion.6
  532.6 7.5 copy.373
  540.6 39.0 %psum.7 = f32[8,960]{1,0:T(8,128)S(1)} all-reduce(f32[8,960]{1,0:T(8,128)S(1)} %stack.21), channel_id=1, replica_groups=mesh['dp'=16,'fsdp'=2] {'dp','fsdp'}, use_global_device_ids=true, to_apply=%region_46.49 | all-reduce | flops 7680 | bytes 61440 | tf_op jit(solution)/shard_map/psum | solution.py:474
  598.6 4.6 copy.349
  619.1 22.1 %collective-permute-done.28 = bf16[1,240,2560]{2,1,0:T(8,128)(2,1)} collective-permute-done((bf16[1,240,2560]{2,1,0:T(8,128)(2,1)}, bf16[1,240,2560]{2,1,0:T(8,128)(2,1)}, u32[]{:S(2)}, u32[]{:S(2)}) %collective-permute-start.28) | collective-permute-done | bytes 1228832 | tf_op jit(solution)/shard_map/ppermute | solution.py:259
  644.6 23.0 %collective-permute-done.37 = bf16[1,240,2560]{2,1,0:T(8,128)(2,1)} collective-permute-done((bf16[1,240,2560]{2,1,0:T(8,128)(2,1)}, bf16[1,240,2560]{2,1,0:T(8,128)(2,1)}, u32[]{:S(2)}, u32[]{:S(2)}) %collective-permute-start.37) | collective-permute-done | bytes 1228832 | tf_op jit(solution)/shard_map/ppermute | solution.py:259
  671.9 22.0 %collective-permute-done.46 = bf16[1,640,960]{1,2,0:T(8,128)(2,1)} collective-permute-done((bf16[1,640,960]{1,2,0:T(8,128)(2,1)}, bf16[1,640,960]{1,2,0:T(8,128)(2,1)}, u32[]{:S(2)}, u32[]{:S(2)}) %collective-permute-start.46) | collective-permute-done | bytes 1228832 | tf_op jit(solution)/shard_map/ppermute | solution.py:259
  705.7 6.6 collective-permute-done.47
  717.2 5.1 collective-permute-done.39
  722.5 11.8 %collective-permute-done.48 = bf16[160,960]{1,0:T(8,128)(2,1)S(1)} collective-permute-done((bf16[160,960]{1,0:T(8,128)(2,1)S(1)}, bf16[160,960]{1,0:T(8,128)(2,1)S(1)}, u32[]{:S(2)}, u32[]{:S(2)}) %collective-permute-start.48) | collective-permute-done | bytes 307232 | tf_op jit(solution)/shard_map/ppermute | solution.py:259
  739.5 22.1 %collective-permute-done.23 = bf16[120,640]{1,0:T(8,128)(2,1)S(1)} collective-permute-done((bf16[120,640]{1,0:T(8,128)(2,1)S(1)}, bf16[120,640]{1,0:T(8,128)(2,1)S(1)}, u32[]{:S(2)}, u32[]{:S(2)}) %collective-permute-start.23) | collective-permute-done | bytes 153632 | tf_op jit(solution)/shard_map/ppermute | solution.py:259
  765.0 13.0 %collective-permute-done.24 = bf16[120,1280]{1,0:T(8,128)(2,1)S(1)} collective-permute-done((bf16[120,1280]{1,0:T(8,128)(2,1)S(1)}, bf16[120,1280]{1,0:T(8,128)(2,1)S(1)}, u32[]{:S(2)}, u32[]{:S(2)}) %collective-permute-start.24) | collective-permute-done | bytes 307232 | tf_op jit(solution)/shard_map/ppermute | solution.py:259
  785.5 12.7 %collective-permute-done.51 = bf16[160,960]{1,0:T(8,128)(2,1)S(1)} collective-permute-done((bf16[160,960]{1,0:T(8,128)(2,1)S(1)}, bf16[160,960]{1,0:T(8,128)(2,1)S(1)}, u32[]{:S(2)}, u32[]{:S(2)}) %collective-permute-start.51) | collective-permute-done | bytes 307232 | tf_op jit(solution)/shard_map/ppermute | solution.py:259
  804.5 11.9 %collective-permute-done.52 = bf16[320,960]{1,0:T(8,128)(2,1)S(1)} collective-permute-done((bf16[320,960]{1,0:T(8,128)(2,1)S(1)}, bf16[320,960]{1,0:T(8,128)(2,1)S(1)}, u32[]{:S(2)}, u32[]{:S(2)}) %collective-permute-start.52) | collective-permute-done | bytes 614432 | tf_op jit(solution)/shard_map/ppermute | solution.py:259
  818.5 10.1 %collective-permute-start.53 = (bf16[640,960]{0,1:T(8,128)(2,1)}, bf16[640,960]{0,1:T(8,128)(2,1)}, u32[]{:S(2)}, u32[]{:S(2)}) collective-permute-start(bf16[640,960]{0,1:T(8,128)(2,1)} %copy.352), channel_id=1, source_target_pairs={{0,2},{2,0},{4,6},{6,4},{8,10},{10,8},{12,14},{14,12},{16,18},{18,... | collective-permute-start | bytes 3686408 | tf_op jit(solution)/shard_map/ppermute | solution.py:259
  838.0 4.6 fusion.188
  851.4 5.8 copy.358
  857.1 4.6 fusion.349
  861.7 5.5 fusion.189
  867.2 5.8 fusion.190
  (992 shorter events, 488.3 us)
Async XLA Ops:
  3.1 46.9 %collective-permute-start = (bf16[16,480]{1,0:T(8,128)(2,1)S(1)}, bf16[16,480]{1,0:T(8,128)(2,1)S(1)}, u32[]{:S(2)}, u32[]{:S(2)}) collective-permute-start(bf16[16,480]{1,0:T(8,128)(2,1)S(1)} %maximum_maximum_fusion), channel_id=1, source_target_pairs={{0,1},{1,0},{2,3},{3,2},{4,5},{5,4},{6,7},{7,6},{8,9},{9,8},{10,11... | collective-permute-start | bytes 46088 | tf_op jit(solution)/shard_map/ppermute | solution.py:259
  14.2 76.9 %collective-permute-start.1 = (bf16[240,2560]{1,0:T(8,128)(2,1)}, bf16[240,2560]{1,0:T(8,128)(2,1)}, u32[]{:S(2)}, u32[]{:S(2)}) collective-permute-start(bf16[240,2560]{1,0:T(8,128)(2,1)} %constant_dynamic-slice_fusion.20), channel_id=1, source_target_pairs={{0,1},{1,0},{2,3},{3,2},{4,5},{5,4},{6,7},{7,6},{8,9},{9,8},{10,11... | collective-permute-start | bytes 3686408 | tf_op jit(solution)/shard_map/ppermute | solution.py:259
  18.5 34.0 %collective-permute-start.3 = (bf16[120,640]{1,0:T(8,128)(2,1)}, bf16[120,640]{1,0:T(8,128)(2,1)}, u32[]{:S(2)}, u32[]{:S(2)}) collective-permute-start(bf16[120,640]{1,0:T(8,128)(2,1)} %dynamic_slice.254), channel_id=1, source_target_pairs={{0,1},{1,0},{2,3},{3,2},{4,5},{5,4},{6,7},{7,6},{8,9},{9,8},{10,11... | collective-permute-start | bytes 460808 | tf_op jit(solution)/shard_map/ppermute | solution.py:259
  23.7 31.3 %collective-permute-start.8 = (bf16[120,640]{1,0:T(8,128)(2,1)}, bf16[120,640]{1,0:T(8,128)(2,1)}, u32[]{:S(2)}, u32[]{:S(2)}) collective-permute-start(bf16[120,640]{1,0:T(8,128)(2,1)} %dynamic_slice.255), channel_id=1, source_target_pairs={{0,1},{1,0},{2,3},{3,2},{4,5},{5,4},{6,7},{7,6},{8,9},{9,8},{10,11... | collective-permute-start | bytes 460808 | tf_op jit(solution)/shard_map/ppermute | solution.py:259
  30.7 25.1 %collective-permute-start.13 = (bf16[80,960]{1,0:T(8,128)(2,1)S(1)}, bf16[80,960]{1,0:T(8,128)(2,1)S(1)}, u32[]{:S(2)}, u32[]{:S(2)}) collective-permute-start(bf16[80,960]{1,0:T(8,128)(2,1)S(1)} %constant_dynamic-slice_fusion.19), channel_id=1, source_target_pairs={{0,1},{1,0},{2,3},{3,2},{4,5},{5,4},{6,7},{7,6},{8,9},{9,8},{10,11... | collective-permute-start | bytes 460808 | tf_op jit(solution)/shard_map/ppermute | solution.py:259
  52.5 16.1 %collective-permute-start.4 = (bf16[120,640]{1,0:T(8,128)(2,1)}, bf16[120,640]{1,0:T(8,128)(2,1)S(1)}, u32[]{:S(2)}, u32[]{:S(2)}) collective-permute-start(bf16[120,640]{1,0:T(8,128)(2,1)} %collective-permute-done.3), channel_id=1, source_target_pairs={{0,16},{2,18},{4,20},{6,22},{8,24},{10,26},{12,28},{14,30},{16,0},... | collective-permute-start | bytes 460808 | tf_op jit(solution)/shard_map/ppermute | solution.py:259
  55.0 16.8 %collective-permute-start.9 = (bf16[120,640]{1,0:T(8,128)(2,1)}, bf16[120,640]{1,0:T(8,128)(2,1)S(1)}, u32[]{:S(2)}, u32[]{:S(2)}) collective-permute-start(bf16[120,640]{1,0:T(8,128)(2,1)} %collective-permute-done.8), channel_id=1, source_target_pairs={{0,16},{2,18},{4,20},{6,22},{8,24},{10,26},{12,28},{14,30},{16,0},... | collective-permute-start | bytes 460808 | tf_op jit(solution)/shard_map/ppermute | solution.py:259
  55.8 19.6 %collective-permute-start.14 = (bf16[80,960]{1,0:T(8,128)(2,1)S(1)}, bf16[80,960]{1,0:T(8,128)(2,1)S(1)}, u32[]{:S(2)}, u32[]{:S(2)}) collective-permute-start(bf16[80,960]{1,0:T(8,128)(2,1)S(1)} %collective-permute-done.13), channel_id=1, source_target_pairs={{0,16},{2,18},{4,20},{6,22},{8,24},{10,26},{12,28},{14,30},{16,0},... | collective-permute-start | bytes 460808 | tf_op jit(solution)/shard_map/ppermute | solution.py:259
  72.9 16.7 %collective-permute-start.10 = (bf16[120,1280]{1,0:T(8,128)(2,1)S(1)}, bf16[120,1280]{1,0:T(8,128)(2,1)S(1)}, u32[]{:S(2)}, u32[]{:S(2)}) collective-permute-start(bf16[120,1280]{1,0:T(8,128)(2,1)S(1)} %maximum_select_fusion.25), channel_id=1, source_target_pairs={{0,8},{2,10},{4,12},{6,14},{8,0},{10,2},{12,4},{14,6},{16,24},{18,... | collective-permute-start | bytes 921608 | tf_op jit(solution)/shard_map/ppermute | solution.py:259
  75.5 21.2 %collective-permute-start.15 = (bf16[160,960]{1,0:T(8,128)(2,1)S(1)}, bf16[160,960]{1,0:T(8,128)(2,1)S(1)}, u32[]{:S(2)}, u32[]{:S(2)}) collective-permute-start(bf16[160,960]{1,0:T(8,128)(2,1)S(1)} %maximum_select_fusion.22), channel_id=1, source_target_pairs={{0,8},{2,10},{4,12},{6,14},{8,0},{10,2},{12,4},{14,6},{16,24},{18,... | collective-permute-start | bytes 921608 | tf_op jit(solution)/shard_map/ppermute | solution.py:259
  89.8 21.5 %collective-permute-start.11 = (bf16[120,2560]{1,0:T(8,128)(2,1)S(1)}, bf16[120,2560]{1,0:T(8,128)(2,1)S(1)}, u32[]{:S(2)}, u32[]{:S(2)}) collective-permute-start(bf16[120,2560]{1,0:T(8,128)(2,1)S(1)} %maximum_select_fusion.18), channel_id=1, source_target_pairs={{0,4},{2,6},{4,0},{6,2},{8,12},{10,14},{12,8},{14,10},{16,20},{18,... | collective-permute-start | bytes 1843208 | tf_op jit(solution)/shard_map/ppermute | solution.py:259
  91.1 37.7 %collective-permute-start.2 = (bf16[240,2560]{1,0:T(8,128)(2,1)}, bf16[240,2560]{1,0:T(8,128)(2,1)}, u32[]{:S(2)}, u32[]{:S(2)}) collective-permute-start(bf16[240,2560]{1,0:T(8,128)(2,1)} %collective-permute-done.1), channel_id=1, source_target_pairs={{0,2},{2,0},{4,6},{6,4},{8,10},{10,8},{12,14},{14,12},{16,18},{18,... | collective-permute-start | bytes 3686408 | tf_op jit(solution)/shard_map/ppermute | solution.py:259
  96.9 28.4 %collective-permute-start.16 = (bf16[320,960]{1,0:T(8,128)(2,1)S(1)}, bf16[320,960]{1,0:T(8,128)(2,1)S(1)}, u32[]{:S(2)}, u32[]{:S(2)}) collective-permute-start(bf16[320,960]{1,0:T(8,128)(2,1)S(1)} %maximum_select_fusion.15), channel_id=1, source_target_pairs={{0,4},{2,6},{4,0},{6,2},{8,12},{10,14},{12,8},{14,10},{16,20},{18,... | collective-permute-start | bytes 1843208 | tf_op jit(solution)/shard_map/ppermute | solution.py:259
  99.4 56.0 %collective-permute-start.7 = (bf16[240,2560]{1,0:T(8,128)(2,1)}, bf16[240,2560]{1,0:T(8,128)(2,1)}, u32[]{:S(2)}, u32[]{:S(2)}) collective-permute-start(bf16[240,2560]{1,0:T(8,128)(2,1)} %maximum_select_fusion.10), channel_id=1, source_target_pairs={{0,2},{2,0},{4,6},{6,4},{8,10},{10,8},{12,14},{14,12},{16,18},{18,... | collective-permute-start | bytes 3686408 | tf_op jit(solution)/shard_map/ppermute | solution.py:259
  112.5 50.9 %collective-permute-start.12 = (bf16[240,2560]{1,0:T(8,128)(2,1)}, bf16[240,2560]{1,0:T(8,128)(2,1)}, u32[]{:S(2)}, u32[]{:S(2)}) collective-permute-start(bf16[240,2560]{1,0:T(8,128)(2,1)} %maximum_select_fusion.11), channel_id=1, source_target_pairs={{0,2},{2,0},{4,6},{6,4},{8,10},{10,8},{12,14},{14,12},{16,18},{18,... | collective-permute-start | bytes 3686408 | tf_op jit(solution)/shard_map/ppermute | solution.py:259
  127.4 43.5 %collective-permute-start.17 = (bf16[640,960]{0,1:T(8,128)(2,1)}, bf16[640,960]{0,1:T(8,128)(2,1)}, u32[]{:S(2)}, u32[]{:S(2)}) collective-permute-start(bf16[640,960]{0,1:T(8,128)(2,1)} %copy.314), channel_id=1, source_target_pairs={{0,2},{2,0},{4,6},{6,4},{8,10},{10,8},{12,14},{14,12},{16,18},{18,... | collective-permute-start | bytes 3686408 | tf_op jit(solution)/shard_map/ppermute | solution.py:259
  496.2 87.3 %collective-permute-start.18 = (bf16[2,240,2560]{2,1,0:T(8,128)(2,1)}, bf16[2,240,2560]{2,1,0:T(8,128)(2,1)}, u32[]{:S(2)}, u32[]{:S(2)}) collective-permute-start(bf16[2,240,2560]{2,1,0:T(8,128)(2,1)} %constant_dynamic-slice_fusion.18), channel_id=1, source_target_pairs={{0,2},{2,0},{4,6},{6,4},{8,10},{10,8},{12,14},{14,12},{16,18},{18,... | collective-permute-start | bytes 7372808 | tf_op jit(solution)/shard_map/ppermute | solution.py:259
  499.6 89.3 %collective-permute-start.27 = (bf16[2,240,2560]{2,1,0:T(8,128)(2,1)}, bf16[2,240,2560]{2,1,0:T(8,128)(2,1)}, u32[]{:S(2)}, u32[]{:S(2)}) collective-permute-start(bf16[2,240,2560]{2,1,0:T(8,128)(2,1)} %constant_dynamic-slice_fusion.14), channel_id=1, source_target_pairs={{0,2},{2,0},{4,6},{6,4},{8,10},{10,8},{12,14},{14,12},{16,18},{18,... | collective-permute-start | bytes 7372808 | tf_op jit(solution)/shard_map/ppermute | solution.py:259
  503.5 90.3 %collective-permute-start.36 = (bf16[2,240,2560]{2,1,0:T(8,128)(2,1)}, bf16[2,240,2560]{2,1,0:T(8,128)(2,1)}, u32[]{:S(2)}, u32[]{:S(2)}) collective-permute-start(bf16[2,240,2560]{2,1,0:T(8,128)(2,1)} %constant_dynamic-slice_fusion.10), channel_id=1, source_target_pairs={{0,2},{2,0},{4,6},{6,4},{8,10},{10,8},{12,14},{14,12},{16,18},{18,... | collective-permute-start | bytes 7372808 | tf_op jit(solution)/shard_map/ppermute | solution.py:259
  528.3 70.3 %collective-permute-start.45 = (bf16[2,640,960]{1,2,0:T(8,128)(2,1)}, bf16[2,640,960]{1,2,0:T(8,128)(2,1)}, u32[]{:S(2)}, u32[]{:S(2)}) collective-permute-start(bf16[2,640,960]{1,2,0:T(8,128)(2,1)} %copy.374), channel_id=1, source_target_pairs={{0,2},{2,0},{4,6},{6,4},{8,10},{10,8},{12,14},{14,12},{16,18},{18,... | collective-permute-start | bytes 7372808 | tf_op jit(solution)/shard_map/ppermute | solution.py:259
  587.7 27.2 %collective-permute-start.19 = (bf16[1,240,2560]{2,1,0:T(8,128)(2,1)}, bf16[1,240,2560]{2,1,0:T(8,128)(2,1)}, u32[]{:S(2)}, u32[]{:S(2)}) collective-permute-start(bf16[1,240,2560]{2,1,0:T(8,128)(2,1)} %constant_dynamic-slice_fusion.17), channel_id=1, source_target_pairs={{0,1},{1,0},{2,3},{3,2},{4,5},{5,4},{6,7},{7,6},{8,9},{9,8},{10,11... | collective-permute-start | bytes 3686408 | tf_op jit(solution)/shard_map/ppermute | solution.py:259
  592.9 48.3 %collective-permute-start.28 = (bf16[1,240,2560]{2,1,0:T(8,128)(2,1)}, bf16[1,240,2560]{2,1,0:T(8,128)(2,1)}, u32[]{:S(2)}, u32[]{:S(2)}) collective-permute-start(bf16[1,240,2560]{2,1,0:T(8,128)(2,1)} %constant_dynamic-slice_fusion.13), channel_id=1, source_target_pairs={{0,1},{1,0},{2,3},{3,2},{4,5},{5,4},{6,7},{7,6},{8,9},{9,8},{10,11... | collective-permute-start | bytes 3686408 | tf_op jit(solution)/shard_map/ppermute | solution.py:259
  598.1 69.4 %collective-permute-start.37 = (bf16[1,240,2560]{2,1,0:T(8,128)(2,1)}, bf16[1,240,2560]{2,1,0:T(8,128)(2,1)}, u32[]{:S(2)}, u32[]{:S(2)}) collective-permute-start(bf16[1,240,2560]{2,1,0:T(8,128)(2,1)} %constant_dynamic-slice_fusion.9), channel_id=1, source_target_pairs={{0,1},{1,0},{2,3},{3,2},{4,5},{5,4},{6,7},{7,6},{8,9},{9,8},{10,11... | collective-permute-start | bytes 3686408 | tf_op jit(solution)/shard_map/ppermute | solution.py:259
  611.3 82.5 %collective-permute-start.46 = (bf16[1,640,960]{1,2,0:T(8,128)(2,1)}, bf16[1,640,960]{1,2,0:T(8,128)(2,1)}, u32[]{:S(2)}, u32[]{:S(2)}) collective-permute-start(bf16[1,640,960]{1,2,0:T(8,128)(2,1)} %copy.350), channel_id=1, source_target_pairs={{0,1},{1,0},{2,3},{3,2},{4,5},{5,4},{6,7},{7,6},{8,9},{9,8},{10,11... | collective-permute-start | bytes 3686408 | tf_op jit(solution)/shard_map/ppermute | solution.py:259
  618.3 81.1 %collective-permute-start.20 = (bf16[120,2560]{1,0:T(8,128)(2,1)}, bf16[120,2560]{1,0:T(8,128)(2,1)S(1)}, u32[]{:S(2)}, u32[]{:S(2)}) collective-permute-start(bf16[120,2560]{1,0:T(8,128)(2,1)} %dynamic-slice_bitcast_fusion.5), channel_id=1, source_target_pairs={{0,4},{2,6},{4,0},{6,2},{8,12},{10,14},{12,8},{14,10},{16,20},{18,... | collective-permute-start | bytes 1843208 | tf_op jit(solution)/shard_map/ppermute | solution.py:259
  643.8 57.8 %collective-permute-start.29 = (bf16[120,2560]{1,0:T(8,128)(2,1)}, bf16[120,2560]{1,0:T(8,128)(2,1)}, u32[]{:S(2)}, u32[]{:S(2)}) collective-permute-start(bf16[120,2560]{1,0:T(8,128)(2,1)} %dynamic-slice_bitcast_fusion.4), channel_id=1, source_target_pairs={{0,4},{2,6},{4,0},{6,2},{8,12},{10,14},{12,8},{14,10},{16,20},{18,... | collective-permute-start | bytes 1843208 | tf_op jit(solution)/shard_map/ppermute | solution.py:259
  671.1 31.9 %collective-permute-start.38 = (bf16[120,2560]{1,0:T(8,128)(2,1)}, bf16[120,2560]{1,0:T(8,128)(2,1)}, u32[]{:S(2)}, u32[]{:S(2)}) collective-permute-start(bf16[120,2560]{1,0:T(8,128)(2,1)} %dynamic-slice_bitcast_fusion.3), channel_id=1, source_target_pairs={{0,4},{2,6},{4,0},{6,2},{8,12},{10,14},{12,8},{14,10},{16,20},{18,... | collective-permute-start | bytes 1843208 | tf_op jit(solution)/shard_map/ppermute | solution.py:259
  704.2 18.1 %collective-permute-start.39 = (bf16[120,1280]{1,0:T(8,128)(2,1)S(1)}, bf16[120,1280]{1,0:T(8,128)(2,1)S(1)}, u32[]{:S(2)}, u32[]{:S(2)}) collective-permute-start(bf16[120,1280]{1,0:T(8,128)(2,1)S(1)} %constant_dynamic-slice_fusion.8), channel_id=1, source_target_pairs={{0,8},{2,10},{4,12},{6,14},{8,0},{10,2},{12,4},{14,6},{16,24},{18,... | collective-permute-start | bytes 921608 | tf_op jit(solution)/shard_map/ppermute | solution.py:259
  712.6 21.7 %collective-permute-start.48 = (bf16[160,960]{1,0:T(8,128)(2,1)S(1)}, bf16[160,960]{1,0:T(8,128)(2,1)S(1)}, u32[]{:S(2)}, u32[]{:S(2)}) collective-permute-start(bf16[160,960]{1,0:T(8,128)(2,1)S(1)} %constant_dynamic-slice_fusion.3), channel_id=1, source_target_pairs={{0,8},{2,10},{4,12},{6,14},{8,0},{10,2},{12,4},{14,6},{16,24},{18,... | collective-permute-start | bytes 921608 | tf_op jit(solution)/shard_map/ppermute | solution.py:259
  714.6 19.9 %collective-permute-start.22 = (bf16[120,640]{1,0:T(8,128)(2,1)S(1)}, bf16[120,640]{1,0:T(8,128)(2,1)S(1)}, u32[]{:S(2)}, u32[]{:S(2)}) collective-permute-start(bf16[120,640]{1,0:T(8,128)(2,1)S(1)} %constant_dynamic-slice_fusion.15), channel_id=1, source_target_pairs={{0,16},{2,18},{4,20},{6,22},{8,24},{10,26},{12,28},{14,30},{16,0},... | collective-permute-start | bytes 460808 | tf_op jit(solution)/shard_map/ppermute | solution.py:259
  715.6 21.3 %collective-permute-start.31 = (bf16[120,640]{1,0:T(8,128)(2,1)S(1)}, bf16[120,640]{1,0:T(8,128)(2,1)S(1)}, u32[]{:S(2)}, u32[]{:S(2)}) collective-permute-start(bf16[120,640]{1,0:T(8,128)(2,1)S(1)} %constant_dynamic-slice_fusion.11), channel_id=1, source_target_pairs={{0,16},{2,18},{4,20},{6,22},{8,24},{10,26},{12,28},{14,30},{16,0},... | collective-permute-start | bytes 460808 | tf_op jit(solution)/shard_map/ppermute | solution.py:259
  734.4 27.4 %collective-permute-start.49 = (bf16[80,960]{1,0:T(8,128)(2,1)S(1)}, bf16[80,960]{1,0:T(8,128)(2,1)S(1)}, u32[]{:S(2)}, u32[]{:S(2)}) collective-permute-start(bf16[80,960]{1,0:T(8,128)(2,1)S(1)} %constant_dynamic-slice_fusion.2), channel_id=1, source_target_pairs={{0,16},{2,18},{4,20},{6,22},{8,24},{10,26},{12,28},{14,30},{16,0},... | collective-permute-start | bytes 460808 | tf_op jit(solution)/shard_map/ppermute | solution.py:259
  734.6 27.0 %collective-permute-start.23 = (bf16[120,640]{1,0:T(8,128)(2,1)S(1)}, bf16[120,640]{1,0:T(8,128)(2,1)S(1)}, u32[]{:S(2)}, u32[]{:S(2)}) collective-permute-start(bf16[120,640]{1,0:T(8,128)(2,1)S(1)} %add_convert_fusion.19), channel_id=1, source_target_pairs={{0,16},{2,18},{4,20},{6,22},{8,24},{10,26},{12,28},{14,30},{16,0},... | collective-permute-start | bytes 460808 | tf_op jit(solution)/shard_map/ppermute | solution.py:259
  737.0 27.9 %collective-permute-start.32 = (bf16[120,640]{1,0:T(8,128)(2,1)S(1)}, bf16[120,640]{1,0:T(8,128)(2,1)S(1)}, u32[]{:S(2)}, u32[]{:S(2)}) collective-permute-start(bf16[120,640]{1,0:T(8,128)(2,1)S(1)} %add_convert_fusion.18), channel_id=1, source_target_pairs={{0,16},{2,18},{4,20},{6,22},{8,24},{10,26},{12,28},{14,30},{16,0},... | collective-permute-start | bytes 460808 | tf_op jit(solution)/shard_map/ppermute | solution.py:259
  737.2 41.8 %collective-permute-start.41 = (bf16[120,640]{1,0:T(8,128)(2,1)S(1)}, bf16[120,640]{1,0:T(8,128)(2,1)S(1)}, u32[]{:S(2)}, u32[]{:S(2)}) collective-permute-start(bf16[120,640]{1,0:T(8,128)(2,1)S(1)} %add_convert_fusion.17), channel_id=1, source_target_pairs={{0,16},{2,18},{4,20},{6,22},{8,24},{10,26},{12,28},{14,30},{16,0},... | collective-permute-start | bytes 460808 | tf_op jit(solution)/shard_map/ppermute | solution.py:259
  761.7 16.4 %collective-permute-start.24 = (bf16[120,1280]{1,0:T(8,128)(2,1)S(1)}, bf16[120,1280]{1,0:T(8,128)(2,1)S(1)}, u32[]{:S(2)}, u32[]{:S(2)}) collective-permute-start(bf16[120,1280]{1,0:T(8,128)(2,1)S(1)} %maximum_select_fusion.26), channel_id=1, source_target_pairs={{0,8},{2,10},{4,12},{6,14},{8,0},{10,2},{12,4},{14,6},{16,24},{18,... | collective-permute-start | bytes 921608 | tf_op jit(solution)/shard_map/ppermute | solution.py:259
  761.8 17.3 %collective-permute-start.50 = (bf16[80,960]{1,0:T(8,128)(2,1)S(1)}, bf16[80,960]{1,0:T(8,128)(2,1)S(1)}, u32[]{:S(2)}, u32[]{:S(2)}) collective-permute-start(bf16[80,960]{1,0:T(8,128)(2,1)S(1)} %add_convert_fusion.16), channel_id=1, source_target_pairs={{0,16},{2,18},{4,20},{6,22},{8,24},{10,26},{12,28},{14,30},{16,0},... | collective-permute-start | bytes 460808 | tf_op jit(solution)/shard_map/ppermute | solution.py:259
  765.0 19.6 %collective-permute-start.33 = (bf16[120,1280]{1,0:T(8,128)(2,1)S(1)}, bf16[120,1280]{1,0:T(8,128)(2,1)S(1)}, u32[]{:S(2)}, u32[]{:S(2)}) collective-permute-start(bf16[120,1280]{1,0:T(8,128)(2,1)S(1)} %maximum_select_fusion.27), channel_id=1, source_target_pairs={{0,8},{2,10},{4,12},{6,14},{8,0},{10,2},{12,4},{14,6},{16,24},{18,... | collective-permute-start | bytes 921608 | tf_op jit(solution)/shard_map/ppermute | solution.py:259
  778.2 21.0 %collective-permute-start.25 = (bf16[120,2560]{1,0:T(8,128)(2,1)S(1)}, bf16[120,2560]{1,0:T(8,128)(2,1)S(1)}, u32[]{:S(2)}, u32[]{:S(2)}) collective-permute-start(bf16[120,2560]{1,0:T(8,128)(2,1)S(1)} %maximum_select_fusion.19), channel_id=1, source_target_pairs={{0,4},{2,6},{4,0},{6,2},{8,12},{10,14},{12,8},{14,10},{16,20},{18,... | collective-permute-start | bytes 1843208 | tf_op jit(solution)/shard_map/ppermute | solution.py:259
  779.0 23.0 %collective-permute-start.42 = (bf16[120,1280]{1,0:T(8,128)(2,1)S(1)}, bf16[120,1280]{1,0:T(8,128)(2,1)S(1)}, u32[]{:S(2)}, u32[]{:S(2)}) collective-permute-start(bf16[120,1280]{1,0:T(8,128)(2,1)S(1)} %maximum_select_fusion.28), channel_id=1, source_target_pairs={{0,8},{2,10},{4,12},{6,14},{8,0},{10,2},{12,4},{14,6},{16,24},{18,... | collective-permute-start | bytes 921608 | tf_op jit(solution)/shard_map/ppermute | solution.py:259
  779.2 19.0 %collective-permute-start.51 = (bf16[160,960]{1,0:T(8,128)(2,1)S(1)}, bf16[160,960]{1,0:T(8,128)(2,1)S(1)}, u32[]{:S(2)}, u32[]{:S(2)}) collective-permute-start(bf16[160,960]{1,0:T(8,128)(2,1)S(1)} %maximum_select_fusion.23), channel_id=1, source_target_pairs={{0,8},{2,10},{4,12},{6,14},{8,0},{10,2},{12,4},{14,6},{16,24},{18,... | collective-permute-start | bytes 921608 | tf_op jit(solution)/shard_map/ppermute | solution.py:259
  784.8 43.8 %collective-permute-start.34 = (bf16[120,2560]{1,0:T(8,128)(2,1)S(1)}, bf16[120,2560]{1,0:T(8,128)(2,1)}, u32[]{:S(2)}, u32[]{:S(2)}) collective-permute-start(bf16[120,2560]{1,0:T(8,128)(2,1)S(1)} %maximum_select_fusion.20), channel_id=1, source_target_pairs={{0,4},{2,6},{4,0},{6,2},{8,12},{10,14},{12,8},{14,10},{16,20},{18,... | collective-permute-start | bytes 1843208 | tf_op jit(solution)/shard_map/ppermute | solution.py:259
  798.4 18.1 %collective-permute-start.52 = (bf16[320,960]{1,0:T(8,128)(2,1)S(1)}, bf16[320,960]{1,0:T(8,128)(2,1)S(1)}, u32[]{:S(2)}, u32[]{:S(2)}) collective-permute-start(bf16[320,960]{1,0:T(8,128)(2,1)S(1)} %maximum_select_fusion.16), channel_id=1, source_target_pairs={{0,4},{2,6},{4,0},{6,2},{8,12},{10,14},{12,8},{14,10},{16,20},{18,... | collective-permute-start | bytes 1843208 | tf_op jit(solution)/shard_map/ppermute | solution.py:259
  799.4 38.6 %collective-permute-start.26 = (bf16[240,2560]{1,0:T(8,128)(2,1)S(1)}, bf16[240,2560]{1,0:T(8,128)(2,1)}, u32[]{:S(2)}, u32[]{:S(2)}) collective-permute-start(bf16[240,2560]{1,0:T(8,128)(2,1)S(1)} %maximum_select_fusion.12), channel_id=1, source_target_pairs={{0,2},{2,0},{4,6},{6,4},{8,10},{10,8},{12,14},{14,12},{16,18},{18,... | collective-permute-start | bytes 3686408 | tf_op jit(solution)/shard_map/ppermute | solution.py:259
  803.0 28.3 %collective-permute-start.43 = (bf16[120,2560]{1,0:T(8,128)(2,1)}, bf16[120,2560]{1,0:T(8,128)(2,1)}, u32[]{:S(2)}, u32[]{:S(2)}) collective-permute-start(bf16[120,2560]{1,0:T(8,128)(2,1)} %maximum_select_fusion.21), channel_id=1, source_target_pairs={{0,4},{2,6},{4,0},{6,2},{8,12},{10,14},{12,8},{14,10},{16,20},{18,... | collective-permute-start | bytes 1843208 | tf_op jit(solution)/shard_map/ppermute | solution.py:259
  818.5 28.2 %collective-permute-start.53 = (bf16[640,960]{0,1:T(8,128)(2,1)}, bf16[640,960]{0,1:T(8,128)(2,1)}, u32[]{:S(2)}, u32[]{:S(2)}) collective-permute-start(bf16[640,960]{0,1:T(8,128)(2,1)} %copy.352), channel_id=1, source_target_pairs={{0,2},{2,0},{4,6},{6,4},{8,10},{10,8},{12,14},{14,12},{16,18},{18,... | collective-permute-start | bytes 3686408 | tf_op jit(solution)/shard_map/ppermute | solution.py:259
  831.3 30.4 %collective-permute-start.35 = (bf16[240,2560]{1,0:T(8,128)(2,1)}, bf16[240,2560]{1,0:T(8,128)(2,1)}, u32[]{:S(2)}, u32[]{:S(2)}) collective-permute-start(bf16[240,2560]{1,0:T(8,128)(2,1)} %maximum_select_fusion.13), channel_id=1, source_target_pairs={{0,2},{2,0},{4,6},{6,4},{8,10},{10,8},{12,14},{14,12},{16,18},{18,... | collective-permute-start | bytes 3686408 | tf_op jit(solution)/shard_map/ppermute | solution.py:259
  834.4 32.9 %collective-permute-start.44 = (bf16[240,2560]{1,0:T(8,128)(2,1)}, bf16[240,2560]{1,0:T(8,128)(2,1)}, u32[]{:S(2)}, u32[]{:S(2)}) collective-permute-start(bf16[240,2560]{1,0:T(8,128)(2,1)} %maximum_select_fusion.14), channel_id=1, source_target_pairs={{0,2},{2,0},{4,6},{6,4},{8,10},{10,8},{12,14},{14,12},{16,18},{18,... | collective-permute-start | bytes 3686408 | tf_op jit(solution)/shard_map/ppermute | solution.py:259
  (215 other events, 2487.3 us)
where the time goes:
time: 890 us; the launch traced here: 873 us
  matrix products  263 us (30%)
  waiting for transfers between devices  208 us (23%)
  local copies, waits for them, and re-layouts  168 us (19%)
  other arithmetic  121 us (14%)
  starting transfers between devices  67.8 us (8%)
  blocking collectives  39 us (4%)
    ppermute x54, waiting for transfers between devices, partner(): return lax.ppermute(value, axis, [(i, i ^ bit) for i in range(count)])  208 us
    ppermute x54, starting transfers between devices, partner(): return lax.ppermute(value, axis, [(i, i ^ bit) for i in range(count)])  67.8 us
    psum x1, blocking collectives, local(): small_sum = lax.psum(small_grads, ('dp', 'fsdp'))  39 us
    unnamed x429, local copies, waits for them, and re-layouts  37.1 us
    dot_general x15, matrix products, head_backward(): jnp.einsum('gqk,kd->qgd', d_raw, rotated_keys, preferred_element_type=wid...  24.4 us
    dot_general x6, matrix products, outer(): jnp.einsum('na,nb->ab', left, right, preferred_element_type=wide_type)  22.1 us
    dot_general x15, matrix products, head_backward(): jnp.einsum('gqk,qgd->kd', d_raw, query_rows, preferred_element_type=wide_...  22.1 us
    convert_element_type x20, other arithmetic, add_half(): (keep.astype(wide_type) + received.astype(wide_type)).astype(narrow_dtype)  21.2 us
  transfers between devices with their start and end apart: 54, of which 21 were waited for; matrix products, arithmetic and copies ran while one was open for 25% of the time, Pallas kernels for 0%

commit v1 on v0

v1 whole, which is shorter than its diff:
```python
from functools import partial

import jax
import jax.numpy as jnp
from jax import lax
from jax.experimental import pallas as pl
from jax.experimental.pallas import tpu as pltpu
from jax.sharding import PartitionSpec as P

QUERY_HEADS = 15
KEY_VALUE_HEADS = 5
HEAD_SIZE = 64
GROUP = QUERY_HEADS // KEY_VALUE_HEADS
MODEL = QUERY_HEADS * HEAD_SIZE
QK_WIDTH = (QUERY_HEADS + KEY_VALUE_HEADS) * HEAD_SIZE
V_START = QK_WIDTH + MODEL - HEAD_SIZE
V_HEAD = 1
SCALE = HEAD_SIZE ** (-0.5)
CHUNK = 512
VMEM_LIMIT = 60 * 2**20

epsilon = 1e-05
negative = -1e30
narrow_dtype = jnp.bfloat16
wide_type = jnp.float32


def rows_dot(left, right):
    return lax.dot_general(left, right, (((1,), (0,)), ((), ())), preferred_element_type=wide_type)


def rows_dot_t(left, right):
    return lax.dot_general(left, right, (((1,), (1,)), ((), ())), preferred_element_type=wide_type)


def columns_dot(left, right):
    return lax.dot_general(left, right, (((0,), (0,)), ((), ())), preferred_element_type=wide_type)


def inverse_rms(rows):
    return lax.rsqrt(jnp.mean(rows * rows, axis=-1, keepdims=True) + epsilon)


def norm_back(rows, inverse, gain, incoming):
    weighted = incoming * gain
    mean = jnp.mean(weighted * rows, axis=-1, keepdims=True)
    d_rows = inverse * weighted - rows * (inverse * inverse * inverse * mean)
    return d_rows, jnp.sum(incoming * rows * inverse, axis=0, keepdims=True)


def rotate(block, cosines, sines):
    lanes = lax.broadcasted_iota(jnp.int32, block.shape, 1)
    swapped = jnp.where(lanes % HEAD_SIZE < HEAD_SIZE // 2, pltpu.roll(block, 96, 1), pltpu.roll(block, 32, 1))
    return block * cosines + swapped * sines


def causal_bias(count, length):
    row = lax.broadcasted_iota(jnp.int32, (count, count), 0)
    column = lax.broadcasted_iota(jnp.int32, (count, count), 1)
    allowed = column <= row
    if length is not None:
        allowed = allowed & (column < length)
    bias = jnp.where(allowed, 0.0, negative)
    return jnp.concatenate([bias] * GROUP, axis=0)


def head_columns(ref, first, count):
    return jnp.concatenate(
        [ref[:, (first + i) * HEAD_SIZE : (first + i + 1) * HEAD_SIZE] for i in range(count)], axis=0
    )


def attention_forward(rows, gain, router_row, cosines, sines, bias, weight, normed_ref, qk_ref, v_ref, att_ref, log_ref):
    count = rows.shape[0]
    normed_ref[...] = (rows * inverse_rms(rows) * gain).astype(narrow_dtype)
    normed = normed_ref[...]
    gating = jax.nn.sigmoid(jnp.sum(normed.astype(wide_type) * router_row, axis=-1, keepdims=True))
    for block in range(QK_WIDTH // 256):
        product = rows_dot(normed, weight[:, block * 256 : (block + 1) * 256])
        for part in range(2):
            piece = rotate(product[:, part * 128 : (part + 1) * 128], cosines, sines)
            at = block * 256 + part * 128
            qk_ref[:, at : at + 128] = piece.astype(narrow_dtype)
    v_ref[...] = rows_dot(normed, weight[:, V_START:]).astype(narrow_dtype)
    for head in range(KEY_VALUE_HEADS):
        queries = head_columns(qk_ref, head * GROUP, GROUP)
        keys = head_columns(qk_ref, QUERY_HEADS + head, 1)
        values = head_columns(v_ref, V_HEAD + head, 1)
        scores = rows_dot_t(queries, keys) * SCALE + bias
        peak = jnp.max(scores, axis=-1, keepdims=True)
        expanded = jnp.exp(scores - peak)
        total = jnp.sum(expanded, axis=-1, keepdims=True)
        log_ref[:, head : head + 1] = peak + jnp.log(total)
        attended = rows_dot((expanded / total).astype(narrow_dtype), values).astype(narrow_dtype)
        for i in range(GROUP):
            at = (head * GROUP + i) * HEAD_SIZE
            att_ref[:, at : at + HEAD_SIZE] = attended[i * count : (i + 1) * count]
    return rows_dot(att_ref[...], weight[:, QK_WIDTH : QK_WIDTH + MODEL]), gating


def attention_backward(
    rows, gain, router_row, cosines, sines, bias, weight, normed_ref, qk_ref, v_ref, log_ref,
    d_attn_low, d_gating, gating, d_att_ref, d_raw_ref, d_qk_ref, d_v_ref,
):
    count = rows.shape[0]
    d_att_ref[...] = rows_dot_t(d_attn_low, weight[:, QK_WIDTH : QK_WIDTH + MODEL]).astype(narrow_dtype)
    d_v_ref[...] = jnp.zeros_like(d_v_ref)
    for head in range(KEY_VALUE_HEADS):
        queries = head_columns(qk_ref, head * GROUP, GROUP)
        keys = head_columns(qk_ref, QUERY_HEADS + head, 1)
        values = head_columns(v_ref, V_HEAD + head, 1)
        d_attended = head_columns(d_att_ref, head * GROUP, GROUP)
        scores = rows_dot_t(queries, keys) * SCALE + bias
        probabilities = jnp.exp(scores - log_ref[:, head : head + 1])
        d_probs = rows_dot_t(d_attended, values)
        row_dot = jnp.sum(probabilities * d_probs, axis=-1, keepdims=True)
        d_raw = (probabilities * (d_probs - row_dot) * SCALE).astype(narrow_dtype)
        d_queries = rows_dot(d_raw, keys)
        for i in range(GROUP):
            at = (head * GROUP + i) * HEAD_SIZE
            d_raw_ref[:, at : at + HEAD_SIZE] = d_queries[i * count : (i + 1) * count]
        at = (QUERY_HEADS + head) * HEAD_SIZE
        d_raw_ref[:, at : at + HEAD_SIZE] = columns_dot(queries, d_raw).T
        at = (V_HEAD + head) * HEAD_SIZE
        d_values = columns_dot(d_attended, probabilities.astype(narrow_dtype)).T
        d_v_ref[:, at : at + HEAD_SIZE] = d_values.astype(narrow_dtype)
    for block in range(QK_WIDTH // 128):
        at = block * 128
        d_qk_ref[:, at : at + 128] = rotate(d_raw_ref[:, at : at + 128], cosines, -sines).astype(narrow_dtype)
    d_normed = rows_dot_t(d_qk_ref[...], weight[:, :QK_WIDTH]) + rows_dot_t(d_v_ref[...], weight[:, V_START:])
    d_logit = d_gating * gating * (1.0 - gating)
    d_normed = d_normed + d_logit * router_row
    router_gradient = jnp.sum(d_logit * normed_ref[...].astype(wide_type), axis=0, keepdims=True)
    d_rows, gain_gradient = norm_back(rows, inverse_rms(rows), gain, d_normed)
    return d_rows, gain_gradient, router_gradient


def ffn_forward(after, gain, w_gate, w_up, w_down, ffn_ref, gate_ref, up_ref, hidden_ref, total_ref, chunk):
    ffn_ref[...] = (after * inverse_rms(after) * gain).astype(narrow_dtype)
    total_ref[...] = jnp.zeros_like(total_ref)

    def step(index, carry):
        columns = pl.ds(pl.multiple_of(index * chunk, chunk), chunk)
        gate = rows_dot(ffn_ref[...], w_gate[:, columns])
        up = rows_dot(ffn_ref[...], w_up[:, columns])
        gate_ref[:, columns] = gate
        up_ref[:, columns] = up
        hidden = (gate * jax.nn.sigmoid(gate) * up).astype(narrow_dtype)
        hidden_ref[:, columns] = hidden
        total_ref[...] += rows_dot(hidden, w_down[columns, :])
        return carry

    lax.fori_loop(0, gate_ref.shape[1] // chunk, step, 0)


def ffn_backward(after, gain, w_gate, w_up, w_down, d_ffn_ref, gate_ref, up_ref, d_gate_ref, d_up_ref, total_ref, chunk):
    total_ref[...] = jnp.zeros_like(total_ref)

    def step(index, carry):
        columns = pl.ds(pl.multiple_of(index * chunk, chunk), chunk)
        d_hidden = rows_dot_t(d_ffn_ref[...], w_down[columns, :])
        gate = gate_ref[:, columns]
        sig = jax.nn.sigmoid(gate)
        d_gate = (d_hidden * up_ref[:, columns] * sig * (1.0 + gate * (1.0 - sig))).astype(narrow_dtype)
        d_up = (d_hidden * gate * sig).astype(narrow_dtype)
        d_gate_ref[:, columns] = d_gate
        d_up_ref[:, columns] = d_up
        total_ref[...] += rows_dot_t(d_gate, w_gate[:, columns]) + rows_dot_t(d_up, w_up[:, columns])
        return carry

    lax.fori_loop(0, gate_ref.shape[1] // chunk, step, 0)
    return norm_back(after, inverse_rms(after), gain, total_ref[...])


def pick_exact(selector, rows):
    high = rows.astype(narrow_dtype)
    rest = rows - high.astype(wide_type)
    middle = rest.astype(narrow_dtype)
    low = (rest - middle.astype(wide_type)).astype(narrow_dtype)
    return rows_dot(selector, high) + rows_dot(selector, middle) + rows_dot(selector, low)


def first_attention_kernel(
    length_ref, hidden_in, small, cosines, sines, weight, normed_ref, qk_ref, v_ref, att_ref, log_ref, out_ref, gating_ref
):
    rows = hidden_in[...].astype(wide_type)
    bias = causal_bias(rows.shape[0], length_ref[0])
    attn_out, gating = attention_forward(
        rows, small[0:1], small[2:3], cosines[...], sines[...], bias, weight, normed_ref, qk_ref, v_ref, att_ref, log_ref
    )
    out_ref[...] = attn_out
    gating_ref[...] = jnp.broadcast_to(gating, gating_ref.shape)


def last_attention_kernel(
    length_ref, hidden_in, small, cosines, sines, weight, normed_ref, qk_ref, v_ref, log_ref, gating_ref, d_gating_ref,
    d_attn_ref, d_input_ref, d_qk_ref, d_v_ref, grad_hidden_ref, small_out, d_att_ref, d_raw_ref,
):
    rows = hidden_in[...].astype(wide_type)
    bias = causal_bias(rows.shape[0], length_ref[0])
    d_rows, gain_gradient, router_gradient = attention_backward(
        rows, small[0:1], small[2:3], cosines[...], sines[...], bias, weight, normed_ref, qk_ref, v_ref, log_ref,
        d_attn_ref[...], d_gating_ref[:, 0:1], gating_ref[:, 0:1], d_att_ref, d_raw_ref, d_qk_ref, d_v_ref,
    )
    grad_hidden_ref[...] = d_input_ref[...] + d_rows
    small_out[...] = jnp.zeros_like(small_out)
    small_out[0:1] = gain_gradient
    small_out[2:3] = router_gradient


def middle_kernel(
    length_ref, hidden_in, cotangent, small, attn_out_ref, gating_ref, cos_two, sin_two, cos_three, sin_three,
    column_two, row_two, column_three, row_three, w_attn_hbm, w_gate_hbm, w_up_hbm, w_down_hbm,
    hidden_out, d_input_ref, d_gating_ref, small_out,
    hidden_one, d_ffn_one, ffn_one, d_gate_one, d_up_one, d_attn_one,
    hidden_in_r, d_ffn_in_r, ffn_in_r, d_gate_in_r, d_up_in_r, d_attn_in_r, att_in_r, normed_in_r, d_qk_in_r, d_v_in_r,
    w_attn, w_gate, w_up, w_down, sems,
    gate_one, up_one, gate_two, up_two, gate_three, up_three, total_one, total_two, total_three,
    qk_two, v_two, log_two, qk_three, v_three, log_three, d_att_two, d_raw_two, d_att_three, d_raw_three,
):
    copies = [
        pltpu.make_async_copy(source, target, sems.at[i])
        for i, (source, target) in enumerate(
            ((w_gate_hbm, w_gate), (w_up_hbm, w_up), (w_down_hbm, w_down), (w_attn_hbm, w_attn))
        )
    ]
    for copy in copies:
        copy.start()
    count_two, count_three = column_two.shape[0], column_three.shape[0]
    count_one = hidden_in.shape[0]
    two = pl.ds(0, count_two)
    three = pl.ds(count_two, count_three)
    gain_attn, gain_ffn = small[0:1], small[1:2]

    def selector(shape, hit):
        return jnp.where(hit, 1.0, 0.0).astype(narrow_dtype)

    pick_two = selector(
        None, lax.broadcasted_iota(jnp.int32, (count_two, count_one), 1) == column_two[...]
    )
    put_two = selector(None, lax.broadcasted_iota(jnp.int32, (count_one, count_two), 0) == row_two[...])
    pick_three = selector(None, column_three[...] == row_two[...])
    put_three = selector(None, column_two[...] == row_three[...])

    after_one = hidden_in[...].astype(wide_type) + attn_out_ref[...]
    for copy in copies[:3]:
        copy.wait()
    ffn_forward(after_one, gain_ffn, w_gate, w_up, w_down, ffn_one, gate_one, up_one, hidden_one, total_one, CHUNK)
    valid = lax.broadcasted_iota(jnp.int32, (count_one, 1), 0) < length_ref[0]
    scale_one = jnp.where(valid, gating_ref[:, 0:1], 0.0)
    change_one = attn_out_ref[...] + total_one[...]
    d_input_ref[...] = hidden_in[...].astype(wide_type) + scale_one * change_one
    total_one[...] = change_one

    copies[3].wait()
    state_two = pick_exact(pick_two, d_input_ref[...])
    bias_two = causal_bias(count_two, None)
    attn_two, gating_two = attention_forward(
        state_two, gain_attn, small[3:4], cos_two[...], sin_two[...], bias_two, w_attn,
        normed_in_r.at[two], qk_two, v_two, att_in_r.at[two], log_two,
    )
    after_two = state_two + attn_two
    ffn_forward(
        after_two, gain_ffn, w_gate, w_up, w_down, ffn_in_r.at[two], gate_two, up_two, hidden_in_r.at[two], total_two, CHUNK
    )
    change_two = attn_two + total_two[...]
    delta_two = gating_two * change_two

    state_three = pick_exact(pick_three, state_two + delta_two)
    bias_three = causal_bias(count_three, None)
    attn_three, gating_three = attention_forward(
        state_three, gain_attn, small[4:5], cos_three[...], sin_three[...], bias_three, w_attn,
        normed_in_r.at[three], qk_three, v_three, att_in_r.at[three], log_three,
    )
    after_three = state_three + attn_three
    ffn_forward(
        after_three, gain_ffn, w_gate, w_up, w_down, ffn_in_r.at[three], gate_three, up_three,
        hidden_in_r.at[three], total_three, CHUNK,
    )
    change_three = attn_three + total_three[...]
    added = delta_two + pick_exact(put_three, gating_three * change_three)
    hidden_out[...] = (d_input_ref[...] + pick_exact(put_two, added)).astype(narrow_dtype)

    incoming_two = rows_dot(pick_two, cotangent[...])
    incoming_three = rows_dot(pick_three, incoming_two.astype(narrow_dtype))
    d_change = gating_three * incoming_three
    d_gating = jnp.sum(change_three * incoming_three, axis=-1, keepdims=True)
    d_ffn_in_r[three] = d_change.astype(narrow_dtype)
    d_after, gain_ffn_three = ffn_backward(
        after_three, gain_ffn, w_gate, w_up, w_down, d_ffn_in_r.at[three], gate_three, up_three,
        d_gate_in_r.at[three], d_up_in_r.at[three], total_three, CHUNK,
    )
    d_attn_in_r[three] = (d_change + d_after).astype(narrow_dtype)
    d_rows, gain_attn_three, router_three = attention_backward(
        state_three, gain_attn, small[4:5], cos_three[...], sin_three[...], bias_three, w_attn, normed_in_r.at[three],
        qk_three, v_three, log_three, d_attn_in_r[three], d_gating, gating_three, d_att_three, d_raw_three,
        d_qk_in_r.at[three], d_v_in_r.at[three],
    )
    back_three = pick_exact(put_three, d_rows + d_after)

    incoming_two = incoming_two + back_three
    d_change = gating_two * incoming_two
    d_gating = jnp.sum(change_two * incoming_two, axis=-1, keepdims=True)
    d_ffn_in_r[two] = d_change.astype(narrow_dtype)
    d_after, gain_ffn_two = ffn_backward(
        after_two, gain_ffn, w_gate, w_up, w_down, d_ffn_in_r.at[two], gate_two, up_two,
        d_gate_in_r.at[two], d_up_in_r.at[two], total_two, CHUNK,
    )
    d_attn_in_r[two] = (d_change + d_after).astype(narrow_dtype)
    d_rows, gain_attn_two, router_two = attention_backward(
        state_two, gain_attn, small[3:4], cos_two[...], sin_two[...], bias_two, w_attn, normed_in_r.at[two],
        qk_two, v_two, log_two, d_attn_in_r[two], d_gating, gating_two, d_att_two, d_raw_two,
        d_qk_in_r.at[two], d_v_in_r.at[two],
    )
    back_two = back_three + d_rows + d_after

    incoming = cotangent[...].astype(wide_type) + pick_exact(put_two, back_two)
    d_input_ref[...] = incoming
    d_change = scale_one * incoming
    d_gating = jnp.where(valid, jnp.sum(total_one[...] * incoming, axis=-1, keepdims=True), 0.0)
    d_gating_ref[...] = jnp.broadcast_to(d_gating, d_gating_ref.shape)
    d_ffn_one[...] = d_change.astype(narrow_dtype)
    after_one = hidden_in[...].astype(wide_type) + attn_out_ref[...]
    d_after, gain_ffn_one = ffn_backward(
        after_one, gain_ffn, w_gate, w_up, w_down, d_ffn_one, gate_one, up_one, d_gate_one, d_up_one, total_one, CHUNK
    )
    d_attn_one[...] = (scale_one * d_input_ref[...] + d_after).astype(narrow_dtype)
    d_input_ref[...] += d_after
    small_out[...] = jnp.zeros_like(small_out)
    small_out[0:1] = gain_attn_two + gain_attn_three
    small_out[1:2] = gain_ffn_one + gain_ffn_two + gain_ffn_three
    small_out[3:4] = router_two
    small_out[4:5] = router_three


def rotary_tables(positions):
    half = HEAD_SIZE // 2
    lanes = jnp.arange(2 * HEAD_SIZE)
    frequency = 10000.0 ** (-(lanes % half).astype(wide_type) / half)
    angles = positions.astype(wide_type)[:, None] * frequency[None, :]
    sign = jnp.where(lanes % HEAD_SIZE < half, -1.0, 1.0)
    return jnp.cos(angles), jnp.sin(angles) * sign[None, :]


def call(kernel, operands, outputs, scratch=(), hbm=(), scalars=1, flops=0):
    specs = [
        pl.BlockSpec(memory_space=pltpu.SMEM if i < scalars else (pl.ANY if i in hbm else pltpu.VMEM))
        for i in range(len(operands))
    ]
    return pl.pallas_call(
        kernel,
        out_shape=[jax.ShapeDtypeStruct(shape, kind) for shape, kind in outputs],
        in_specs=specs,
        out_specs=[pl.BlockSpec(memory_space=pltpu.VMEM)] * len(outputs),
        scratch_shapes=list(scratch),
        compiler_params=pltpu.CompilerParams(vmem_limit_bytes=VMEM_LIMIT),
        cost_estimate=pl.CostEstimate(flops=flops, bytes_accessed=flops // 400, transcendentals=0),
    )(*operands)


def partner(value, axis, bit):
    count = lax.axis_size(axis)
    return lax.ppermute(value, axis, [(i, i ^ bit) for i in range(count)])


def side(axis, bit):
    return (lax.axis_index(axis) // bit) % 2


def take_half(value, axis, bit, dim):
    size = value.shape[dim] // 2
    which = side(axis, bit)
    keep = lax.dynamic_slice_in_dim(value, which * size, size, dim)
    send = lax.dynamic_slice_in_dim(value, (1 - which) * size, size, dim)
    return keep, send


def add_half(value, axis, bit, dim):
    keep, send = take_half(value, axis, bit, dim)
    received = partner(send, axis, bit)
    return (keep.astype(wide_type) + received.astype(wide_type)).astype(narrow_dtype)


def join_half(value, axis, bit, dim):
    received = partner(value, axis, bit)
    first = side(axis, bit) == 0
    return jnp.where(
        first,
        jnp.concatenate([value, received], axis=dim),
        jnp.concatenate([received, value], axis=dim),
    )


def bits_of(axis, low):
    found = []
    bit = low
    while bit < lax.axis_size(axis):
        found.append(bit)
        bit = bit * 2
    return found


def split_steps(row_steps):
    steps = [("dp", 1, 0), ("dp", 2, 0)]
    return steps + [("dp", bit, 0 if row_steps else 1) for bit in bits_of("dp", 4)]


def reduce_matrix(gradient, row_steps):
    owners = lax.axis_size("fsdp")
    rows, columns = gradient.shape
    value = gradient.reshape(owners, rows // owners, columns)
    value = add_half(value, "dp", 1, 1)
    for bit in reversed(bits_of("fsdp", 1)):
        value = add_half(value, "fsdp", bit, 0)
    value = value[0]
    steps = split_steps(row_steps)
    for axis, bit, dim in steps[1:]:
        value = add_half(value, axis, bit, dim)
    for axis, bit, dim in reversed(steps):
        value = join_half(value, axis, bit, dim)
    return value


def place(parts, rows, shape):
    full = jnp.zeros(shape, narrow_dtype)
    for index, part in parts:
        full = lax.dynamic_update_slice_in_dim(full, part, index * rows, 0)
    return full


def gather_near(shard):
    owners = lax.axis_size("fsdp")
    mine = lax.axis_index("fsdp")
    half, _ = take_half(shard, "dp", 1, 0)
    parts = [(mine, shard)]
    for offset in range(1, owners):
        parts.append((mine ^ offset, join_half(partner(half, "fsdp", offset), "dp", 1, 0)))
    return place(parts, shard.shape[0], (shard.shape[0] * owners,) + shard.shape[1:])


def gather_far(shard, row_steps):
    owners = lax.axis_size("fsdp")
    mine = lax.axis_index("fsdp")
    steps = split_steps(row_steps)
    piece = shard
    for axis, bit, dim in steps:
        piece, _ = take_half(piece, axis, bit, dim)
    parts = [(mine, shard)]
    for offset in range(1, owners):
        other = partner(piece, "fsdp", offset)
        for axis, bit, dim in reversed(steps):
            other = join_half(other, axis, bit, dim)
        parts.append((mine ^ offset, other))
    return place(parts, shard.shape[0], (shard.shape[0] * owners,) + shard.shape[1:])


def local(
    hidden_in,
    cotangent,
    norm_attn,
    norm_ffn,
    router,
    w_query,
    key_weight,
    value_weight,
    w_out,
    w_gate,
    w_up,
    w_down,
    lengths,
    chosen_second,
    chosen_third,
):
    owners = lax.axis_size("fsdp")
    mine = lax.axis_index("fsdp")
    small = jnp.concatenate(
        [norm_attn[None, :], norm_ffn[None, :], router.T, jnp.zeros((11, norm_attn.shape[0]), wide_type)]
    ).astype(narrow_dtype)
    small_parts = [(mine, small)] + [
        (mine ^ offset, partner(small, "fsdp", offset)) for offset in range(1, owners)
    ]
    small_rows = jnp.zeros((16, owners * small.shape[1]), narrow_dtype)
    for index, part in small_parts:
        small_rows = lax.dynamic_update_slice_in_dim(small_rows, part, index * small.shape[1], 1)
    width = w_query.shape[1]
    kv_width = key_weight.shape[1]
    attn_shard = jnp.concatenate([w_query, key_weight, w_out, value_weight], axis=1).astype(narrow_dtype)
    attn_full = gather_near(attn_shard)
    gate_full = gather_far(w_gate.astype(narrow_dtype), False)
    up_full = gather_far(w_up.astype(narrow_dtype), False)
    down_full = gather_far(w_down.astype(narrow_dtype), True)
    small_wide = small_rows[:8].astype(wide_type)
    count_one, model = hidden_in.shape
    ff = gate_full.shape[1]
    chosen_two, chosen_three = chosen_second[0], chosen_third[0]
    count_two, count_three = chosen_two.shape[0], chosen_three.shape[0]
    count_rest = count_two + count_three
    cos_one, sin_one = rotary_tables(jnp.arange(count_one))
    cos_two, sin_two = rotary_tables(chosen_two)
    cos_three, sin_three = rotary_tables(chosen_three)
    v_width = attn_full.shape[1] - V_START

    normed_one, qk_one, v_one, att_one, log_one, attn_out_one, gating_one = call(
        first_attention_kernel,
        (lengths, hidden_in, small_wide, cos_one, sin_one, attn_full),
        [
            ((count_one, model), narrow_dtype),
            ((count_one, QK_WIDTH), narrow_dtype),
            ((count_one, v_width), narrow_dtype),
            ((count_one, model), narrow_dtype),
            ((GROUP * count_one, 128), wide_type),
            ((count_one, model), wide_type),
            ((count_one, 128), wide_type),
        ],
    )
    rest = lambda width: ((count_rest, width), narrow_dtype)
    first = lambda width: ((count_one, width), narrow_dtype)
    scratch_for = lambda count: [
        pltpu.VMEM((count, QK_WIDTH), narrow_dtype),
        pltpu.VMEM((count, v_width), narrow_dtype),
        pltpu.VMEM((GROUP * count, 128), wide_type),
    ]
    back_scratch = lambda count: [
        pltpu.VMEM((count, model), narrow_dtype),
        pltpu.VMEM((count, QK_WIDTH), wide_type),
    ]
    wide = lambda count, width: pltpu.VMEM((count, width), wide_type)
    (
        hidden_out, d_input, d_gating_one, small_middle,
        hidden_one, d_ffn_one, ffn_one, d_gate_one, d_up_one, d_attn_one,
        hidden_r, d_ffn_r, ffn_r, d_gate_r, d_up_r, d_attn_r, att_r, normed_r, d_qk_r, d_v_r,
    ) = call(
        middle_kernel,
        (
            lengths, hidden_in, cotangent, small_wide, attn_out_one, gating_one, cos_two, sin_two, cos_three, sin_three,
            chosen_two[:, None], chosen_two[None, :], chosen_three[:, None], chosen_three[None, :],
            attn_full, gate_full, up_full, down_full,
        ),
        [
            first(model), ((count_one, model), wide_type), ((count_one, 128), wide_type), ((8, model), wide_type),
            first(ff), first(model), first(model), first(ff), first(ff), first(model),
            rest(ff), rest(model), rest(model), rest(ff), rest(ff), rest(model), rest(model), rest(model),
            rest(QK_WIDTH), rest(v_width),
        ],
        [
            pltpu.VMEM(attn_full.shape, narrow_dtype),
            pltpu.VMEM(gate_full.shape, narrow_dtype),
            pltpu.VMEM(up_full.shape, narrow_dtype),
            pltpu.VMEM(down_full.shape, narrow_dtype),
            pltpu.SemaphoreType.DMA((4,)),
            wide(count_one, ff), wide(count_one, ff), wide(count_two, ff), wide(count_two, ff),
            wide(count_three, ff), wide(count_three, ff),
            wide(count_one, model), wide(count_two, model), wide(count_three, model),
        ]
        + scratch_for(count_two) + scratch_for(count_three) + back_scratch(count_two) + back_scratch(count_three),
        hbm=(14, 15, 16, 17),
    )
    d_qk_one, d_v_one, grad_hidden, small_last = call(
        last_attention_kernel,
        (
            lengths, hidden_in, small_wide, cos_one, sin_one, attn_full, normed_one, qk_one, v_one, log_one, gating_one,
            d_gating_one, d_attn_one, d_input,
        ),
        [
            first(QK_WIDTH), first(v_width), ((count_one, model), wide_type), ((8, model), wide_type),
        ],
        back_scratch(count_one),
    )

    def outer(left, left_r, right, right_r):
        left = jnp.concatenate([left, left_r])
        right = jnp.concatenate([right, right_r])
        return jnp.einsum("na,nb->ab", left, right, preferred_element_type=wide_type).astype(narrow_dtype)

    down_shard = reduce_matrix(outer(hidden_one, hidden_r, d_ffn_one, d_ffn_r), True).astype(wide_type)
    gate_shard = reduce_matrix(outer(ffn_one, ffn_r, d_gate_one, d_gate_r), False).astype(wide_type)
    up_shard = reduce_matrix(outer(ffn_one, ffn_r, d_up_one, d_up_r), False).astype(wide_type)
    skip = V_HEAD * HEAD_SIZE
    attn_grad = jnp.concatenate(
        [
            outer(normed_one, normed_r, d_qk_one, d_qk_r),
            outer(att_one, att_r, d_attn_one, d_attn_r),
            outer(normed_one, normed_r, d_v_one[:, skip:], d_v_r[:, skip:]),
        ],
        axis=1,
    )
    attn_out_shard = reduce_matrix(attn_grad, False).astype(wide_type)
    small_sum = lax.psum(small_middle + small_last, ("dp", "fsdp"))
    small_sum = lax.dynamic_slice_in_dim(small_sum, mine * small.shape[1], small.shape[1], 1)
    return (
        hidden_out,
        grad_hidden,
        small_sum[0],
        small_sum[1],
        small_sum[2:5].T,
        attn_out_shard[:, :width],
        attn_out_shard[:, width : width + kv_width],
        attn_out_shard[:, 2 * width + kv_width :],
        attn_out_shard[:, width + kv_width : 2 * width + kv_width],
        gate_shard,
        up_shard,
        down_shard,
    )


def solution(mesh):
    in_specs = (
        P(("dp", "fsdp"), None),
        P(("dp", "fsdp"), None),
        P("fsdp"),
        P("fsdp"),
        P("fsdp", None),
        P("fsdp", None),
        P("fsdp", None),
        P("fsdp", None),
        P("fsdp", None),
        P("fsdp", None),
        P("fsdp", None),
        P("fsdp", None),
        P(("dp", "fsdp")),
        P(("dp", "fsdp"), None),
        P(("dp", "fsdp"), None),
    )
    out_specs = (
        P(("dp", "fsdp"), None),
        P(("dp", "fsdp"), None),
        P("fsdp"),
        P("fsdp"),
        P("fsdp", None),
        P("fsdp", None),
        P("fsdp", None),
        P("fsdp", None),
        P("fsdp", None),
        P("fsdp", None),
        P("fsdp", None),
        P("fsdp", None),
    )
    return jax.shard_map(local, mesh=mesh, in_specs=in_specs, out_specs=out_specs, check_vma=False)
```

time: 890 us -> 614 us (0.69)
  matrix products: 263 us -> 22.5 us
  Pallas kernels: 0 us -> 80.8 us
  local copies, waits for them, and re-layouts: 168 us -> 106 us
  other arithmetic: 121 us -> 77.1 us
  starting transfers between devices: 67.8 us -> 86.1 us
  waiting for transfers between devices: 208 us -> 191 us
    dot_general x153 -> x0, matrix products: 241 us -> none  [the longest x15 24.4 us: head_backward(): jnp.einsum('gqk,kd->qgd', d_raw, rotated_keys, preferred_element_type=wid...]
    pallas_call x0 -> x3, Pallas kernels: none -> 80.8 us  [call(): pl.pallas_call(kernel, out_shape=[jax.ShapeDtypeStruct(shape, kind) for s...]
    ppermute x54, starting transfers between devices: 67.8 us -> 86.1 us  [partner(): return lax.ppermute(value, axis, [(i, i ^ bit) for i in range(count)])]
    ppermute x54, waiting for transfers between devices: 208 us -> 191 us  [partner(): return lax.ppermute(value, axis, [(i, i ^ bit) for i in range(count)])]
    reshape x7 -> x0, local copies, waits for them, and re-layouts: 13.8 us -> none  [the longest x1 11 us: reduce_matrix(): value = gradient.reshape(owners, rows // owners, columns)]
    unnamed x429 -> x84, local copies, waits for them, and re-layouts: 37.1 us -> 25.8 us
    sub x15 -> x0, local copies, waits for them, and re-layouts: 9.94 us -> none  [head_backward(): probabilities = jnp.exp(scores - log_total)]
    convert_element_type x19 -> x7, other arithmetic: 18.2 us -> 14.6 us  [the longest x1 5.58 us: local(): reduce_matrix(outer(ffn_one, ffn_r, d_up_one, d_up_r), False)]
  transfers between devices with their start and end apart: 54 -> 54, of which waited for: 21 -> 22; matrix products, arithmetic and copies ran while one was open for 25% -> 27% of each run, Pallas kernels for 0% -> 4%
where the time goes in v1:
time: 614 us; the launch traced here: 605 us
  waiting for transfers between devices  191 us (31%)
  local copies, waits for them, and re-layouts  106 us (17%)
  starting transfers between devices  86.1 us (14%)
  Pallas kernels  80.8 us (13%)
  other arithmetic  77.1 us (13%)
  blocking collectives  38.3 us (6%)
  matrix products  22.5 us (4%)
    ppermute x54, waiting for transfers between devices, partner(): return lax.ppermute(value, axis, [(i, i ^ bit) for i in range(count)])  191 us
    ppermute x54, starting transfers between devices, partner(): return lax.ppermute(value, axis, [(i, i ^ bit) for i in range(count)])  86.1 us
    pallas_call x3, Pallas kernels, call(): pl.pallas_call(kernel, out_shape=[jax.ShapeDtypeStruct(shape, kind) for s...  80.8 us
    psum x1, blocking collectives, local(): small_sum = lax.psum(small_middle + small_last, ('dp', 'fsdp'))  38.3 us
    unnamed x84, local copies, waits for them, and re-layouts  25.8 us
    dot_general x6, matrix products, outer(): jnp.einsum('na,nb->ab', left, right, preferred_element_type=wide_type)  22.5 us
    convert_element_type x20, other arithmetic, add_half(): (keep.astype(wide_type) + received.astype(wide_type)).astype(narrow_dtype)  20.8 us
    dynamic_slice x22, local copies, waits for them, and re-layouts, take_half(): send = lax.dynamic_slice_in_dim(value, (1 - which) * size, size, dim)  18.8 us
  transfers between devices with their start and end apart: 54, of which 22 were waited for; matrix products, arithmetic and copies ran while one was open for 27% of the time, Pallas kernels for 4%

profile of v1, /device:TPU:1, one launch (start us, length us, event | category | flops | bytes accessed | tf_op | source)
XLA Modules:
  0.0 605.0 jit_solution(12632243358960377834)
XLA Ops:
  0.8 3.6 copy.72
  20.7 3.5 concatenate.218
  31.3 3.0 broadcast_in_dim.44
  43.0 10.6 %collective-permute-done.14 = bf16[80,960]{1,0:T(8,128)(2,1)S(1)} collective-permute-done((bf16[80,960]{1,0:T(8,128)(2,1)}, bf16[80,960]{1,0:T(8,128)(2,1)S(1)}, u32[]{:S(2)}, u32[]{:S(2)}) %collective-permute-start.14) | collective-permute-done | bytes 153632 | tf_op jit(solution)/shard_map/ppermute | solution.py:363
  62.9 5.3 collective-permute-done.15
  69.8 5.1 collective-permute-done.10
  76.3 5.1 collective-permute-done.5
  88.8 8.7 %collective-permute-done.11 = bf16[120,2560]{1,0:T(8,128)(2,1)} collective-permute-done((bf16[120,2560]{1,0:T(8,128)(2,1)S(1)}, bf16[120,2560]{1,0:T(8,128)(2,1)}, u32[]{:S(2)}, u32[]{:S(2)}) %collective-permute-start.11) | collective-permute-done | bytes 614432 | tf_op jit(solution)/shard_map/ppermute | solution.py:363
  113.3 3.9 fusion.2.weight.w_attn_hbm
  117.2 10.3 %shard_map.238 = (bf16[256,960]{1,0:T(8,128)(2,1)}, bf16[256,1280]{1,0:T(8,128)(2,1)}, bf16[256,384]{1,0:T(8,128)(2,1)}, bf16[256,960]{1,0:T(8,128)(2,1)}, f32[7...) custom-call(s32[1]{0:T(128)S(6)} %copy.107.length_ref, bf16[256,960]{1,0:T(8,128)(2,1)} %copy.76.hidden_in, ...), custom_call_target="tpu_custom_call" | custom-call | tf_op jit(solution)/shard_map/pallas_call | solution.py:350
  129.1 3.9 fusion.4.w_up_hbm
  135.6 3.8 fusion.3.w_gate_hbm
  139.4 57.1 %shard_map.239 = (bf16[256,960]{1,0:T(8,128)(2,1)}, f32[256,960]{1,0:T(8,128)}, f32[256,128]{1,0:T(8,128)}, f32[8,960]{1,0:T(8,128)}, bf16[256,2560]{1,0:T(8,128...) custom-call(s32[1]{0:T(128)S(6)} %copy.107.length_ref, ...), custom_call_target="tpu_custom_call" | custom-call | tf_op jit(solution)/shard_map/pallas_call | solution.py:350
  196.5 6.8 %convolution_convert_fusion = bf16[2560,960]{0,1:T(8,128)(2,1)} fusion(bf16[160,2560]{1,0:T(8,128)(2,1)} %get-tuple-element.71, bf16[256,2560]{1,0:T(8,128)(2,1)} %get-tuple-element.70, bf16[160,960]{1,0:T(8,128)(2,1)} %get-tuple-element.73, bf16[256,960]{1,0:T(8,128)(2,1)} %get-tuple-element.72), kind=kOutput, calls=%fused_computation | convolution fusion | flops 2053038080 | bytes 7843840 | tf_op jit(solution)/shard_map/na,nb->ab/dot_general | solution.py:573
  203.2 7.9 %copy.82 = bf16[2560,960]{1,0:T(8,128)(2,1)} copy(bf16[2560,960]{0,1:T(8,128)(2,1)} %convolution_convert_fusion) | data formatting | bytes 9830400 | tf_op jit(solution)/shard_map/convert_element_type | solution.py:573
  215.8 4.4 convolution_convert_fusion.1
  223.9 3.4 convolution_convert_fusion.2
  230.3 13.5 %shard_map.240 = (bf16[256,1280]{1,0:T(8,128)(2,1)}, bf16[256,384]{1,0:T(8,128)(2,1)}, f32[256,960]{1,0:T(8,128)}, f32[8,960]{1,0:T(8,128)}) custom-call(s32[1]{0:T(128)S(6)} %copy.107.length_ref, bf16[256,960]{1,0:T(8,128)(2,1)} %copy.76.hidden_in, f32[8,960]{1,0:T(8,128)} %slice_convert_fusion.small, f32[256,128]{1,0:T(8,128)} %get-tuple-element.121.cosines, ...), custom_call_target="tpu_custom_call" | custom-call | tf_op jit(solution)/shard_map/pallas_call | solution.py:350
  250.6 3.8 convolution_convert_fusion.4
  254.4 7.5 %concatenate.250 = bf16[960,2560]{1,0:T(8,128)(2,1)} concatenate(bf16[960,1280]{1,0:T(8,128)(2,1)S(1)} %convolution_convert_fusion.3, bf16[960,960]{1,0:T(8,128)(2,1)} %convolution_convert_fusion.4, bf16[960,320]{1,0:T(8,128)(2,1)S(1)} %copy.81), dimensions={1} | concatenate | bytes 9830400 | tf_op jit(solution)/shard_map/concatenate | solution.py:579
  261.9 3.4 constant_dynamic-slice_fusion.16
  268.1 38.3 %psum.7 = f32[8,960]{1,0:T(8,128)S(1)} all-reduce(f32[8,960]{1,0:T(8,128)S(1)} %add.330), channel_id=1, replica_groups=mesh['dp'=16,'fsdp'=2] {'dp','fsdp'}, use_global_device_ids=true, to_apply=%region_0.1 | all-reduce | flops 7680 | bytes 61440 | tf_op jit(solution)/shard_map/psum | solution.py:588
  307.1 4.5 copy.84
  311.6 3.8 add_convert_fusion
  320.4 3.0 add_convert_fusion.1
  326.0 3.6 add_convert_fusion.2
  337.2 8.9 %collective-permute-done.46 = bf16[1,640,960]{1,2,0:T(8,128)(2,1)} collective-permute-done((bf16[1,640,960]{1,2,0:T(8,128)(2,1)}, bf16[1,640,960]{1,2,0:T(8,128)(2,1)}, u32[]{:S(2)}, u32[]{:S(2)}) %collective-permute-start.46) | collective-permute-done | bytes 1228832 | tf_op jit(solution)/shard_map/ppermute | solution.py:363
  351.9 20.5 %collective-permute-done.37 = bf16[1,240,2560]{2,1,0:T(8,128)(2,1)} collective-permute-done((bf16[1,240,2560]{2,1,0:T(8,128)(2,1)}, bf16[1,240,2560]{2,1,0:T(8,128)(2,1)}, u32[]{:S(2)}, u32[]{:S(2)}) %collective-permute-start.37) | collective-permute-done | bytes 1228832 | tf_op jit(solution)/shard_map/ppermute | solution.py:363
  375.5 23.3 %collective-permute-done.28 = bf16[1,240,2560]{2,1,0:T(8,128)(2,1)} collective-permute-done((bf16[1,240,2560]{2,1,0:T(8,128)(2,1)}, bf16[1,240,2560]{2,1,0:T(8,128)(2,1)}, u32[]{:S(2)}, u32[]{:S(2)}) %collective-permute-start.28) | collective-permute-done | bytes 1228832 | tf_op jit(solution)/shard_map/ppermute | solution.py:363
  401.8 23.3 %collective-permute-done.19 = bf16[1,240,2560]{2,1,0:T(8,128)(2,1)} collective-permute-done((bf16[1,240,2560]{2,1,0:T(8,128)(2,1)}, bf16[1,240,2560]{2,1,0:T(8,128)(2,1)}, u32[]{:S(2)}, u32[]{:S(2)}) %collective-permute-start.19) | collective-permute-done | bytes 1228832 | tf_op jit(solution)/shard_map/ppermute | solution.py:363
  432.6 7.1 %collective-permute-done.20 = bf16[120,2560]{1,0:T(8,128)(2,1)S(1)} collective-permute-done((bf16[120,2560]{1,0:T(8,128)(2,1)S(1)}, bf16[120,2560]{1,0:T(8,128)(2,1)S(1)}, u32[]{:S(2)}, u32[]{:S(2)}) %collective-permute-start.20) | collective-permute-done | bytes 614432 | tf_op jit(solution)/shard_map/ppermute | solution.py:363
  444.8 9.1 %collective-permute-done.30 = bf16[120,1280]{1,0:T(8,128)(2,1)S(1)} collective-permute-done((bf16[120,1280]{1,0:T(8,128)(2,1)S(1)}, bf16[120,1280]{1,0:T(8,128)(2,1)S(1)}, u32[]{:S(2)}, u32[]{:S(2)}) %collective-permute-start.30) | collective-permute-done | bytes 307232 | tf_op jit(solution)/shard_map/ppermute | solution.py:363
  454.2 9.1 %collective-permute-done.21 = bf16[120,1280]{1,0:T(8,128)(2,1)S(1)} collective-permute-done((bf16[120,1280]{1,0:T(8,128)(2,1)S(1)}, bf16[120,1280]{1,0:T(8,128)(2,1)S(1)}, u32[]{:S(2)}, u32[]{:S(2)}) %collective-permute-start.21) | collective-permute-done | bytes 307232 | tf_op jit(solution)/shard_map/ppermute | solution.py:363
  466.1 16.5 %collective-permute-done.22 = bf16[120,640]{1,0:T(8,128)(2,1)S(1)} collective-permute-done((bf16[120,640]{1,0:T(8,128)(2,1)S(1)}, bf16[120,640]{1,0:T(8,128)(2,1)S(1)}, u32[]{:S(2)}, u32[]{:S(2)}) %collective-permute-start.22) | collective-permute-done | bytes 153632 | tf_op jit(solution)/shard_map/ppermute | solution.py:363
  485.1 15.7 %collective-permute-done.23 = bf16[120,640]{1,0:T(8,128)(2,1)S(1)} collective-permute-done((bf16[120,640]{1,0:T(8,128)(2,1)S(1)}, bf16[120,640]{1,0:T(8,128)(2,1)S(1)}, u32[]{:S(2)}, u32[]{:S(2)}) %collective-permute-start.23) | collective-permute-done | bytes 153632 | tf_op jit(solution)/shard_map/ppermute | solution.py:363
  502.8 7.4 %collective-permute-done.24 = bf16[120,1280]{1,0:T(8,128)(2,1)S(1)} collective-permute-done((bf16[120,1280]{1,0:T(8,128)(2,1)S(1)}, bf16[120,1280]{1,0:T(8,128)(2,1)S(1)}, u32[]{:S(2)}, u32[]{:S(2)}) %collective-permute-start.24) | collective-permute-done | bytes 307232 | tf_op jit(solution)/shard_map/ppermute | solution.py:363
  511.0 6.2 %collective-permute-done.51 = bf16[160,960]{1,0:T(8,128)(2,1)S(1)} collective-permute-done((bf16[160,960]{1,0:T(8,128)(2,1)S(1)}, bf16[160,960]{1,0:T(8,128)(2,1)S(1)}, u32[]{:S(2)}, u32[]{:S(2)}) %collective-permute-start.51) | collective-permute-done | bytes 307232 | tf_op jit(solution)/shard_map/ppermute | solution.py:363
  517.9 5.9 collective-permute-done.42
  524.7 7.5 %collective-permute-start.26 = (bf16[240,2560]{1,0:T(8,128)(2,1)S(1)}, bf16[240,2560]{1,0:T(8,128)(2,1)}, u32[]{:S(2)}, u32[]{:S(2)}) collective-permute-start(bf16[240,2560]{1,0:T(8,128)(2,1)S(1)} %maximum_select_fusion.12), channel_id=1, source_target_pairs={{0,2},{2,0},{4,6},{6,4},{8,10},{10,8},{12,14},{14,12},{16,18},{18,... | collective-permute-start | bytes 3686408 | tf_op jit(solution)/shard_map/ppermute | solution.py:363
  537.2 10.7 %collective-permute-start.53 = (bf16[640,960]{0,1:T(8,128)(2,1)}, bf16[640,960]{0,1:T(8,128)(2,1)}, u32[]{:S(2)}, u32[]{:S(2)}) collective-permute-start(bf16[640,960]{0,1:T(8,128)(2,1)} %copy.87), channel_id=1, source_target_pairs={{0,2},{2,0},{4,6},{6,4},{8,10},{10,8},{12,14},{14,12},{16,18},{18,... | collective-permute-start | bytes 3686408 | tf_op jit(solution)/shard_map/ppermute | solution.py:363
  551.1 10.7 %collective-permute-start.44 = (bf16[240,2560]{1,0:T(8,128)(2,1)}, bf16[240,2560]{1,0:T(8,128)(2,1)}, u32[]{:S(2)}, u32[]{:S(2)}) collective-permute-start(bf16[240,2560]{1,0:T(8,128)(2,1)} %maximum_select_fusion.14), channel_id=1, source_target_pairs={{0,2},{2,0},{4,6},{6,4},{8,10},{10,8},{12,14},{14,12},{16,18},{18,... | collective-permute-start | bytes 3686408 | tf_op jit(solution)/shard_map/ppermute | solution.py:363
  564.7 5.4 collective-permute-start.35
  570.2 4.6 fusion.5
  576.4 3.0 fusion.1
  579.4 5.8 copy.94
  589.2 4.6 fusion.49
  593.9 5.6 fusion.7
  599.4 5.3 fusion.6
  (285 shorter events, 158.5 us)
Async XLA Ops:
  5.2 32.1 %collective-permute-start.13 = (bf16[80,960]{1,0:T(8,128)(2,1)}, bf16[80,960]{1,0:T(8,128)(2,1)}, u32[]{:S(2)}, u32[]{:S(2)}) collective-permute-start(bf16[80,960]{1,0:T(8,128)(2,1)} %constant_dynamic-slice_fusion.17), channel_id=1, source_target_pairs={{0,1},{1,0},{2,3},{3,2},{4,5},{5,4},{6,7},{7,6},{8,9},{9,8},{10,11... | collective-permute-start | bytes 460808 | tf_op jit(solution)/shard_map/ppermute | solution.py:363
  10.8 28.8 %collective-permute-start.8 = (bf16[120,640]{1,0:T(8,128)(2,1)}, bf16[120,640]{1,0:T(8,128)(2,1)}, u32[]{:S(2)}, u32[]{:S(2)}) collective-permute-start(bf16[120,640]{1,0:T(8,128)(2,1)} %dynamic_slice.174), channel_id=1, source_target_pairs={{0,1},{1,0},{2,3},{3,2},{4,5},{5,4},{6,7},{7,6},{8,9},{9,8},{10,11... | collective-permute-start | bytes 460808 | tf_op jit(solution)/shard_map/ppermute | solution.py:363
  16.5 24.3 %collective-permute-start.3 = (bf16[120,640]{1,0:T(8,128)(2,1)}, bf16[120,640]{1,0:T(8,128)(2,1)}, u32[]{:S(2)}, u32[]{:S(2)}) collective-permute-start(bf16[120,640]{1,0:T(8,128)(2,1)} %dynamic_slice.173), channel_id=1, source_target_pairs={{0,1},{1,0},{2,3},{3,2},{4,5},{5,4},{6,7},{7,6},{8,9},{9,8},{10,11... | collective-permute-start | bytes 460808 | tf_op jit(solution)/shard_map/ppermute | solution.py:363
  25.4 57.5 %collective-permute-start.1 = (bf16[240,2560]{1,0:T(8,128)(2,1)}, bf16[240,2560]{1,0:T(8,128)(2,1)}, u32[]{:S(2)}, u32[]{:S(2)}) collective-permute-start(bf16[240,2560]{1,0:T(8,128)(2,1)} %constant_dynamic-slice_fusion.18), channel_id=1, source_target_pairs={{0,1},{1,0},{2,3},{3,2},{4,5},{5,4},{6,7},{7,6},{8,9},{9,8},{10,11... | collective-permute-start | bytes 3686408 | tf_op jit(solution)/shard_map/ppermute | solution.py:363
  26.3 83.5 %collective-permute-start = (bf16[16,480]{1,0:T(8,128)(2,1)S(1)}, bf16[16,480]{1,0:T(8,128)(2,1)S(1)}, u32[]{:S(2)}, u32[]{:S(2)}) collective-permute-start(bf16[16,480]{1,0:T(8,128)(2,1)S(1)} %maximum_maximum_fusion), channel_id=1, source_target_pairs={{0,1},{1,0},{2,3},{3,2},{4,5},{5,4},{6,7},{7,6},{8,9},{9,8},{10,11... | collective-permute-start | bytes 46088 | tf_op jit(solution)/shard_map/ppermute | solution.py:363
  37.3 16.3 %collective-permute-start.14 = (bf16[80,960]{1,0:T(8,128)(2,1)}, bf16[80,960]{1,0:T(8,128)(2,1)S(1)}, u32[]{:S(2)}, u32[]{:S(2)}) collective-permute-start(bf16[80,960]{1,0:T(8,128)(2,1)} %collective-permute-done.13), channel_id=1, source_target_pairs={{0,16},{2,18},{4,20},{6,22},{8,24},{10,26},{12,28},{14,30},{16,0},... | collective-permute-start | bytes 460808 | tf_op jit(solution)/shard_map/ppermute | solution.py:363
  39.7 17.2 %collective-permute-start.9 = (bf16[120,640]{1,0:T(8,128)(2,1)}, bf16[120,640]{1,0:T(8,128)(2,1)S(1)}, u32[]{:S(2)}, u32[]{:S(2)}) collective-permute-start(bf16[120,640]{1,0:T(8,128)(2,1)} %collective-permute-done.8), channel_id=1, source_target_pairs={{0,16},{2,18},{4,20},{6,22},{8,24},{10,26},{12,28},{14,30},{16,0},... | collective-permute-start | bytes 460808 | tf_op jit(solution)/shard_map/ppermute | solution.py:363
  40.7 19.5 %collective-permute-start.4 = (bf16[120,640]{1,0:T(8,128)(2,1)}, bf16[120,640]{1,0:T(8,128)(2,1)S(1)}, u32[]{:S(2)}, u32[]{:S(2)}) collective-permute-start(bf16[120,640]{1,0:T(8,128)(2,1)} %collective-permute-done.3), channel_id=1, source_target_pairs={{0,16},{2,18},{4,20},{6,22},{8,24},{10,26},{12,28},{14,30},{16,0},... | collective-permute-start | bytes 460808 | tf_op jit(solution)/shard_map/ppermute | solution.py:363
  58.0 16.9 %collective-permute-start.10 = (bf16[120,1280]{1,0:T(8,128)(2,1)S(1)}, bf16[120,1280]{1,0:T(8,128)(2,1)S(1)}, u32[]{:S(2)}, u32[]{:S(2)}) collective-permute-start(bf16[120,1280]{1,0:T(8,128)(2,1)S(1)} %maximum_select_fusion.25), channel_id=1, source_target_pairs={{0,8},{2,10},{4,12},{6,14},{8,0},{10,2},{12,4},{14,6},{16,24},{18,... | collective-permute-start | bytes 921608 | tf_op jit(solution)/shard_map/ppermute | solution.py:363
  61.3 20.2 %collective-permute-start.5 = (bf16[120,1280]{1,0:T(8,128)(2,1)S(1)}, bf16[120,1280]{1,0:T(8,128)(2,1)S(1)}, u32[]{:S(2)}, u32[]{:S(2)}) collective-permute-start(bf16[120,1280]{1,0:T(8,128)(2,1)S(1)} %maximum_select_fusion.24), channel_id=1, source_target_pairs={{0,8},{2,10},{4,12},{6,14},{8,0},{10,2},{12,4},{14,6},{16,24},{18,... | collective-permute-start | bytes 921608 | tf_op jit(solution)/shard_map/ppermute | solution.py:363
  68.5 15.8 %collective-permute-start.16 = (bf16[320,960]{1,0:T(8,128)(2,1)S(1)}, bf16[320,960]{1,0:T(8,128)(2,1)S(1)}, u32[]{:S(2)}, u32[]{:S(2)}) collective-permute-start(bf16[320,960]{1,0:T(8,128)(2,1)S(1)} %maximum_select_fusion.15), channel_id=1, source_target_pairs={{0,4},{2,6},{4,0},{6,2},{8,12},{10,14},{12,8},{14,10},{16,20},{18,... | collective-permute-start | bytes 1843208 | tf_op jit(solution)/shard_map/ppermute | solution.py:363
  75.0 22.5 %collective-permute-start.11 = (bf16[120,2560]{1,0:T(8,128)(2,1)S(1)}, bf16[120,2560]{1,0:T(8,128)(2,1)}, u32[]{:S(2)}, u32[]{:S(2)}) collective-permute-start(bf16[120,2560]{1,0:T(8,128)(2,1)S(1)} %maximum_select_fusion.18), channel_id=1, source_target_pairs={{0,4},{2,6},{4,0},{6,2},{8,12},{10,14},{12,8},{14,10},{16,20},{18,... | collective-permute-start | bytes 1843208 | tf_op jit(solution)/shard_map/ppermute | solution.py:363
  81.6 29.2 %collective-permute-start.6 = (bf16[120,2560]{1,0:T(8,128)(2,1)S(1)}, bf16[120,2560]{1,0:T(8,128)(2,1)S(1)}, u32[]{:S(2)}, u32[]{:S(2)}) collective-permute-start(bf16[120,2560]{1,0:T(8,128)(2,1)S(1)} %maximum_select_fusion.17), channel_id=1, source_target_pairs={{0,4},{2,6},{4,0},{6,2},{8,12},{10,14},{12,8},{14,10},{16,20},{18,... | collective-permute-start | bytes 1843208 | tf_op jit(solution)/shard_map/ppermute | solution.py:363
  82.9 30.4 %collective-permute-start.2 = (bf16[240,2560]{1,0:T(8,128)(2,1)}, bf16[240,2560]{1,0:T(8,128)(2,1)}, u32[]{:S(2)}, u32[]{:S(2)}) collective-permute-start(bf16[240,2560]{1,0:T(8,128)(2,1)} %collective-permute-done.1), channel_id=1, source_target_pairs={{0,2},{2,0},{4,6},{6,4},{8,10},{10,8},{12,14},{14,12},{16,18},{18,... | collective-permute-start | bytes 3686408 | tf_op jit(solution)/shard_map/ppermute | solution.py:363
  86.3 41.2 %collective-permute-start.17 = (bf16[640,960]{0,1:T(8,128)(2,1)}, bf16[640,960]{0,1:T(8,128)(2,1)}, u32[]{:S(2)}, u32[]{:S(2)}) collective-permute-start(bf16[640,960]{0,1:T(8,128)(2,1)} %copy.73), channel_id=1, source_target_pairs={{0,2},{2,0},{4,6},{6,4},{8,10},{10,8},{12,14},{14,12},{16,18},{18,... | collective-permute-start | bytes 3686408 | tf_op jit(solution)/shard_map/ppermute | solution.py:363
  100.2 28.9 %collective-permute-start.12 = (bf16[240,2560]{1,0:T(8,128)(2,1)}, bf16[240,2560]{1,0:T(8,128)(2,1)}, u32[]{:S(2)}, u32[]{:S(2)}) collective-permute-start(bf16[240,2560]{1,0:T(8,128)(2,1)} %maximum_select_fusion.11), channel_id=1, source_target_pairs={{0,2},{2,0},{4,6},{6,4},{8,10},{10,8},{12,14},{14,12},{16,18},{18,... | collective-permute-start | bytes 3686408 | tf_op jit(solution)/shard_map/ppermute | solution.py:363
  112.1 23.5 %collective-permute-start.7 = (bf16[240,2560]{1,0:T(8,128)(2,1)}, bf16[240,2560]{1,0:T(8,128)(2,1)}, u32[]{:S(2)}, u32[]{:S(2)}) collective-permute-start(bf16[240,2560]{1,0:T(8,128)(2,1)} %maximum_select_fusion.10), channel_id=1, source_target_pairs={{0,2},{2,0},{4,6},{6,4},{8,10},{10,8},{12,14},{14,12},{16,18},{18,... | collective-permute-start | bytes 3686408 | tf_op jit(solution)/shard_map/ppermute | solution.py:363
  215.8 91.4 %collective-permute-start.45 = (bf16[2,640,960]{1,2,0:T(8,128)(2,1)}, bf16[2,640,960]{1,2,0:T(8,128)(2,1)}, u32[]{:S(2)}, u32[]{:S(2)}) collective-permute-start(bf16[2,640,960]{1,2,0:T(8,128)(2,1)} %copy.83), channel_id=1, source_target_pairs={{0,2},{2,0},{4,6},{6,4},{8,10},{10,8},{12,14},{14,12},{16,18},{18,... | collective-permute-start | bytes 7372808 | tf_op jit(solution)/shard_map/ppermute | solution.py:363
  223.4 97.0 %collective-permute-start.36 = (bf16[2,240,2560]{2,1,0:T(8,128)(2,1)}, bf16[2,240,2560]{2,1,0:T(8,128)(2,1)}, u32[]{:S(2)}, u32[]{:S(2)}) collective-permute-start(bf16[2,240,2560]{2,1,0:T(8,128)(2,1)} %constant_dynamic-slice_fusion.8), channel_id=1, source_target_pairs={{0,2},{2,0},{4,6},{6,4},{8,10},{10,8},{12,14},{14,12},{16,18},{18,... | collective-permute-start | bytes 7372808 | tf_op jit(solution)/shard_map/ppermute | solution.py:363
  230.3 95.7 %collective-permute-start.27 = (bf16[2,240,2560]{2,1,0:T(8,128)(2,1)}, bf16[2,240,2560]{2,1,0:T(8,128)(2,1)}, u32[]{:S(2)}, u32[]{:S(2)}) collective-permute-start(bf16[2,240,2560]{2,1,0:T(8,128)(2,1)} %constant_dynamic-slice_fusion.12), channel_id=1, source_target_pairs={{0,2},{2,0},{4,6},{6,4},{8,10},{10,8},{12,14},{14,12},{16,18},{18,... | collective-permute-start | bytes 7372808 | tf_op jit(solution)/shard_map/ppermute | solution.py:363
  265.4 66.4 %collective-permute-start.18 = (bf16[2,240,2560]{2,1,0:T(8,128)(2,1)}, bf16[2,240,2560]{2,1,0:T(8,128)(2,1)}, u32[]{:S(2)}, u32[]{:S(2)}) collective-permute-start(bf16[2,240,2560]{2,1,0:T(8,128)(2,1)} %constant_dynamic-slice_fusion.16), channel_id=1, source_target_pairs={{0,2},{2,0},{4,6},{6,4},{8,10},{10,8},{12,14},{14,12},{16,18},{18,... | collective-permute-start | bytes 7372808 | tf_op jit(solution)/shard_map/ppermute | solution.py:363
  318.9 27.2 %collective-permute-start.46 = (bf16[1,640,960]{1,2,0:T(8,128)(2,1)}, bf16[1,640,960]{1,2,0:T(8,128)(2,1)}, u32[]{:S(2)}, u32[]{:S(2)}) collective-permute-start(bf16[1,640,960]{1,2,0:T(8,128)(2,1)} %copy.85), channel_id=1, source_target_pairs={{0,1},{1,0},{2,3},{3,2},{4,5},{5,4},{6,7},{7,6},{8,9},{9,8},{10,11... | collective-permute-start | bytes 3686408 | tf_op jit(solution)/shard_map/ppermute | solution.py:363
  326.0 46.5 %collective-permute-start.37 = (bf16[1,240,2560]{2,1,0:T(8,128)(2,1)}, bf16[1,240,2560]{2,1,0:T(8,128)(2,1)}, u32[]{:S(2)}, u32[]{:S(2)}) collective-permute-start(bf16[1,240,2560]{2,1,0:T(8,128)(2,1)} %constant_dynamic-slice_fusion.7), channel_id=1, source_target_pairs={{0,1},{1,0},{2,3},{3,2},{4,5},{5,4},{6,7},{7,6},{8,9},{9,8},{10,11... | collective-permute-start | bytes 3686408 | tf_op jit(solution)/shard_map/ppermute | solution.py:363
  330.9 67.9 %collective-permute-start.28 = (bf16[1,240,2560]{2,1,0:T(8,128)(2,1)}, bf16[1,240,2560]{2,1,0:T(8,128)(2,1)}, u32[]{:S(2)}, u32[]{:S(2)}) collective-permute-start(bf16[1,240,2560]{2,1,0:T(8,128)(2,1)} %constant_dynamic-slice_fusion.11), channel_id=1, source_target_pairs={{0,1},{1,0},{2,3},{3,2},{4,5},{5,4},{6,7},{7,6},{8,9},{9,8},{10,11... | collective-permute-start | bytes 3686408 | tf_op jit(solution)/shard_map/ppermute | solution.py:363
  336.6 88.5 %collective-permute-start.19 = (bf16[1,240,2560]{2,1,0:T(8,128)(2,1)}, bf16[1,240,2560]{2,1,0:T(8,128)(2,1)}, u32[]{:S(2)}, u32[]{:S(2)}) collective-permute-start(bf16[1,240,2560]{2,1,0:T(8,128)(2,1)} %constant_dynamic-slice_fusion.15), channel_id=1, source_target_pairs={{0,1},{1,0},{2,3},{3,2},{4,5},{5,4},{6,7},{7,6},{8,9},{9,8},{10,11... | collective-permute-start | bytes 3686408 | tf_op jit(solution)/shard_map/ppermute | solution.py:363
  350.6 77.5 %collective-permute-start.47 = (bf16[320,960]{1,0:T(8,128)(2,1)S(1)}, bf16[320,960]{1,0:T(8,128)(2,1)S(1)}, u32[]{:S(2)}, u32[]{:S(2)}) collective-permute-start(bf16[320,960]{1,0:T(8,128)(2,1)S(1)} %dynamic-slice_bitcast_fusion), channel_id=1, source_target_pairs={{0,4},{2,6},{4,0},{6,2},{8,12},{10,14},{12,8},{14,10},{16,20},{18,... | collective-permute-start | bytes 1843208 | tf_op jit(solution)/shard_map/ppermute | solution.py:363
  374.2 56.4 %collective-permute-start.38 = (bf16[120,2560]{1,0:T(8,128)(2,1)S(1)}, bf16[120,2560]{1,0:T(8,128)(2,1)S(1)}, u32[]{:S(2)}, u32[]{:S(2)}) collective-permute-start(bf16[120,2560]{1,0:T(8,128)(2,1)S(1)} %dynamic-slice_bitcast_fusion.1), channel_id=1, source_target_pairs={{0,4},{2,6},{4,0},{6,2},{8,12},{10,14},{12,8},{14,10},{16,20},{18,... | collective-permute-start | bytes 1843208 | tf_op jit(solution)/shard_map/ppermute | solution.py:363
  400.5 30.4 %collective-permute-start.29 = (bf16[120,2560]{1,0:T(8,128)(2,1)S(1)}, bf16[120,2560]{1,0:T(8,128)(2,1)S(1)}, u32[]{:S(2)}, u32[]{:S(2)}) collective-permute-start(bf16[120,2560]{1,0:T(8,128)(2,1)S(1)} %dynamic-slice_bitcast_fusion.2), channel_id=1, source_target_pairs={{0,4},{2,6},{4,0},{6,2},{8,12},{10,14},{12,8},{14,10},{16,20},{18,... | collective-permute-start | bytes 1843208 | tf_op jit(solution)/shard_map/ppermute | solution.py:363
  431.1 22.9 %collective-permute-start.30 = (bf16[120,1280]{1,0:T(8,128)(2,1)S(1)}, bf16[120,1280]{1,0:T(8,128)(2,1)S(1)}, u32[]{:S(2)}, u32[]{:S(2)}) collective-permute-start(bf16[120,1280]{1,0:T(8,128)(2,1)S(1)} %constant_dynamic-slice_fusion.10), channel_id=1, source_target_pairs={{0,8},{2,10},{4,12},{6,14},{8,0},{10,2},{12,4},{14,6},{16,24},{18,... | collective-permute-start | bytes 921608 | tf_op jit(solution)/shard_map/ppermute | solution.py:363
  439.8 23.5 %collective-permute-start.21 = (bf16[120,1280]{1,0:T(8,128)(2,1)S(1)}, bf16[120,1280]{1,0:T(8,128)(2,1)S(1)}, u32[]{:S(2)}, u32[]{:S(2)}) collective-permute-start(bf16[120,1280]{1,0:T(8,128)(2,1)S(1)} %constant_dynamic-slice_fusion.14), channel_id=1, source_target_pairs={{0,8},{2,10},{4,12},{6,14},{8,0},{10,2},{12,4},{14,6},{16,24},{18,... | collective-permute-start | bytes 921608 | tf_op jit(solution)/shard_map/ppermute | solution.py:363
  442.2 21.3 %collective-permute-start.49 = (bf16[80,960]{1,0:T(8,128)(2,1)S(1)}, bf16[80,960]{1,0:T(8,128)(2,1)S(1)}, u32[]{:S(2)}, u32[]{:S(2)}) collective-permute-start(bf16[80,960]{1,0:T(8,128)(2,1)S(1)} %constant_dynamic-slice_fusion.1), channel_id=1, source_target_pairs={{0,16},{2,18},{4,20},{6,22},{8,24},{10,26},{12,28},{14,30},{16,0},... | collective-permute-start | bytes 460808 | tf_op jit(solution)/shard_map/ppermute | solution.py:363
  443.2 22.7 %collective-permute-start.40 = (bf16[120,640]{1,0:T(8,128)(2,1)S(1)}, bf16[120,640]{1,0:T(8,128)(2,1)S(1)}, u32[]{:S(2)}, u32[]{:S(2)}) collective-permute-start(bf16[120,640]{1,0:T(8,128)(2,1)S(1)} %constant_dynamic-slice_fusion.5), channel_id=1, source_target_pairs={{0,16},{2,18},{4,20},{6,22},{8,24},{10,26},{12,28},{14,30},{16,0},... | collective-permute-start | bytes 460808 | tf_op jit(solution)/shard_map/ppermute | solution.py:363
  454.0 28.6 %collective-permute-start.31 = (bf16[120,640]{1,0:T(8,128)(2,1)S(1)}, bf16[120,640]{1,0:T(8,128)(2,1)S(1)}, u32[]{:S(2)}, u32[]{:S(2)}) collective-permute-start(bf16[120,640]{1,0:T(8,128)(2,1)S(1)} %constant_dynamic-slice_fusion.9), channel_id=1, source_target_pairs={{0,16},{2,18},{4,20},{6,22},{8,24},{10,26},{12,28},{14,30},{16,0},... | collective-permute-start | bytes 460808 | tf_op jit(solution)/shard_map/ppermute | solution.py:363
  463.4 19.1 %collective-permute-start.22 = (bf16[120,640]{1,0:T(8,128)(2,1)S(1)}, bf16[120,640]{1,0:T(8,128)(2,1)S(1)}, u32[]{:S(2)}, u32[]{:S(2)}) collective-permute-start(bf16[120,640]{1,0:T(8,128)(2,1)S(1)} %constant_dynamic-slice_fusion.13), channel_id=1, source_target_pairs={{0,16},{2,18},{4,20},{6,22},{8,24},{10,26},{12,28},{14,30},{16,0},... | collective-permute-start | bytes 460808 | tf_op jit(solution)/shard_map/ppermute | solution.py:363
  463.6 37.5 %collective-permute-start.50 = (bf16[80,960]{1,0:T(8,128)(2,1)S(1)}, bf16[80,960]{1,0:T(8,128)(2,1)S(1)}, u32[]{:S(2)}, u32[]{:S(2)}) collective-permute-start(bf16[80,960]{1,0:T(8,128)(2,1)S(1)} %add_convert_fusion.12), channel_id=1, source_target_pairs={{0,16},{2,18},{4,20},{6,22},{8,24},{10,26},{12,28},{14,30},{16,0},... | collective-permute-start | bytes 460808 | tf_op jit(solution)/shard_map/ppermute | solution.py:363
  466.0 36.6 %collective-permute-start.41 = (bf16[120,640]{1,0:T(8,128)(2,1)S(1)}, bf16[120,640]{1,0:T(8,128)(2,1)S(1)}, u32[]{:S(2)}, u32[]{:S(2)}) collective-permute-start(bf16[120,640]{1,0:T(8,128)(2,1)S(1)} %add_convert_fusion.13), channel_id=1, source_target_pairs={{0,16},{2,18},{4,20},{6,22},{8,24},{10,26},{12,28},{14,30},{16,0},... | collective-permute-start | bytes 460808 | tf_op jit(solution)/shard_map/ppermute | solution.py:363
  482.6 18.3 %collective-permute-start.23 = (bf16[120,640]{1,0:T(8,128)(2,1)S(1)}, bf16[120,640]{1,0:T(8,128)(2,1)S(1)}, u32[]{:S(2)}, u32[]{:S(2)}) collective-permute-start(bf16[120,640]{1,0:T(8,128)(2,1)S(1)} %add_convert_fusion.15), channel_id=1, source_target_pairs={{0,16},{2,18},{4,20},{6,22},{8,24},{10,26},{12,28},{14,30},{16,0},... | collective-permute-start | bytes 460808 | tf_op jit(solution)/shard_map/ppermute | solution.py:363
  482.7 28.1 %collective-permute-start.32 = (bf16[120,640]{1,0:T(8,128)(2,1)S(1)}, bf16[120,640]{1,0:T(8,128)(2,1)S(1)}, u32[]{:S(2)}, u32[]{:S(2)}) collective-permute-start(bf16[120,640]{1,0:T(8,128)(2,1)S(1)} %add_convert_fusion.14), channel_id=1, source_target_pairs={{0,16},{2,18},{4,20},{6,22},{8,24},{10,26},{12,28},{14,30},{16,0},... | collective-permute-start | bytes 460808 | tf_op jit(solution)/shard_map/ppermute | solution.py:363
  501.1 16.1 %collective-permute-start.51 = (bf16[160,960]{1,0:T(8,128)(2,1)S(1)}, bf16[160,960]{1,0:T(8,128)(2,1)S(1)}, u32[]{:S(2)}, u32[]{:S(2)}) collective-permute-start(bf16[160,960]{1,0:T(8,128)(2,1)S(1)} %maximum_select_fusion.23), channel_id=1, source_target_pairs={{0,8},{2,10},{4,12},{6,14},{8,0},{10,2},{12,4},{14,6},{16,24},{18,... | collective-permute-start | bytes 921608 | tf_op jit(solution)/shard_map/ppermute | solution.py:363
  502.7 21.1 %collective-permute-start.42 = (bf16[120,1280]{1,0:T(8,128)(2,1)S(1)}, bf16[120,1280]{1,0:T(8,128)(2,1)S(1)}, u32[]{:S(2)}, u32[]{:S(2)}) collective-permute-start(bf16[120,1280]{1,0:T(8,128)(2,1)S(1)} %maximum_select_fusion.28), channel_id=1, source_target_pairs={{0,8},{2,10},{4,12},{6,14},{8,0},{10,2},{12,4},{14,6},{16,24},{18,... | collective-permute-start | bytes 921608 | tf_op jit(solution)/shard_map/ppermute | solution.py:363
  510.9 21.2 %collective-permute-start.33 = (bf16[120,1280]{1,0:T(8,128)(2,1)S(1)}, bf16[120,1280]{1,0:T(8,128)(2,1)S(1)}, u32[]{:S(2)}, u32[]{:S(2)}) collective-permute-start(bf16[120,1280]{1,0:T(8,128)(2,1)S(1)} %maximum_select_fusion.27), channel_id=1, source_target_pairs={{0,8},{2,10},{4,12},{6,14},{8,0},{10,2},{12,4},{14,6},{16,24},{18,... | collective-permute-start | bytes 921608 | tf_op jit(solution)/shard_map/ppermute | solution.py:363
  517.5 17.7 %collective-permute-start.52 = (bf16[320,960]{1,0:T(8,128)(2,1)S(1)}, bf16[320,960]{1,0:T(8,128)(2,1)S(1)}, u32[]{:S(2)}, u32[]{:S(2)}) collective-permute-start(bf16[320,960]{1,0:T(8,128)(2,1)S(1)} %maximum_select_fusion.16), channel_id=1, source_target_pairs={{0,4},{2,6},{4,0},{6,2},{8,12},{10,14},{12,8},{14,10},{16,20},{18,... | collective-permute-start | bytes 1843208 | tf_op jit(solution)/shard_map/ppermute | solution.py:363
  524.0 24.5 %collective-permute-start.43 = (bf16[120,2560]{1,0:T(8,128)(2,1)S(1)}, bf16[120,2560]{1,0:T(8,128)(2,1)}, u32[]{:S(2)}, u32[]{:S(2)}) collective-permute-start(bf16[120,2560]{1,0:T(8,128)(2,1)S(1)} %maximum_select_fusion.21), channel_id=1, source_target_pairs={{0,4},{2,6},{4,0},{6,2},{8,12},{10,14},{12,8},{14,10},{16,20},{18,... | collective-permute-start | bytes 1843208 | tf_op jit(solution)/shard_map/ppermute | solution.py:363
  524.7 45.5 %collective-permute-start.26 = (bf16[240,2560]{1,0:T(8,128)(2,1)S(1)}, bf16[240,2560]{1,0:T(8,128)(2,1)}, u32[]{:S(2)}, u32[]{:S(2)}) collective-permute-start(bf16[240,2560]{1,0:T(8,128)(2,1)S(1)} %maximum_select_fusion.12), channel_id=1, source_target_pairs={{0,2},{2,0},{4,6},{6,4},{8,10},{10,8},{12,14},{14,12},{16,18},{18,... | collective-permute-start | bytes 3686408 | tf_op jit(solution)/shard_map/ppermute | solution.py:363
  533.2 28.6 %collective-permute-start.34 = (bf16[120,2560]{1,0:T(8,128)(2,1)}, bf16[120,2560]{1,0:T(8,128)(2,1)}, u32[]{:S(2)}, u32[]{:S(2)}) collective-permute-start(bf16[120,2560]{1,0:T(8,128)(2,1)} %maximum_select_fusion.20), channel_id=1, source_target_pairs={{0,4},{2,6},{4,0},{6,2},{8,12},{10,14},{12,8},{14,10},{16,20},{18,... | collective-permute-start | bytes 1843208 | tf_op jit(solution)/shard_map/ppermute | solution.py:363
  537.2 37.6 %collective-permute-start.53 = (bf16[640,960]{0,1:T(8,128)(2,1)}, bf16[640,960]{0,1:T(8,128)(2,1)}, u32[]{:S(2)}, u32[]{:S(2)}) collective-permute-start(bf16[640,960]{0,1:T(8,128)(2,1)} %copy.87), channel_id=1, source_target_pairs={{0,2},{2,0},{4,6},{6,4},{8,10},{10,8},{12,14},{14,12},{16,18},{18,... | collective-permute-start | bytes 3686408 | tf_op jit(solution)/shard_map/ppermute | solution.py:363
  551.1 42.8 %collective-permute-start.44 = (bf16[240,2560]{1,0:T(8,128)(2,1)}, bf16[240,2560]{1,0:T(8,128)(2,1)}, u32[]{:S(2)}, u32[]{:S(2)}) collective-permute-start(bf16[240,2560]{1,0:T(8,128)(2,1)} %maximum_select_fusion.14), channel_id=1, source_target_pairs={{0,2},{2,0},{4,6},{6,4},{8,10},{10,8},{12,14},{14,12},{16,18},{18,... | collective-permute-start | bytes 3686408 | tf_op jit(solution)/shard_map/ppermute | solution.py:363
  564.7 34.7 %collective-permute-start.35 = (bf16[240,2560]{1,0:T(8,128)(2,1)}, bf16[240,2560]{1,0:T(8,128)(2,1)}, u32[]{:S(2)}, u32[]{:S(2)}) collective-permute-start(bf16[240,2560]{1,0:T(8,128)(2,1)} %maximum_select_fusion.13), channel_id=1, source_target_pairs={{0,2},{2,0},{4,6},{6,4},{8,10},{10,8},{12,14},{14,12},{16,18},{18,... | collective-permute-start | bytes 3686408 | tf_op jit(solution)/shard_map/ppermute | solution.py:363
  (43 other events, 378.7 us)

commit v2 on v1

--- a/solution.py
+++ b/solution.py
@@ -18,6 +18,7 @@
 SCALE = HEAD_SIZE ** (-0.5)
 CHUNK = 512
 VMEM_LIMIT = 60 * 2**20
+FLOPS_PER_US = 10**9
 
 epsilon = 1e-05
 negative = -1e30
@@ -193,30 +194,38 @@
 
 
 def last_attention_kernel(
-    length_ref, hidden_in, small, cosines, sines, weight, normed_ref, qk_ref, v_ref, log_ref, gating_ref, d_gating_ref,
-    d_attn_ref, d_input_ref, d_qk_ref, d_v_ref, grad_hidden_ref, small_out, d_att_ref, d_raw_ref,
+    length_ref, hidden_in, small, cosines, sines, weight, normed_ref, qk_ref, v_ref, att_ref, log_ref, gating_ref,
+    d_gating_ref, d_attn_ref, d_input_ref, normed_rest, att_rest, d_qk_rest, d_v_rest, small_middle,
+    d_qk_ref, d_v_ref, normed_t_ref, att_t_ref, grad_hidden_ref, small_out, d_att_ref, d_raw_ref,
 ):
+    count = hidden_in.shape[0]
+    one = pl.ds(0, count)
+    rest = pl.ds(count, d_qk_ref.shape[0] - count)
     rows = hidden_in[...].astype(wide_type)
-    bias = causal_bias(rows.shape[0], length_ref[0])
+    bias = causal_bias(count, length_ref[0])
     d_rows, gain_gradient, router_gradient = attention_backward(
         rows, small[0:1], small[2:3], cosines[...], sines[...], bias, weight, normed_ref, qk_ref, v_ref, log_ref,
-        d_attn_ref[...], d_gating_ref[:, 0:1], gating_ref[:, 0:1], d_att_ref, d_raw_ref, d_qk_ref, d_v_ref,
+        d_attn_ref[one], d_gating_ref[:, 0:1], gating_ref[:, 0:1], d_att_ref, d_raw_ref, d_qk_ref.at[one], d_v_ref.at[one],
     )
     grad_hidden_ref[...] = d_input_ref[...] + d_rows
-    small_out[...] = jnp.zeros_like(small_out)
-    small_out[0:1] = gain_gradient
+    small_out[...] = small_middle[...]
+    small_out[0:1] += gain_gradient
     small_out[2:3] = router_gradient
+    d_qk_ref[rest] = d_qk_rest[...]
+    d_v_ref[rest] = d_v_rest[...]
+    normed_t_ref[...] = jnp.concatenate([normed_ref[...], normed_rest[...]], axis=0).T
+    att_t_ref[...] = jnp.concatenate([att_ref[...], att_rest[...]], axis=0).T
 
 
 def middle_kernel(
     length_ref, hidden_in, cotangent, small, attn_out_ref, gating_ref, cos_two, sin_two, cos_three, sin_three,
     column_two, row_two, column_three, row_three, w_attn_hbm, w_gate_hbm, w_up_hbm, w_down_hbm,
-    hidden_out, d_input_ref, d_gating_ref, small_out,
-    hidden_one, d_ffn_one, ffn_one, d_gate_one, d_up_one, d_attn_one,
-    hidden_in_r, d_ffn_in_r, ffn_in_r, d_gate_in_r, d_up_in_r, d_attn_in_r, att_in_r, normed_in_r, d_qk_in_r, d_v_in_r,
+    hidden_out, d_input_ref, d_gating_ref, small_out, hidden_all, d_ffn_t_ref, ffn_t_ref, d_gate_all, d_up_all, d_attn_all,
+    att_rest, normed_rest, d_qk_rest, d_v_rest,
     w_attn, w_gate, w_up, w_down, sems,
     gate_one, up_one, gate_two, up_two, gate_three, up_three, total_one, total_two, total_three,
     qk_two, v_two, log_two, qk_three, v_three, log_three, d_att_two, d_raw_two, d_att_three, d_raw_three,
+    ffn_all, d_ffn_all,
 ):
     copies = [
         pltpu.make_async_copy(source, target, sems.at[i])
@@ -228,6 +237,8 @@
         copy.start()
     count_two, count_three = column_two.shape[0], column_three.shape[0]
     count_one = hidden_in.shape[0]
+    in_one, in_two = pl.ds(0, count_one), pl.ds(count_one, count_two)
+    in_three = pl.ds(count_one + count_two, count_three)
     two = pl.ds(0, count_two)
     three = pl.ds(count_two, count_three)
     gain_attn, gain_ffn = small[0:1], small[1:2]
@@ -245,7 +256,7 @@
     after_one = hidden_in[...].astype(wide_type) + attn_out_ref[...]
     for copy in copies[:3]:
         copy.wait()
-    ffn_forward(after_one, gain_ffn, w_gate, w_up, w_down, ffn_one, gate_one, up_one, hidden_one, total_one, CHUNK)
+    ffn_forward(after_one, gain_ffn, w_gate, w_up, w_down, ffn_all.at[in_one], gate_one, up_one, hidden_all.at[in_one], total_one, CHUNK)
     valid = lax.broadcasted_iota(jnp.int32, (count_one, 1), 0) < length_ref[0]
     scale_one = jnp.where(valid, gating_ref[:, 0:1], 0.0)
     change_one = attn_out_ref[...] + total_one[...]
@@ -257,11 +268,11 @@
     bias_two = causal_bias(count_two, None)
     attn_two, gating_two = attention_forward(
         state_two, gain_attn, small[3:4], cos_two[...], sin_two[...], bias_two, w_attn,
-        normed_in_r.at[two], qk_two, v_two, att_in_r.at[two], log_two,
+        normed_rest.at[two], qk_two, v_two, att_rest.at[two], log_two,
     )
     after_two = state_two + attn_two
     ffn_forward(
-        after_two, gain_ffn, w_gate, w_up, w_down, ffn_in_r.at[two], gate_two, up_two, hidden_in_r.at[two], total_two, CHUNK
+        after_two, gain_ffn, w_gate, w_up, w_down, ffn_all.at[in_two], gate_two, up_two, hidden_all.at[in_two], total_two, CHUNK
     )
     change_two = attn_two + total_two[...]
     delta_two = gating_two * change_two
@@ -270,12 +281,12 @@
     bias_three = causal_bias(count_three, None)
     attn_three, gating_three = attention_forward(
         state_three, gain_attn, small[4:5], cos_three[...], sin_three[...], bias_three, w_attn,
-        normed_in_r.at[three], qk_three, v_three, att_in_r.at[three], log_three,
+        normed_rest.at[three], qk_three, v_three, att_rest.at[three], log_three,
     )
     after_three = state_three + attn_three
     ffn_forward(
-        after_three, gain_ffn, w_gate, w_up, w_down, ffn_in_r.at[three], gate_three, up_three,
-        hidden_in_r.at[three], total_three, CHUNK,
+        after_three, gain_ffn, w_gate, w_up, w_down, ffn_all.at[in_three], gate_three, up_three,
+        hidden_all.at[in_three], total_three, CHUNK,
     )
     change_three = attn_three + total_three[...]
     added = delta_two + pick_exact(put_three, gating_three * change_three)
@@ -285,32 +296,32 @@
     incoming_three = rows_dot(pick_three, incoming_two.astype(narrow_dtype))
     d_change = gating_three * incoming_three
     d_gating = jnp.sum(change_three * incoming_three, axis=-1, keepdims=True)
-    d_ffn_in_r[three] = d_change.astype(narrow_dtype)
+    d_ffn_all[in_three] = d_change.astype(narrow_dtype)
     d_after, gain_ffn_three = ffn_backward(
-        after_three, gain_ffn, w_gate, w_up, w_down, d_ffn_in_r.at[three], gate_three, up_three,
-        d_gate_in_r.at[three], d_up_in_r.at[three], total_three, CHUNK,
-    )
-    d_attn_in_r[three] = (d_change + d_after).astype(narrow_dtype)
+        after_three, gain_ffn, w_gate, w_up, w_down, d_ffn_all.at[in_three], gate_three, up_three,
+        d_gate_all.at[in_three], d_up_all.at[in_three], total_three, CHUNK,
+    )
+    d_attn_all[in_three] = (d_change + d_after).astype(narrow_dtype)
     d_rows, gain_attn_three, router_three = attention_backward(
-        state_three, gain_attn, small[4:5], cos_three[...], sin_three[...], bias_three, w_attn, normed_in_r.at[three],
-        qk_three, v_three, log_three, d_attn_in_r[three], d_gating, gating_three, d_att_three, d_raw_three,
-        d_qk_in_r.at[three], d_v_in_r.at[three],
+        state_three, gain_attn, small[4:5], cos_three[...], sin_three[...], bias_three, w_attn, normed_rest.at[three],
+        qk_three, v_three, log_three, d_attn_all[in_three], d_gating, gating_three, d_att_three, d_raw_three,
+        d_qk_rest.at[three], d_v_rest.at[three],
     )
     back_three = pick_exact(put_three, d_rows + d_after)
 
     incoming_two = incoming_two + back_three
     d_change = gating_two * incoming_two
     d_gating = jnp.sum(change_two * incoming_two, axis=-1, keepdims=True)
-    d_ffn_in_r[two] = d_change.astype(narrow_dtype)
+    d_ffn_all[in_two] = d_change.astype(narrow_dtype)
     d_after, gain_ffn_two = ffn_backward(
-        after_two, gain_ffn, w_gate, w_up, w_down, d_ffn_in_r.at[two], gate_two, up_two,
-        d_gate_in_r.at[two], d_up_in_r.at[two], total_two, CHUNK,
-    )
-    d_attn_in_r[two] = (d_change + d_after).astype(narrow_dtype)
+        after_two, gain_ffn, w_gate, w_up, w_down, d_ffn_all.at[in_two], gate_two, up_two,
+        d_gate_all.at[in_two], d_up_all.at[in_two], total_two, CHUNK,
+    )
+    d_attn_all[in_two] = (d_change + d_after).astype(narrow_dtype)
     d_rows, gain_attn_two, router_two = attention_backward(
-        state_two, gain_attn, small[3:4], cos_two[...], sin_two[...], bias_two, w_attn, normed_in_r.at[two],
-        qk_two, v_two, log_two, d_attn_in_r[two], d_gating, gating_two, d_att_two, d_raw_two,
-        d_qk_in_r.at[two], d_v_in_r.at[two],
+        state_two, gain_attn, small[3:4], cos_two[...], sin_two[...], bias_two, w_attn, normed_rest.at[two],
+        qk_two, v_two, log_two, d_attn_all[in_two], d_gating, gating_two, d_att_two, d_raw_two,
+        d_qk_rest.at[two], d_v_rest.at[two],
     )
     back_two = back_three + d_rows + d_after
 
@@ -319,18 +330,21 @@
     d_change = scale_one * incoming
     d_gating = jnp.where(valid, jnp.sum(total_one[...] * incoming, axis=-1, keepdims=True), 0.0)
     d_gating_ref[...] = jnp.broadcast_to(d_gating, d_gating_ref.shape)
-    d_ffn_one[...] = d_change.astype(narrow_dtype)
+    d_ffn_all[in_one] = d_change.astype(narrow_dtype)
     after_one = hidden_in[...].astype(wide_type) + attn_out_ref[...]
     d_after, gain_ffn_one = ffn_backward(
-        after_one, gain_ffn, w_gate, w_up, w_down, d_ffn_one, gate_one, up_one, d_gate_one, d_up_one, total_one, CHUNK
-    )
-    d_attn_one[...] = (scale_one * d_input_ref[...] + d_after).astype(narrow_dtype)
+        after_one, gain_ffn, w_gate, w_up, w_down, d_ffn_all.at[in_one], gate_one, up_one,
+        d_gate_all.at[in_one], d_up_all.at[in_one], total_one, CHUNK,
+    )
+    d_attn_all[in_one] = (scale_one * d_input_ref[...] + d_after).astype(narrow_dtype)
     d_input_ref[...] += d_after
     small_out[...] = jnp.zeros_like(small_out)
     small_out[0:1] = gain_attn_two + gain_attn_three
     small_out[1:2] = gain_ffn_one + gain_ffn_two + gain_ffn_three
     small_out[3:4] = router_two
     small_out[4:5] = router_three
+    d_ffn_t_ref[...] = d_ffn_all[...].T
+    ffn_t_ref[...] = ffn_all[...].T
 
 
 def rotary_tables(positions):
@@ -342,7 +356,7 @@
     return jnp.cos(angles), jnp.sin(angles) * sign[None, :]
 
 
-def call(kernel, operands, outputs, scratch=(), hbm=(), scalars=1, flops=0):
+def call(kernel, operands, outputs, flops, scratch=(), hbm=(), scalars=1):
     specs = [
         pl.BlockSpec(memory_space=pltpu.SMEM if i < scalars else (pl.ANY if i in hbm else pltpu.VMEM))
         for i in range(len(operands))
@@ -367,28 +381,8 @@
     return (lax.axis_index(axis) // bit) % 2
 
 
-def take_half(value, axis, bit, dim):
-    size = value.shape[dim] // 2
-    which = side(axis, bit)
-    keep = lax.dynamic_slice_in_dim(value, which * size, size, dim)
-    send = lax.dynamic_slice_in_dim(value, (1 - which) * size, size, dim)
-    return keep, send
-
-
-def add_half(value, axis, bit, dim):
-    keep, send = take_half(value, axis, bit, dim)
-    received = partner(send, axis, bit)
-    return (keep.astype(wide_type) + received.astype(wide_type)).astype(narrow_dtype)
-
-
-def join_half(value, axis, bit, dim):
-    received = partner(value, axis, bit)
-    first = side(axis, bit) == 0
-    return jnp.where(
-        first,
-        jnp.concatenate([value, received], axis=dim),
-        jnp.concatenate([received, value], axis=dim),
-    )
+def after(value, *others):
+    return lax.optimization_barrier((value,) + others)[0]
 
 
 def bits_of(axis, low):
@@ -400,25 +394,153 @@
     return found
 
 
+def piece_of(value, index, size, dim):
+    return lax.dynamic_slice_in_dim(value, index * size, size, dim)
+
+
+def take_half(value, axis, bit, dim):
+    size = value.shape[dim] // 2
+    which = side(axis, bit)
+    return piece_of(value, which, size, dim), piece_of(value, 1 - which, size, dim)
+
+
+def add(*values):
+    total = values[0].astype(wide_type)
+    for value in values[1:]:
+        total = total + value.astype(wide_type)
+    return total.astype(narrow_dtype)
+
+
+def in_order(parts, index):
+    bit = 1
+    while bit < len(parts):
+        swap = (index // bit) % 2 == 1
+        parts = [jnp.where(swap, parts[i ^ bit], parts[i]) for i in range(len(parts))]
+        bit = bit * 2
+    return parts
+
+
+def join(parts, index, dim):
+    return jnp.concatenate(in_order(parts, index), axis=dim)
+
+
+def join_half(value, axis, bit, dim):
+    return join([value, partner(value, axis, bit)], side(axis, bit), dim)
+
+
+CORE, ROW, LAYER = 1, 2, 4
+
+
+class Part:
+    def __init__(self, y_dim, z_dim, fsdp_dim, core_dim):
+        self.y_dim, self.z_dim, self.fsdp_dim, self.core_dim = y_dim, z_dim, fsdp_dim, core_dim
+
+    def layers(self):
+        return lax.axis_size("dp") // LAYER
+
+    def layer(self):
+        return lax.axis_index("dp") // LAYER
+
+    def split_x(self, value):
+        owners = lax.axis_size("fsdp")
+        size = value.shape[self.fsdp_dim] // owners
+        mine = lax.axis_index("fsdp")
+        return [piece_of(value, mine ^ offset, size, self.fsdp_dim) for offset in range(owners)]
+
+    def send_x(self, parts):
+        return [parts[0]] + [partner(part, "fsdp", offset) for offset, part in enumerate(parts) if offset]
+
+    def send_y(self, value):
+        keep, send = take_half(value, "dp", ROW, self.y_dim)
+        return [keep, partner(send, "dp", ROW)]
+
+    def split_z(self, value):
+        size = value.shape[self.z_dim] // self.layers()
+        return [piece_of(value, self.layer() ^ offset, size, self.z_dim) for offset in range(self.layers())]
+
+    def send_z(self, parts):
+        return [parts[0]] + [partner(part, "dp", offset * LAYER) for offset, part in enumerate(parts) if offset]
+
+    def back_z(self, piece):
+        return [piece] + [partner(piece, "dp", offset * LAYER) for offset in range(1, self.layers())]
+
+    def back_y(self, value):
+        return [value, partner(value, "dp", ROW)]
+
+    def back_core(self, value):
+        return [value, partner(value, "dp", CORE)]
+
+    def join_z(self, parts):
+        return join(parts, self.layer(), self.z_dim)
+
+    def join_y(self, parts):
+        return join(parts, side("dp", ROW), self.y_dim)
+
+    def join_core(self, parts):
+        return join(parts, side("dp", CORE), self.core_dim)
+
+
+class Order:
+    def __init__(self):
+        self.last = None
+
+    def hold(self, value):
+        return value if self.last is None else after(value, self.last)
+
+    def step(self, work, values):
+        result = work([self.hold(values[0])] + list(values[1:]))
+        self.last = result
+        return result
+
+
+def reduce_all(parts, makers, order, beside, between, finish):
+    core = side("dp", CORE)
+    count = len(parts)
+    done, halves, joined, pieces, cores = ([None] * count for _ in range(5))
+
+    def produce(k):
+        away = makers[k](1 - core, None)
+        order.last = away
+        value = makers[k](core, partner(away, "dp", CORE))
+        order.last = value
+        return parts[k].split_x(value)
+
+    def added(values):
+        return add(*values)
+
+    waiting = produce(0)
+    x_parts = parts[0].send_x(waiting)
+    beside()
+    waiting = produce(1)
+    for k in range(count + 3):
+        if k < count:
+            halves[k] = order.step(added, x_parts)
+            y_parts = parts[k].send_y(halves[k])
+        if k + 1 < count:
+            x_parts = parts[k + 1].send_x([order.hold(part) for part in waiting])
+        if 1 <= k <= count:
+            piece = order.step(added, z_parts)
+            pieces[k - 1] = parts[k - 1].back_z(piece)
+        if 2 <= k <= count + 1:
+            value = order.step(parts[k - 2].join_y, back)
+            cores[k - 2] = parts[k - 2].back_core(value)
+        if k >= 3:
+            done[k - 3] = order.step(lambda values: finish[k - 3](parts[k - 3].join_core(values)), cores[k - 3])
+        if k + 2 < count:
+            waiting = produce(k + 2)
+        between(k)
+        if k < count:
+            z_value = order.step(added, y_parts)
+            z_parts = parts[k].send_z(parts[k].split_z(z_value))
+        if 1 <= k <= count:
+            value = order.step(parts[k - 1].join_z, pieces[k - 1])
+            back = parts[k - 1].back_y(value)
+    return done
+
+
 def split_steps(row_steps):
     steps = [("dp", 1, 0), ("dp", 2, 0)]
     return steps + [("dp", bit, 0 if row_steps else 1) for bit in bits_of("dp", 4)]
-
-
-def reduce_matrix(gradient, row_steps):
-    owners = lax.axis_size("fsdp")
-    rows, columns = gradient.shape
-    value = gradient.reshape(owners, rows // owners, columns)
-    value = add_half(value, "dp", 1, 1)
-    for bit in reversed(bits_of("fsdp", 1)):
-        value = add_half(value, "fsdp", bit, 0)
-    value = value[0]
-    steps = split_steps(row_steps)
-    for axis, bit, dim in steps[1:]:
-        value = add_half(value, axis, bit, dim)
-    for axis, bit, dim in reversed(steps):
-        value = join_half(value, axis, bit, dim)
-    return value
 
 
 def place(parts, rows, shape):
@@ -512,9 +634,12 @@
             ((count_one, model), wide_type),
             ((count_one, 128), wide_type),
         ],
-    )
+        10 * FLOPS_PER_US,
+    )
+    count_all = count_one + count_rest
     rest = lambda width: ((count_rest, width), narrow_dtype)
-    first = lambda width: ((count_one, width), narrow_dtype)
+    every = lambda width: ((count_all, width), narrow_dtype)
+    turned = ((model, count_all), narrow_dtype)
     scratch_for = lambda count: [
         pltpu.VMEM((count, QK_WIDTH), narrow_dtype),
         pltpu.VMEM((count, v_width), narrow_dtype),
@@ -526,9 +651,8 @@
     ]
     wide = lambda count, width: pltpu.VMEM((count, width), wide_type)
     (
-        hidden_out, d_input, d_gating_one, small_middle,
-        hidden_one, d_ffn_one, ffn_one, d_gate_one, d_up_one, d_attn_one,
-        hidden_r, d_ffn_r, ffn_r, d_gate_r, d_up_r, d_attn_r, att_r, normed_r, d_qk_r, d_v_r,
+        hidden_out, d_input, d_gating_one, small_middle, hidden, d_ffn_t, ffn_t, d_gate, d_up, d_attn,
+        att_rest, normed_rest, d_qk_rest, d_v_rest,
     ) = call(
         middle_kernel,
         (
@@ -537,11 +661,11 @@
             attn_full, gate_full, up_full, down_full,
         ),
         [
-            first(model), ((count_one, model), wide_type), ((count_one, 128), wide_type), ((8, model), wide_type),
-            first(ff), first(model), first(model), first(ff), first(ff), first(model),
-            rest(ff), rest(model), rest(model), rest(ff), rest(ff), rest(model), rest(model), rest(model),
-            rest(QK_WIDTH), rest(v_width),
+            ((count_one, model), narrow_dtype), ((count_one, model), wide_type), ((count_one, 128), wide_type),
+            ((8, model), wide_type), every(ff), turned, turned, every(ff), every(ff), every(model),
+            rest(model), rest(model), rest(QK_WIDTH), rest(v_width),
         ],
+        57 * FLOPS_PER_US,
         [
             pltpu.VMEM(attn_full.shape, narrow_dtype),
             pltpu.VMEM(gate_full.shape, narrow_dtype),
@@ -552,40 +676,94 @@
             wide(count_three, ff), wide(count_three, ff),
             wide(count_one, model), wide(count_two, model), wide(count_three, model),
         ]
-        + scratch_for(count_two) + scratch_for(count_three) + back_scratch(count_two) + back_scratch(count_three),
+        + scratch_for(count_two) + scratch_for(count_three) + back_scratch(count_two) + back_scratch(count_three)
+        + [pltpu.VMEM((count_all, model), narrow_dtype)] * 2,
         hbm=(14, 15, 16, 17),
     )
-    d_qk_one, d_v_one, grad_hidden, small_last = call(
-        last_attention_kernel,
-        (
-            lengths, hidden_in, small_wide, cos_one, sin_one, attn_full, normed_one, qk_one, v_one, log_one, gating_one,
-            d_gating_one, d_attn_one, d_input,
-        ),
-        [
-            first(QK_WIDTH), first(v_width), ((count_one, model), wide_type), ((8, model), wide_type),
-        ],
-        back_scratch(count_one),
-    )
-
-    def outer(left, left_r, right, right_r):
-        left = jnp.concatenate([left, left_r])
-        right = jnp.concatenate([right, right_r])
-        return jnp.einsum("na,nb->ab", left, right, preferred_element_type=wide_type).astype(narrow_dtype)
-
-    down_shard = reduce_matrix(outer(hidden_one, hidden_r, d_ffn_one, d_ffn_r), True).astype(wide_type)
-    gate_shard = reduce_matrix(outer(ffn_one, ffn_r, d_gate_one, d_gate_r), False).astype(wide_type)
-    up_shard = reduce_matrix(outer(ffn_one, ffn_r, d_up_one, d_up_r), False).astype(wide_type)
+
+    order = Order()
+    attention = []
+
+    def last_attention():
+        attention.extend(
+            call(
+                last_attention_kernel,
+                (
+                    lengths, hidden_in, small_wide, cos_one, sin_one, attn_full, normed_one, qk_one, v_one, att_one,
+                    log_one, gating_one, d_gating_one, order.hold(d_attn), d_input, normed_rest, att_rest, d_qk_rest,
+                    d_v_rest, small_middle,
+                ),
+                [
+                    every(QK_WIDTH), every(v_width), turned, turned, ((count_one, model), wide_type),
+                    ((8, model), wide_type),
+                ],
+                1000,
+                back_scratch(count_one),
+            )
+        )
+        order.last = attention[0]
+
+    def dot(left, right):
+        return jnp.dot(left, right, preferred_element_type=wide_type)
+
+    def plus(product, received):
+        if received is not None:
+            product = product + received.astype(wide_type)
+        return product.astype(narrow_dtype)
+
+    def core_rows(left, which):
+        rows = left.reshape(owners, 2, model // owners // 2, left.shape[1])
+        rows = lax.dynamic_index_in_dim(rows, which, 1, keepdims=False)
+        return rows.reshape(model // 2, left.shape[1])
+
+    def make_down(which, received):
+        size = ff // owners // 2
+        columns = jnp.concatenate([piece_of(hidden, 2 * owner + which, size, 1) for owner in range(owners)], axis=1)
+        return plus(dot(order.hold(d_ffn_t), columns), received)
+
+    def make_from(right):
+        def make(which, received):
+            return plus(dot(core_rows(ffn_t, which), order.hold(right)), received)
+
+        return make
+
     skip = V_HEAD * HEAD_SIZE
-    attn_grad = jnp.concatenate(
-        [
-            outer(normed_one, normed_r, d_qk_one, d_qk_r),
-            outer(att_one, att_r, d_attn_one, d_attn_r),
-            outer(normed_one, normed_r, d_v_one[:, skip:], d_v_r[:, skip:]),
-        ],
-        axis=1,
-    )
-    attn_out_shard = reduce_matrix(attn_grad, False).astype(wide_type)
-    small_sum = lax.psum(small_middle + small_last, ("dp", "fsdp"))
+    split = 256
+
+    def make_first(which, received):
+        d_qk, _, normed_t, att_t, _, _ = attention
+        product = [dot(core_rows(normed_t, which), order.hold(d_qk)), dot(core_rows(att_t, which), d_attn[:, :split])]
+        return plus(jnp.concatenate(product, axis=1), received)
+
+    def make_second(which, received):
+        _, d_v, normed_t, att_t, _, _ = attention
+        left = order.hold(att_t)
+        product = [dot(core_rows(left, which), d_attn[:, split:]), dot(core_rows(normed_t, which), d_v[:, skip:])]
+        return plus(jnp.concatenate(product, axis=1), received)
+
+    by_rows = lambda: Part(y_dim=0, z_dim=1, fsdp_dim=0, core_dim=0)
+    small_state = []
+    small_steps = [(axis, bit) for axis in ("fsdp", "dp") for bit in bits_of(axis, 1)]
+
+    def add_small(k):
+        if not small_state:
+            small_state.extend([attention[5], None])
+        value, moved = small_state
+        if moved is not None:
+            value = order.step(lambda values: values[0] + values[1], [value, moved])
+        moved = partner(value, *small_steps[k]) if k < len(small_steps) else None
+        small_state[:] = [value, moved]
+
+    widen = lambda value: value.astype(wide_type)
+    down_shard, gate_shard, up_shard, first_shard, second_shard = reduce_all(
+        [Part(y_dim=0, z_dim=0, fsdp_dim=1, core_dim=1)] + [by_rows() for _ in range(4)],
+        [make_down, make_from(d_gate), make_from(d_up), make_first, make_second],
+        order,
+        last_attention,
+        add_small,
+        [lambda value: widen(value).T] + [widen] * 4,
+    )
+    grad_hidden, small_sum = attention[4], small_state[0]
     small_sum = lax.dynamic_slice_in_dim(small_sum, mine * small.shape[1], small.shape[1], 1)
     return (
         hidden_out,
@@ -593,10 +771,10 @@
         small_sum[0],
         small_sum[1],
         small_sum[2:5].T,
-        attn_out_shard[:, :width],
-        attn_out_shard[:, width : width + kv_width],
-        attn_out_shard[:, 2 * width + kv_width :],
-        attn_out_shard[:, width + kv_width : 2 * width + kv_width],
+        first_shard[:, :width],
+        first_shard[:, width : width + kv_width],
+        second_shard[:, width - split :],
+        jnp.concatenate([first_shard[:, width + kv_width :], second_shard[:, : width - split]], axis=1),
         gate_shard,
         up_shard,
         down_shard,

time: 614 us -> 493 us (0.80)
  waiting for transfers between devices: 191 us -> 147 us
  local copies, waits for them, and re-layouts: 106 us -> 64.3 us
  blocking collectives: 38.3 us -> 0 us
  other arithmetic: 77.1 us -> 54.2 us
  starting transfers between devices: 86.1 us -> 105 us
    ppermute x54 -> x78, waiting for transfers between devices: 191 us -> 147 us  [partner(): return lax.ppermute(value, axis, [(i, i ^ bit) for i in range(count)])]
    psum x1 -> x0, blocking collectives: 38.3 us -> none  [local(): small_sum = lax.psum(small_middle + small_last, ('dp', 'fsdp'))]
    convert_element_type x24 -> x21, other arithmetic: 39.4 us -> 14.5 us  [the longest x4 6.4 us: local(): widen = lambda value: value.astype(wide_type)]
    ppermute x54 -> x78, starting transfers between devices: 86.1 us -> 105 us  [partner(): return lax.ppermute(value, axis, [(i, i ^ bit) for i in range(count)])]
    dynamic_slice x26 -> x25, local copies, waits for them, and re-layouts: 22.3 us -> 10.7 us  [the longest x20 9.63 us: piece_of(): return lax.dynamic_slice_in_dim(value, index * size, size, dim)]
    dynamic_update_slice x6 -> x5, other arithmetic: 16.3 us -> 4.97 us  [place(): full = lax.dynamic_update_slice_in_dim(full, part, index * rows, 0)]
    convert_element_type x2 -> x0, local copies, waits for them, and re-layouts: 9.32 us -> none  [outer(): jnp.einsum('na,nb->ab', left, right, preferred_element_type=wide_type)]
    concatenate x0 -> x22, other arithmetic: none -> 6.7 us  [the longest x19 5.32 us: join(): return jnp.concatenate(in_order(parts, index), axis=dim)]
  transfers between devices with their start and end apart: 54 -> 78, of which waited for: 22 -> 31; matrix products, arithmetic and copies ran while one was open for 27% -> 21% of each run, Pallas kernels for 4% -> 0%
where the time goes in v2:
time: 493 us; the launch traced here: 484 us
  waiting for transfers between devices  147 us (30%)
  starting transfers between devices  105 us (21%)
  Pallas kernels  83.6 us (17%)
  local copies, waits for them, and re-layouts  64.3 us (13%)
  other arithmetic  54.2 us (11%)
  matrix products  26.9 us (5%)
    ppermute x78, waiting for transfers between devices, partner(): return lax.ppermute(value, axis, [(i, i ^ bit) for i in range(count)])  147 us
    ppermute x78, starting transfers between devices, partner(): return lax.ppermute(value, axis, [(i, i ^ bit) for i in range(count)])  105 us
    pallas_call x3, Pallas kernels, call(): pl.pallas_call(kernel, out_shape=[jax.ShapeDtypeStruct(shape, kind) for s...  83.6 us
    unnamed x117, local copies, waits for them, and re-layouts  27.2 us
    dot_general x14, matrix products, dot(): return jnp.dot(left, right, preferred_element_type=wide_type)  26.9 us
    select_n x28, other arithmetic, in_order(): jnp.where(swap, parts[i ^ bit], parts[i])  18.1 us
  transfers between devices with their start and end apart: 78, of which 31 were waited for; matrix products, arithmetic and copies ran while one was open for 21% of the time, Pallas kernels for 0%

profile of v2, /device:TPU:1, one launch (start us, length us, event | category | flops | bytes accessed | tf_op | source)
XLA Modules:
  0.0 484.3 jit_solution(12581620556631537105)
XLA Ops:
  0.8 3.6 copy.63
  20.2 3.5 concatenate.116
  42.6 10.5 %collective-permute-done = bf16[16,480]{1,0:T(8,128)(2,1)S(1)} collective-permute-done((bf16[16,480]{1,0:T(8,128)(2,1)S(1)}, bf16[16,480]{1,0:T(8,128)(2,1)S(1)}, u32[]{:S(2)}, u32[]{:S(2)}) %collective-permute-start) | collective-permute-done | bytes 15392 | tf_op jit(solution)/shard_map/ppermute | solution.py:377
  58.8 10.9 %collective-permute-done.14 = bf16[80,960]{1,0:T(8,128)(2,1)S(1)} collective-permute-done((bf16[80,960]{1,0:T(8,128)(2,1)}, bf16[80,960]{1,0:T(8,128)(2,1)S(1)}, u32[]{:S(2)}, u32[]{:S(2)}) %collective-permute-start.14) | collective-permute-done | bytes 153632 | tf_op jit(solution)/shard_map/ppermute | solution.py:377
  79.0 5.4 %collective-permute-done.15 = bf16[160,960]{1,0:T(8,128)(2,1)S(1)} collective-permute-done((bf16[160,960]{1,0:T(8,128)(2,1)S(1)}, bf16[160,960]{1,0:T(8,128)(2,1)S(1)}, u32[]{:S(2)}, u32[]{:S(2)}) %collective-permute-start.15) | collective-permute-done | bytes 307232 | tf_op jit(solution)/shard_map/ppermute | solution.py:377
  86.0 5.0 %collective-permute-done.10 = bf16[120,1280]{1,0:T(8,128)(2,1)S(1)} collective-permute-done((bf16[120,1280]{1,0:T(8,128)(2,1)S(1)}, bf16[120,1280]{1,0:T(8,128)(2,1)S(1)}, u32[]{:S(2)}, u32[]{:S(2)}) %collective-permute-start.10) | collective-permute-done | bytes 307232 | tf_op jit(solution)/shard_map/ppermute | solution.py:377
  92.5 5.1 %collective-permute-done.5 = bf16[120,1280]{1,0:T(8,128)(2,1)S(1)} collective-permute-done((bf16[120,1280]{1,0:T(8,128)(2,1)S(1)}, bf16[120,1280]{1,0:T(8,128)(2,1)S(1)}, u32[]{:S(2)}, u32[]{:S(2)}) %collective-permute-start.5) | collective-permute-done | bytes 307232 | tf_op jit(solution)/shard_map/ppermute | solution.py:377
  106.9 6.8 %collective-permute-done.11 = bf16[120,2560]{1,0:T(8,128)(2,1)} collective-permute-done((bf16[120,2560]{1,0:T(8,128)(2,1)S(1)}, bf16[120,2560]{1,0:T(8,128)(2,1)}, u32[]{:S(2)}, u32[]{:S(2)}) %collective-permute-start.11) | collective-permute-done | bytes 614432 | tf_op jit(solution)/shard_map/ppermute | solution.py:377
  118.7 8.2 %collective-permute-done.6 = bf16[120,2560]{1,0:T(8,128)(2,1)} collective-permute-done((bf16[120,2560]{1,0:T(8,128)(2,1)}, bf16[120,2560]{1,0:T(8,128)(2,1)}, u32[]{:S(2)}, u32[]{:S(2)}) %collective-permute-start.6) | collective-permute-done | bytes 614432 | tf_op jit(solution)/shard_map/ppermute | solution.py:377
  131.5 2.9 broadcast_select_fusion.13
  134.4 2.6 copy.65
  152.1 10.2 %shard_map.238 = (bf16[256,960]{1,0:T(8,128)(2,1)}, bf16[256,1280]{1,0:T(8,128)(2,1)}, bf16[256,384]{1,0:T(8,128)(2,1)}, bf16[256,960]{1,0:T(8,128)(2,1)}, f32[7...) custom-call(s32[1]{0:T(128)S(6)} %copy.89.length_ref, bf16[256,960]{1,0:T(8,128)(2,1)} %copy.67.hidden_in, ...), custom_call_target="tpu_custom_call" | custom-call | flops 10000000000 | bytes 25000000 | tf_op jit(solution)/shard_map/pallas_call | solution.py:364
  162.3 57.5 %shard_map.239 = (bf16[256,960]{1,0:T(8,128)(2,1)}, f32[256,960]{1,0:T(8,128)}, f32[256,128]{1,0:T(8,128)}, f32[8,960]{1,0:T(8,128)}, bf16[416,2560]{1,0:T(8,128...) custom-call(s32[1]{0:T(128)S(6)} %copy.89.length_ref, ...), custom_call_target="tpu_custom_call" | custom-call | flops 57000001536 | bytes 142500000 | tf_op jit(solution)/shard_map/pallas_call | solution.py:364
  221.6 2.9 convolution_convert_fusion.2
  225.4 4.1 collective-permute-done.18
  229.5 3.4 add_convert_fusion.2
  233.0 15.8 %shard_map.240 = (bf16[416,1280]{1,0:T(8,128)(2,1)}, bf16[416,384]{1,0:T(8,128)(2,1)}, bf16[960,416]{1,0:T(8,128)(2,1)}, bf16[960,416]{1,0:T(8,128)(2,1)}, f32[256,960]{1,0:T(8,128)}, /*index=5*/f32[8,960]{1,0:T(8,128)}) custom-call(s32[1]{0:T(128)S(6)} %copy.89.length_ref, bf16[256,960]{1,0:T(8,128)(2,1)} %copy.67.hidden_in, ...), custom_call_target="tpu_custom_call" | custom-call | flops 1000 | bytes 2 | tf_op jit(solution)/shard_map/pallas_call | solution.py:364
  248.8 4.5 convolution_convert_fusion.1
  254.4 4.1 collective-permute-done.19
  258.5 4.6 add_convert_fusion.1
  263.1 19.0 %collective-permute-done.20 = bf16[960,640]{1,0:T(8,128)(2,1)S(1)} collective-permute-done((bf16[960,640]{1,0:T(8,128)(2,1)S(1)}, bf16[960,640]{1,0:T(8,128)(2,1)S(1)}, u32[]{:S(2)}, u32[]{:S(2)}) %collective-permute-start.20) | collective-permute-done | bytes 1228832 | tf_op jit(solution)/shard_map/ppermute | solution.py:377
  282.5 2.9 convolution_convert_fusion
  291.2 3.2 add_convert_fusion
  294.4 7.1 %collective-permute-done.22 = bf16[480,640]{1,0:T(8,128)(2,1)S(1)} collective-permute-done((bf16[480,640]{1,0:T(8,128)(2,1)S(1)}, bf16[480,640]{1,0:T(8,128)(2,1)S(1)}, u32[]{:S(2)}, u32[]{:S(2)}) %collective-permute-start.22) | collective-permute-done | bytes 614432 | tf_op jit(solution)/shard_map/ppermute | solution.py:377
  301.8 3.5 collective-permute-start.25
  305.4 10.9 %collective-permute-done.23 = bf16[240,2560]{1,0:T(8,128)(2,1)S(1)} collective-permute-done((bf16[240,2560]{1,0:T(8,128)(2,1)S(1)}, bf16[240,2560]{1,0:T(8,128)(2,1)S(1)}, u32[]{:S(2)}, u32[]{:S(2)}) %collective-permute-start.23) | collective-permute-done | bytes 1228832 | tf_op jit(solution)/shard_map/ppermute | solution.py:377
  324.4 3.2 collective-permute-start.29
  329.9 7.4 %collective-permute-done.32 = bf16[120,2560]{1,0:T(8,128)(2,1)S(1)} collective-permute-done((bf16[120,2560]{1,0:T(8,128)(2,1)S(1)}, bf16[120,2560]{1,0:T(8,128)(2,1)S(1)}, u32[]{:S(2)}, u32[]{:S(2)}) %collective-permute-start.32) | collective-permute-done | bytes 614432 | tf_op jit(solution)/shard_map/ppermute | solution.py:377
  344.2 7.1 %collective-permute-done.34 = bf16[240,2560]{1,0:T(8,128)(2,1)S(1)} collective-permute-done((bf16[240,2560]{1,0:T(8,128)(2,1)S(1)}, bf16[240,2560]{1,0:T(8,128)(2,1)S(1)}, u32[]{:S(2)}, u32[]{:S(2)}) %collective-permute-start.34) | collective-permute-done | bytes 1228832 | tf_op jit(solution)/shard_map/ppermute | solution.py:377
  351.4 3.2 collective-permute-start.37
  363.7 3.2 collective-permute-start.38
  370.0 3.2 collective-permute-start.41
  379.0 5.6 %collective-permute-done.44 = bf16[120,2560]{1,0:T(8,128)(2,1)} collective-permute-done((bf16[120,2560]{1,0:T(8,128)(2,1)}, bf16[120,2560]{1,0:T(8,128)(2,1)}, u32[]{:S(2)}, u32[]{:S(2)}) %collective-permute-start.44) | collective-permute-done | bytes 614432 | tf_op jit(solution)/shard_map/ppermute | solution.py:377
  395.5 3.7 collective-permute-done.47
  400.7 5.0 %collective-permute-done.49 = bf16[120,640]{1,0:T(8,128)(2,1)S(1)} collective-permute-done((bf16[120,640]{1,0:T(8,128)(2,1)S(1)}, bf16[120,640]{1,0:T(8,128)(2,1)S(1)}, u32[]{:S(2)}, u32[]{:S(2)}) %collective-permute-start.49) | collective-permute-done | bytes 153632 | tf_op jit(solution)/shard_map/ppermute | solution.py:377
  406.0 3.1 collective-permute-start.52
  411.0 2.6 convert_bitcast_fusion
  413.8 3.5 collective-permute-start.51
  417.5 4.1 collective-permute-done.53
  424.3 3.1 collective-permute-start.59
  434.5 2.6 collective-permute-start.64
  437.3 4.9 %collective-permute-start.65 = (bf16[120,384]{1,0:T(8,128)(2,1)S(1)}, bf16[120,384]{1,0:T(8,128)(2,1)S(1)}, u32[]{:S(2)}, u32[]{:S(2)}) collective-permute-start(bf16[120,384]{1,0:T(8,128)(2,1)S(1)} %add_convert_fusion.16), channel_id=1, source_target_pairs={{0,8},{2,10},{4,12},{6,14},{8,0},{10,2},{12,4},{14,6},{16,24},{18,... | collective-permute-start | bytes 276488 | tf_op jit(solution)/shard_map/ppermute | solution.py:377
  442.5 2.9 maximum_convert_fusion
  445.3 2.9 collective-permute-start.62
  449.9 2.9 collective-permute-start.70
  459.4 4.2 collective-permute-start.72
  463.8 2.9 maximum_convert_fusion.1
  471.3 3.3 collective-permute-done.76
  (397 shorter events, 178.0 us)
Async XLA Ops:
  5.2 48.2 %collective-permute-start.13 = (bf16[80,960]{1,0:T(8,128)(2,1)}, bf16[80,960]{1,0:T(8,128)(2,1)}, u32[]{:S(2)}, u32[]{:S(2)}) collective-permute-start(bf16[80,960]{1,0:T(8,128)(2,1)} %constant_dynamic-slice_fusion.53), channel_id=1, source_target_pairs={{0,1},{1,0},{2,3},{3,2},{4,5},{5,4},{6,7},{7,6},{8,9},{9,8},{10,11... | collective-permute-start | bytes 460808 | tf_op jit(solution)/shard_map/ppermute | solution.py:377
  10.9 45.6 %collective-permute-start.8 = (bf16[120,640]{1,0:T(8,128)(2,1)}, bf16[120,640]{1,0:T(8,128)(2,1)}, u32[]{:S(2)}, u32[]{:S(2)}) collective-permute-start(bf16[120,640]{1,0:T(8,128)(2,1)} %dynamic_slice.207), channel_id=1, source_target_pairs={{0,1},{1,0},{2,3},{3,2},{4,5},{5,4},{6,7},{7,6},{8,9},{9,8},{10,11... | collective-permute-start | bytes 460808 | tf_op jit(solution)/shard_map/ppermute | solution.py:377
  15.4 41.1 %collective-permute-start.3 = (bf16[120,640]{1,0:T(8,128)(2,1)}, bf16[120,640]{1,0:T(8,128)(2,1)}, u32[]{:S(2)}, u32[]{:S(2)}) collective-permute-start(bf16[120,640]{1,0:T(8,128)(2,1)} %dynamic_slice.206), channel_id=1, source_target_pairs={{0,1},{1,0},{2,3},{3,2},{4,5},{5,4},{6,7},{7,6},{8,9},{9,8},{10,11... | collective-permute-start | bytes 460808 | tf_op jit(solution)/shard_map/ppermute | solution.py:377
  24.9 90.1 %collective-permute-start.1 = (bf16[240,2560]{1,0:T(8,128)(2,1)}, bf16[240,2560]{1,0:T(8,128)(2,1)}, u32[]{:S(2)}, u32[]{:S(2)}) collective-permute-start(bf16[240,2560]{1,0:T(8,128)(2,1)} %constant_dynamic-slice_fusion.54), channel_id=1, source_target_pairs={{0,1},{1,0},{2,3},{3,2},{4,5},{5,4},{6,7},{7,6},{8,9},{9,8},{10,11... | collective-permute-start | bytes 3686408 | tf_op jit(solution)/shard_map/ppermute | solution.py:377
  25.9 27.2 %collective-permute-start = (bf16[16,480]{1,0:T(8,128)(2,1)S(1)}, bf16[16,480]{1,0:T(8,128)(2,1)S(1)}, u32[]{:S(2)}, u32[]{:S(2)}) collective-permute-start(bf16[16,480]{1,0:T(8,128)(2,1)S(1)} %maximum_maximum_fusion), channel_id=1, source_target_pairs={{0,1},{1,0},{2,3},{3,2},{4,5},{5,4},{6,7},{7,6},{8,9},{9,8},{10,11... | collective-permute-start | bytes 46088 | tf_op jit(solution)/shard_map/ppermute | solution.py:377
  53.4 16.3 %collective-permute-start.14 = (bf16[80,960]{1,0:T(8,128)(2,1)}, bf16[80,960]{1,0:T(8,128)(2,1)S(1)}, u32[]{:S(2)}, u32[]{:S(2)}) collective-permute-start(bf16[80,960]{1,0:T(8,128)(2,1)} %collective-permute-done.13), channel_id=1, source_target_pairs={{0,16},{2,18},{4,20},{6,22},{8,24},{10,26},{12,28},{14,30},{16,0},... | collective-permute-start | bytes 460808 | tf_op jit(solution)/shard_map/ppermute | solution.py:377
  56.4 16.6 %collective-permute-start.9 = (bf16[120,640]{1,0:T(8,128)(2,1)}, bf16[120,640]{1,0:T(8,128)(2,1)S(1)}, u32[]{:S(2)}, u32[]{:S(2)}) collective-permute-start(bf16[120,640]{1,0:T(8,128)(2,1)} %collective-permute-done.8), channel_id=1, source_target_pairs={{0,16},{2,18},{4,20},{6,22},{8,24},{10,26},{12,28},{14,30},{16,0},... | collective-permute-start | bytes 460808 | tf_op jit(solution)/shard_map/ppermute | solution.py:377
  56.5 19.9 %collective-permute-start.4 = (bf16[120,640]{1,0:T(8,128)(2,1)}, bf16[120,640]{1,0:T(8,128)(2,1)S(1)}, u32[]{:S(2)}, u32[]{:S(2)}) collective-permute-start(bf16[120,640]{1,0:T(8,128)(2,1)} %collective-permute-done.3), channel_id=1, source_target_pairs={{0,16},{2,18},{4,20},{6,22},{8,24},{10,26},{12,28},{14,30},{16,0},... | collective-permute-start | bytes 460808 | tf_op jit(solution)/shard_map/ppermute | solution.py:377
  70.7 13.7 %collective-permute-start.15 = (bf16[160,960]{1,0:T(8,128)(2,1)S(1)}, bf16[160,960]{1,0:T(8,128)(2,1)S(1)}, u32[]{:S(2)}, u32[]{:S(2)}) collective-permute-start(bf16[160,960]{1,0:T(8,128)(2,1)S(1)} %pad_maximum_fusion.19), channel_id=1, source_target_pairs={{0,8},{2,10},{4,12},{6,14},{8,0},{10,2},{12,4},{14,6},{16,24},{18,... | collective-permute-start | bytes 921608 | tf_op jit(solution)/shard_map/ppermute | solution.py:377
  74.0 17.0 %collective-permute-start.10 = (bf16[120,1280]{1,0:T(8,128)(2,1)S(1)}, bf16[120,1280]{1,0:T(8,128)(2,1)S(1)}, u32[]{:S(2)}, u32[]{:S(2)}) collective-permute-start(bf16[120,1280]{1,0:T(8,128)(2,1)S(1)} %pad_maximum_fusion.21), channel_id=1, source_target_pairs={{0,8},{2,10},{4,12},{6,14},{8,0},{10,2},{12,4},{14,6},{16,24},{18,... | collective-permute-start | bytes 921608 | tf_op jit(solution)/shard_map/ppermute | solution.py:377
  77.4 20.2 %collective-permute-start.5 = (bf16[120,1280]{1,0:T(8,128)(2,1)S(1)}, bf16[120,1280]{1,0:T(8,128)(2,1)S(1)}, u32[]{:S(2)}, u32[]{:S(2)}) collective-permute-start(bf16[120,1280]{1,0:T(8,128)(2,1)S(1)} %pad_maximum_fusion.20), channel_id=1, source_target_pairs={{0,8},{2,10},{4,12},{6,14},{8,0},{10,2},{12,4},{14,6},{16,24},{18,... | collective-permute-start | bytes 921608 | tf_op jit(solution)/shard_map/ppermute | solution.py:377
  84.7 15.8 %collective-permute-start.16 = (bf16[320,960]{1,0:T(8,128)(2,1)S(1)}, bf16[320,960]{1,0:T(8,128)(2,1)S(1)}, u32[]{:S(2)}, u32[]{:S(2)}) collective-permute-start(bf16[320,960]{1,0:T(8,128)(2,1)S(1)} %pad_maximum_fusion.11), channel_id=1, source_target_pairs={{0,4},{2,6},{4,0},{6,2},{8,12},{10,14},{12,8},{14,10},{16,20},{18,... | collective-permute-start | bytes 1843208 | tf_op jit(solution)/shard_map/ppermute | solution.py:377
  91.2 22.5 %collective-permute-start.11 = (bf16[120,2560]{1,0:T(8,128)(2,1)S(1)}, bf16[120,2560]{1,0:T(8,128)(2,1)}, u32[]{:S(2)}, u32[]{:S(2)}) collective-permute-start(bf16[120,2560]{1,0:T(8,128)(2,1)S(1)} %pad_maximum_fusion.13), channel_id=1, source_target_pairs={{0,4},{2,6},{4,0},{6,2},{8,12},{10,14},{12,8},{14,10},{16,20},{18,... | collective-permute-start | bytes 1843208 | tf_op jit(solution)/shard_map/ppermute | solution.py:377
  98.6 28.2 %collective-permute-start.6 = (bf16[120,2560]{1,0:T(8,128)(2,1)}, bf16[120,2560]{1,0:T(8,128)(2,1)}, u32[]{:S(2)}, u32[]{:S(2)}) collective-permute-start(bf16[120,2560]{1,0:T(8,128)(2,1)} %pad_maximum_fusion.12), channel_id=1, source_target_pairs={{0,4},{2,6},{4,0},{6,2},{8,12},{10,14},{12,8},{14,10},{16,20},{18,... | collective-permute-start | bytes 1843208 | tf_op jit(solution)/shard_map/ppermute | solution.py:377
  104.4 30.1 %collective-permute-start.17 = (bf16[640,960]{0,1:T(8,128)(2,1)}, bf16[640,960]{0,1:T(8,128)(2,1)}, u32[]{:S(2)}, u32[]{:S(2)}) collective-permute-start(bf16[640,960]{0,1:T(8,128)(2,1)} %copy.64), channel_id=1, source_target_pairs={{0,2},{2,0},{4,6},{6,4},{8,10},{10,8},{12,14},{14,12},{16,18},{18,... | collective-permute-start | bytes 3686408 | tf_op jit(solution)/shard_map/ppermute | solution.py:377
  115.0 16.5 %collective-permute-start.2 = (bf16[240,2560]{1,0:T(8,128)(2,1)}, bf16[240,2560]{1,0:T(8,128)(2,1)S(1)}, u32[]{:S(2)}, u32[]{:S(2)}) collective-permute-start(bf16[240,2560]{1,0:T(8,128)(2,1)} %collective-permute-done.1), channel_id=1, source_target_pairs={{0,2},{2,0},{4,6},{6,4},{8,10},{10,8},{12,14},{14,12},{16,18},{18,... | collective-permute-start | bytes 3686408 | tf_op jit(solution)/shard_map/ppermute | solution.py:377
  118.7 24.5 %collective-permute-start.12 = (bf16[240,2560]{1,0:T(8,128)(2,1)}, bf16[240,2560]{1,0:T(8,128)(2,1)}, u32[]{:S(2)}, u32[]{:S(2)}) collective-permute-start(bf16[240,2560]{1,0:T(8,128)(2,1)} %pad_maximum_fusion.4), channel_id=1, source_target_pairs={{0,2},{2,0},{4,6},{6,4},{8,10},{10,8},{12,14},{14,12},{16,18},{18,... | collective-permute-start | bytes 3686408 | tf_op jit(solution)/shard_map/ppermute | solution.py:377
  130.1 15.0 %collective-permute-start.7 = (bf16[240,2560]{1,0:T(8,128)(2,1)}, bf16[240,2560]{1,0:T(8,128)(2,1)}, u32[]{:S(2)}, u32[]{:S(2)}) collective-permute-start(bf16[240,2560]{1,0:T(8,128)(2,1)} %pad_maximum_fusion.3), channel_id=1, source_target_pairs={{0,2},{2,0},{4,6},{6,4},{8,10},{10,8},{12,14},{14,12},{16,18},{18,... | collective-permute-start | bytes 3686408 | tf_op jit(solution)/shard_map/ppermute | solution.py:377
  253.8 28.3 %collective-permute-start.20 = (bf16[960,640]{1,0:T(8,128)(2,1)S(1)}, bf16[960,640]{1,0:T(8,128)(2,1)S(1)}, u32[]{:S(2)}, u32[]{:S(2)}) collective-permute-start(bf16[960,640]{1,0:T(8,128)(2,1)S(1)} %get-tuple-element.225), channel_id=1, source_target_pairs={{0,1},{1,0},{2,3},{3,2},{4,5},{5,4},{6,7},{7,6},{8,9},{9,8},{10,11... | collective-permute-start | bytes 3686408 | tf_op jit(solution)/shard_map/ppermute | solution.py:377
  287.2 14.3 %collective-permute-start.22 = (bf16[480,640]{1,0:T(8,128)(2,1)S(1)}, bf16[480,640]{1,0:T(8,128)(2,1)S(1)}, u32[]{:S(2)}, u32[]{:S(2)}) collective-permute-start(bf16[480,640]{1,0:T(8,128)(2,1)S(1)} %get-tuple-element.253), channel_id=1, source_target_pairs={{0,4},{2,6},{4,0},{6,2},{8,12},{10,14},{12,8},{14,10},{16,20},{18,... | collective-permute-start | bytes 1843208 | tf_op jit(solution)/shard_map/ppermute | solution.py:377
  288.8 27.4 %collective-permute-start.23 = (bf16[240,2560]{1,0:T(8,128)(2,1)S(1)}, bf16[240,2560]{1,0:T(8,128)(2,1)S(1)}, u32[]{:S(2)}, u32[]{:S(2)}) collective-permute-start(bf16[240,2560]{1,0:T(8,128)(2,1)S(1)} %get-tuple-element.127), channel_id=1, source_target_pairs={{0,1},{1,0},{2,3},{3,2},{4,5},{5,4},{6,7},{7,6},{8,9},{9,8},{10,11... | collective-permute-start | bytes 3686408 | tf_op jit(solution)/shard_map/ppermute | solution.py:377
  289.7 39.1 %collective-permute-start.28 = (f32[8,960]{1,0:T(8,128)S(1)}, f32[8,960]{1,0:T(8,128)S(1)}, u32[]{:S(2)}, u32[]{:S(2)}) collective-permute-start(f32[8,960]{1,0:T(8,128)S(1)} %copy-done.39), channel_id=1, source_target_pairs={{0,1},{1,0},{2,3},{3,2},{4,5},{5,4},{6,7},{7,6},{8,9},{9,8},{10,11... | collective-permute-start | bytes 92168 | tf_op jit(solution)/shard_map/ppermute | solution.py:377
  301.8 14.8 %collective-permute-start.24 = (bf16[120,640]{1,0:T(8,128)(2,1)S(1)}, bf16[120,640]{1,0:T(8,128)(2,1)S(1)}, u32[]{:S(2)}, u32[]{:S(2)}) collective-permute-start(bf16[120,640]{1,0:T(8,128)(2,1)S(1)} %get-tuple-element.297), channel_id=1, source_target_pairs={{0,8},{2,10},{4,12},{6,14},{8,0},{10,2},{12,4},{14,6},{16,24},{18,... | collective-permute-start | bytes 460808 | tf_op jit(solution)/shard_map/ppermute | solution.py:377
  301.8 14.7 %collective-permute-start.25 = (bf16[120,640]{1,0:T(8,128)(2,1)S(1)}, bf16[120,640]{1,0:T(8,128)(2,1)S(1)}, u32[]{:S(2)}, u32[]{:S(2)}) collective-permute-start(bf16[120,640]{1,0:T(8,128)(2,1)S(1)} %get-tuple-element.296), channel_id=1, source_target_pairs={{0,16},{2,18},{4,20},{6,22},{8,24},{10,26},{12,28},{14,30},{16,0},... | collective-permute-start | bytes 460808 | tf_op jit(solution)/shard_map/ppermute | solution.py:377
  322.6 14.7 %collective-permute-start.32 = (bf16[120,2560]{1,0:T(8,128)(2,1)S(1)}, bf16[120,2560]{1,0:T(8,128)(2,1)S(1)}, u32[]{:S(2)}, u32[]{:S(2)}) collective-permute-start(bf16[120,2560]{1,0:T(8,128)(2,1)S(1)} %get-tuple-element.251), channel_id=1, source_target_pairs={{0,4},{2,6},{4,0},{6,2},{8,12},{10,14},{12,8},{14,10},{16,20},{18,... | collective-permute-start | bytes 1843208 | tf_op jit(solution)/shard_map/ppermute | solution.py:377
  323.9 27.5 %collective-permute-start.34 = (bf16[240,2560]{1,0:T(8,128)(2,1)S(1)}, bf16[240,2560]{1,0:T(8,128)(2,1)S(1)}, u32[]{:S(2)}, u32[]{:S(2)}) collective-permute-start(bf16[240,2560]{1,0:T(8,128)(2,1)S(1)} %get-tuple-element.137), channel_id=1, source_target_pairs={{0,1},{1,0},{2,3},{3,2},{4,5},{5,4},{6,7},{7,6},{8,9},{9,8},{10,11... | collective-permute-start | bytes 3686408 | tf_op jit(solution)/shard_map/ppermute | solution.py:377
  324.4 14.7 %collective-permute-start.29 = (bf16[120,640]{1,0:T(8,128)(2,1)S(1)}, bf16[120,640]{1,0:T(8,128)(2,1)S(1)}, u32[]{:S(2)}, u32[]{:S(2)}) collective-permute-start(bf16[120,640]{1,0:T(8,128)(2,1)S(1)} %add_convert_fusion.15), channel_id=1, source_target_pairs={{0,24},{2,26},{4,28},{6,30},{8,16},{10,18},{12,20},{14,22},{16,8},... | collective-permute-start | bytes 460808 | tf_op jit(solution)/shard_map/ppermute | solution.py:377
  337.3 40.6 %collective-permute-start.39 = (f32[8,960]{1,0:T(8,128)}, f32[8,960]{1,0:T(8,128)}, u32[]{:S(2)}, u32[]{:S(2)}) collective-permute-start(f32[8,960]{1,0:T(8,128)} %add.483), channel_id=1, source_target_pairs={{0,2},{2,0},{4,6},{6,4},{8,10},{10,8},{12,14},{14,12},{16,18},{18,... | collective-permute-start | bytes 92168 | tf_op jit(solution)/shard_map/ppermute | solution.py:377
  340.7 17.4 %collective-permute-start.33 = (bf16[480,640]{1,0:T(8,128)(2,1)S(1)}, bf16[480,640]{1,0:T(8,128)(2,1)S(1)}, u32[]{:S(2)}, u32[]{:S(2)}) collective-permute-start(bf16[480,640]{1,0:T(8,128)(2,1)S(1)} %pad_maximum_fusion.14), channel_id=1, source_target_pairs={{0,4},{2,6},{4,0},{6,2},{8,12},{10,14},{12,8},{14,10},{16,20},{18,... | collective-permute-start | bytes 1843208 | tf_op jit(solution)/shard_map/ppermute | solution.py:377
  341.0 14.9 %collective-permute-start.35 = (bf16[120,640]{1,0:T(8,128)(2,1)S(1)}, bf16[120,640]{1,0:T(8,128)(2,1)S(1)}, u32[]{:S(2)}, u32[]{:S(2)}) collective-permute-start(bf16[120,640]{1,0:T(8,128)(2,1)S(1)} %get-tuple-element.289), channel_id=1, source_target_pairs={{0,8},{2,10},{4,12},{6,14},{8,0},{10,2},{12,4},{14,6},{16,24},{18,... | collective-permute-start | bytes 460808 | tf_op jit(solution)/shard_map/ppermute | solution.py:377
  342.1 13.8 %collective-permute-start.36 = (bf16[120,640]{1,0:T(8,128)(2,1)S(1)}, bf16[120,640]{1,0:T(8,128)(2,1)S(1)}, u32[]{:S(2)}, u32[]{:S(2)}) collective-permute-start(bf16[120,640]{1,0:T(8,128)(2,1)S(1)} %get-tuple-element.288), channel_id=1, source_target_pairs={{0,16},{2,18},{4,20},{6,22},{8,24},{10,26},{12,28},{14,30},{16,0},... | collective-permute-start | bytes 460808 | tf_op jit(solution)/shard_map/ppermute | solution.py:377
  369.2 15.3 %collective-permute-start.44 = (bf16[120,2560]{1,0:T(8,128)(2,1)}, bf16[120,2560]{1,0:T(8,128)(2,1)}, u32[]{:S(2)}, u32[]{:S(2)}) collective-permute-start(bf16[120,2560]{1,0:T(8,128)(2,1)} %get-tuple-element.247), channel_id=1, source_target_pairs={{0,4},{2,6},{4,0},{6,2},{8,12},{10,14},{12,8},{14,10},{16,20},{18,... | collective-permute-start | bytes 1843208 | tf_op jit(solution)/shard_map/ppermute | solution.py:377
  369.5 21.0 %collective-permute-start.46 = (bf16[240,1536]{1,0:T(8,128)(2,1)}, bf16[240,1536]{1,0:T(8,128)(2,1)}, u32[]{:S(2)}, u32[]{:S(2)}) collective-permute-start(bf16[240,1536]{1,0:T(8,128)(2,1)} %get-tuple-element.148), channel_id=1, source_target_pairs={{0,1},{1,0},{2,3},{3,2},{4,5},{5,4},{6,7},{7,6},{8,9},{9,8},{10,11... | collective-permute-start | bytes 2211848 | tf_op jit(solution)/shard_map/ppermute | solution.py:377
  370.0 17.1 %collective-permute-start.41 = (bf16[120,640]{1,0:T(8,128)(2,1)}, bf16[120,640]{1,0:T(8,128)(2,1)}, u32[]{:S(2)}, u32[]{:S(2)}) collective-permute-start(bf16[120,640]{1,0:T(8,128)(2,1)} %add_convert_fusion.14), channel_id=1, source_target_pairs={{0,24},{2,26},{4,28},{6,30},{8,16},{10,18},{12,20},{14,22},{16,8},... | collective-permute-start | bytes 460808 | tf_op jit(solution)/shard_map/ppermute | solution.py:377
  373.8 13.7 %collective-permute-start.42 = (bf16[120,640]{1,0:T(8,128)(2,1)}, bf16[120,640]{1,0:T(8,128)(2,1)S(1)}, u32[]{:S(2)}, u32[]{:S(2)}) collective-permute-start(bf16[120,640]{1,0:T(8,128)(2,1)} %add_convert_fusion.14), channel_id=1, source_target_pairs={{0,16},{2,18},{4,20},{6,22},{8,24},{10,26},{12,28},{14,30},{16,0},... | collective-permute-start | bytes 460808 | tf_op jit(solution)/shard_map/ppermute | solution.py:377
  384.6 24.8 %collective-permute-start.40 = (bf16[960,640]{1,0:T(8,128)(2,1)S(1)}, bf16[960,640]{1,0:T(8,128)(2,1)S(1)}, u32[]{:S(2)}, u32[]{:S(2)}) collective-permute-start(bf16[960,640]{1,0:T(8,128)(2,1)S(1)} %pad_maximum_fusion.5), channel_id=1, source_target_pairs={{0,2},{2,0},{4,6},{6,4},{8,10},{10,8},{12,14},{14,12},{16,18},{18,... | collective-permute-start | bytes 3686408 | tf_op jit(solution)/shard_map/ppermute | solution.py:377
  388.7 17.3 %collective-permute-start.45 = (bf16[120,2560]{1,0:T(8,128)(2,1)S(1)}, bf16[120,2560]{1,0:T(8,128)(2,1)S(1)}, u32[]{:S(2)}, u32[]{:S(2)}) collective-permute-start(bf16[120,2560]{1,0:T(8,128)(2,1)S(1)} %pad_maximum_fusion.15), channel_id=1, source_target_pairs={{0,4},{2,6},{4,0},{6,2},{8,12},{10,14},{12,8},{14,10},{16,20},{18,... | collective-permute-start | bytes 1843208 | tf_op jit(solution)/shard_map/ppermute | solution.py:377
  399.2 14.4 %collective-permute-start.50 = (f32[8,960]{1,0:T(8,128)S(1)}, f32[8,960]{1,0:T(8,128)S(1)}, u32[]{:S(2)}, u32[]{:S(2)}) collective-permute-start(f32[8,960]{1,0:T(8,128)S(1)} %add.496), channel_id=1, source_target_pairs={{0,4},{2,6},{4,0},{6,2},{8,12},{10,14},{12,8},{14,10},{16,20},{18,... | collective-permute-start | bytes 92168 | tf_op jit(solution)/shard_map/ppermute | solution.py:377
  399.7 14.1 %collective-permute-start.55 = (bf16[120,1536]{1,0:T(8,128)(2,1)S(1)}, bf16[120,1536]{1,0:T(8,128)(2,1)S(1)}, u32[]{:S(2)}, u32[]{:S(2)}) collective-permute-start(bf16[120,1536]{1,0:T(8,128)(2,1)S(1)} %get-tuple-element.271), channel_id=1, source_target_pairs={{0,4},{2,6},{4,0},{6,2},{8,12},{10,14},{12,8},{14,10},{16,20},{18,... | collective-permute-start | bytes 1105928 | tf_op jit(solution)/shard_map/ppermute | solution.py:377
  405.7 17.1 %collective-permute-start.57 = (bf16[240,1024]{0,1:T(8,128)(2,1)S(1)}, bf16[240,1024]{0,1:T(8,128)(2,1)S(1)}, u32[]{:S(2)}, u32[]{:S(2)}) collective-permute-start(bf16[240,1024]{0,1:T(8,128)(2,1)S(1)} %get-tuple-element.157), channel_id=1, source_target_pairs={{0,1},{1,0},{2,3},{3,2},{4,5},{5,4},{6,7},{7,6},{8,9},{9,8},{10,11... | collective-permute-start | bytes 1474568 | tf_op jit(solution)/shard_map/ppermute | solution.py:377
  413.8 23.5 %collective-permute-start.51 = (bf16[240,2560]{1,0:T(8,128)(2,1)S(1)}, bf16[240,2560]{1,0:T(8,128)(2,1)S(1)}, u32[]{:S(2)}, u32[]{:S(2)}) collective-permute-start(bf16[240,2560]{1,0:T(8,128)(2,1)S(1)} %pad_maximum_fusion.6), channel_id=1, source_target_pairs={{0,2},{2,0},{4,6},{6,4},{8,10},{10,8},{12,14},{14,12},{16,18},{18,... | collective-permute-start | bytes 3686408 | tf_op jit(solution)/shard_map/ppermute | solution.py:377
  427.7 17.7 %collective-permute-start.61 = (f32[8,960]{1,0:T(8,128)S(1)}, f32[8,960]{1,0:T(8,128)S(1)}, u32[]{:S(2)}, u32[]{:S(2)}) collective-permute-start(f32[8,960]{1,0:T(8,128)S(1)} %add.502), channel_id=1, source_target_pairs={{0,8},{2,10},{4,12},{6,14},{8,0},{10,2},{12,4},{14,6},{16,24},{18,... | collective-permute-start | bytes 92168 | tf_op jit(solution)/shard_map/ppermute | solution.py:377
  430.2 18.0 %collective-permute-start.66 = (bf16[120,1024]{0,1:T(8,128)(2,1)S(1)}, bf16[120,1024]{0,1:T(8,128)(2,1)S(1)}, u32[]{:S(2)}, u32[]{:S(2)}) collective-permute-start(bf16[120,1024]{0,1:T(8,128)(2,1)S(1)} %get-tuple-element.305), channel_id=1, source_target_pairs={{0,4},{2,6},{4,0},{6,2},{8,12},{10,14},{12,8},{14,10},{16,20},{18,... | collective-permute-start | bytes 737288 | tf_op jit(solution)/shard_map/ppermute | solution.py:377
  433.2 15.1 %collective-permute-start.63 = (bf16[120,384]{1,0:T(8,128)(2,1)S(1)}, bf16[120,384]{1,0:T(8,128)(2,1)S(1)}, u32[]{:S(2)}, u32[]{:S(2)}) collective-permute-start(bf16[120,384]{1,0:T(8,128)(2,1)S(1)} %add_convert_fusion.16), channel_id=1, source_target_pairs={{0,24},{2,26},{4,28},{6,30},{8,16},{10,18},{12,20},{14,22},{16,8},... | collective-permute-start | bytes 276488 | tf_op jit(solution)/shard_map/ppermute | solution.py:377
  434.5 13.8 %collective-permute-start.64 = (bf16[120,384]{1,0:T(8,128)(2,1)S(1)}, bf16[120,384]{1,0:T(8,128)(2,1)S(1)}, u32[]{:S(2)}, u32[]{:S(2)}) collective-permute-start(bf16[120,384]{1,0:T(8,128)(2,1)S(1)} %add_convert_fusion.16), channel_id=1, source_target_pairs={{0,16},{2,18},{4,20},{6,22},{8,24},{10,26},{12,28},{14,30},{16,0},... | collective-permute-start | bytes 276488 | tf_op jit(solution)/shard_map/ppermute | solution.py:377
  445.3 14.1 %collective-permute-start.62 = (bf16[240,2560]{1,0:T(8,128)(2,1)S(1)}, bf16[240,2560]{1,0:T(8,128)(2,1)S(1)}, u32[]{:S(2)}, u32[]{:S(2)}) collective-permute-start(bf16[240,2560]{1,0:T(8,128)(2,1)S(1)} %pad_maximum_fusion.7), channel_id=1, source_target_pairs={{0,2},{2,0},{4,6},{6,4},{8,10},{10,8},{12,14},{14,12},{16,18},{18,... | collective-permute-start | bytes 3686408 | tf_op jit(solution)/shard_map/ppermute | solution.py:377
  452.8 13.9 %collective-permute-start.71 = (f32[8,960]{1,0:T(8,128)S(1)}, f32[8,960]{1,0:T(8,128)S(1)}, u32[]{:S(2)}, u32[]{:S(2)}) collective-permute-start(f32[8,960]{1,0:T(8,128)S(1)} %add.512), channel_id=1, source_target_pairs={{0,16},{2,18},{4,20},{6,22},{8,24},{10,26},{12,28},{14,30},{16,0},... | collective-permute-start | bytes 92168 | tf_op jit(solution)/shard_map/ppermute | solution.py:377
  459.4 17.6 %collective-permute-start.72 = (bf16[240,1536]{1,0:T(8,128)(2,1)S(1)}, bf16[240,1536]{1,0:T(8,128)(2,1)S(1)}, u32[]{:S(2)}, u32[]{:S(2)}) collective-permute-start(bf16[240,1536]{1,0:T(8,128)(2,1)S(1)} %pad_maximum_fusion.9), channel_id=1, source_target_pairs={{0,2},{2,0},{4,6},{6,4},{8,10},{10,8},{12,14},{14,12},{16,18},{18,... | collective-permute-start | bytes 2211848 | tf_op jit(solution)/shard_map/ppermute | solution.py:377
  (85 other events, 481.1 us)
